TPU v7x, 32 devices: a whole 2x2x4 slice. The times are simulated.
32 devices in a mesh: groups: 2 (over y), dp: 8 (over z, x), tensor: 2 (over core).
Axes of the slice: x: 2, y: 2, z: 4, core: 2. Of those that a mesh axis runs over, the one named last changes fastest.
Arguments:
- activations: bfloat16 [4096, 13824], P(('groups', 'dp'), 'tensor'), parts along dimension 0, may hold values from -6 to 6
- out_grads: bfloat16 [4096, 5120], P(('groups', 'dp'), 'tensor'), parts along dimension 0, may hold values from -6 to 6
- act_factor: bfloat16 [640, 13824], P('dp', 'tensor'), may hold values from -0.009765625 to 0.009765625
- grad_factor: bfloat16 [640, 5120], P('dp', 'tensor'), may hold values from -0.015625 to 0.015625
- query_of_row: int32 [640], replicated, may hold values from 0 to 19, as said below
- live_tokens: int32 [128], P(('groups', 'dp')), parts along dimension 0, may hold values from 0 to 32, as said below
- move_plan: int32 [128, 2], P(('groups', 'dp')), parts along dimension 0, may hold values from -1 to 7, as said below
Outputs:
- influence: float32 [64, 20], P(('groups', 'dp')), parts along dimension 0
There are 2 independent parts, one for each index of `groups`. A program takes and returns all parts, laid end to end along the dimension named above; an argument that names none is the same for every part. Nothing has to cross between parts.
Inputs may be any that keep to these rules, and one draw needn't show every extreme that they name: query_of_row names every query by exactly 32 rows. `live_tokens`: 0 where the slot's move_plan entry is -1, else 1 to 32; live tokens stand at the front of a block. `move_plan`: entry s is -1, -1 for an empty slot; else a live block of device d (slots d * 8 to (d + 1) * 8 - 1) goes to device d, d + 1 or d - 1 along the closed dp loop (indices modulo 8); blocks from device d - 1 land in slots below 2, blocks from device d + 1 in slots 2 and above; at most 2 blocks of one device go to each neighbour; each of the 32 destinations receives exactly one block; some device has all 8 slots live.
All inputs are finite; a program needn't handle non-finite values.
Results may differ from a plain program's by a relative error of at most 0.0003.
Values may be sent and summed in bfloat16 or wider, within the bound.
No kernel may reach another device: no remote copies, remote signals or barrier semaphores. Data moves between devices by JAX's collectives and lax.ppermute only.
A program may use at most 128 MiB of HBM per device.

v0:
```python
import jax
import jax.numpy as jnp
from jax import lax
from jax.sharding import PartitionSpec as P

QUERIES = 20


def shifted(value, axis, steps):
    count = lax.axis_size(axis)
    pairs = [(source, (source + steps) % count) for source in range(count)]
    return lax.ppermute(value, axis, pairs)


def project_rows(rows, factor):
    return lax.dot_general(
        rows, factor, (((1,), (1,)), ((), ())), preferred_element_type=jnp.float32
    )


def shards(activations, out_grads, act_factor, grad_factor, query_of_row, live_tokens, move_plan):
    slots_in = live_tokens.shape[0]
    block_len = activations.shape[0] // slots_in
    slots_out = slots_in // 2
    half_slots = slots_out // 2
    my_rank = lax.axis_index("dp")
    dp_size = lax.axis_size("dp")
    offsets = jnp.arange(block_len, dtype=jnp.int32)
    live_mask = offsets[None, :] < live_tokens[:, None]
    act_blocks = activations.reshape(slots_in, block_len, -1)
    grad_blocks = out_grads.reshape(slots_in, block_len, -1)
    grad_blocks = jnp.where(live_mask[:, :, None], grad_blocks, jnp.zeros_like(grad_blocks))
    dest_rank = move_plan[:, 0]
    dest_slot = move_plan[:, 1]
    keep_here = dest_rank == my_rank
    goes_right = dest_rank == (my_rank + 1) % dp_size
    goes_left = dest_rank == (my_rank + dp_size - 1) % dp_size
    out_ids = jnp.arange(slots_out, dtype=jnp.int32)
    hand_ids = jnp.arange(half_slots, dtype=jnp.int32)
    keep_hits = keep_here[None, :] & (dest_slot[None, :] == out_ids[:, None])
    right_hits = goes_right[None, :] & (dest_slot[None, :] == hand_ids[:, None])
    left_hits = goes_left[None, :] & (dest_slot[None, :] == hand_ids[:, None] + half_slots)
    keep_index = jnp.argmax(keep_hits, axis=1)
    keep_valid = jnp.any(keep_hits, axis=1)
    right_index = jnp.argmax(right_hits, axis=1)
    right_valid = jnp.any(right_hits, axis=1)
    left_index = jnp.argmax(left_hits, axis=1)
    left_valid = jnp.any(left_hits, axis=1)
    factor_rows = query_of_row.shape[0]
    query_onehot = (query_of_row[:, None] == jnp.arange(QUERIES, dtype=jnp.int32)[None, :]).astype(
        jnp.float32
    )
    slot_count = act_blocks.shape[0]
    act_rows = act_blocks.reshape(slot_count * block_len, -1)
    grad_rows = grad_blocks.reshape(slot_count * block_len, -1)
    grad_all = lax.all_gather(grad_factor, "dp", axis=0, tiled=True)
    act_all = lax.all_gather(act_factor, "dp", axis=0, tiled=True)
    proj_grad = project_rows(grad_rows, grad_all)
    proj_act = project_rows(act_rows, act_all)
    full_grad, full_act = lax.psum((proj_grad, proj_act), "tensor")
    per_block = (full_grad * full_act).reshape(slot_count, block_len, factor_rows).sum(axis=1)
    slot_scores = jnp.dot(
        per_block, query_onehot, precision=lax.Precision.HIGHEST, preferred_element_type=jnp.float32
    )
    own_scores = jnp.where(keep_valid[:, None], slot_scores[keep_index], 0.0)
    lower_scores = shifted(jnp.where(right_valid[:, None], slot_scores[right_index], 0.0), "dp", 1)
    upper_scores = shifted(jnp.where(left_valid[:, None], slot_scores[left_index], 0.0), "dp", -1)
    influence = jnp.where(
        keep_valid[:, None], own_scores, jnp.concatenate([lower_scores, upper_scores], axis=0)
    )
    return influence


def solution(mesh):
    return jax.shard_map(
        shards,
        mesh=mesh,
        in_specs=(
            P(("groups", "dp"), "tensor"),
            P(("groups", "dp"), "tensor"),
            P("dp", "tensor"),
            P("dp", "tensor"),
            P(),
            P(("groups", "dp")),
            P(("groups", "dp"), None),
        ),
        out_specs=P(("groups", "dp"), None),
        check_vma=False,
    )
```

profile of v0, /device:TPU:0, one launch (start us, length us, event | category | flops | bytes accessed | tf_op | source)
XLA Modules:
  0.0 255.2 jit_solution(12840324684614084152)
XLA Ops:
  6.5 0.7 all-gather.3.cloned.1.call-update
  7.3 0.7 all-gather.5.cloned.1.call-update
  8.1 0.7 iota_compare_fusion.2
  8.9 0.7 slice_bitcast_fusion
  9.6 1.2 compare_bitcast_fusion.2
  10.8 0.6 iota_reduce_fusion.1
  11.4 62.8 %all-gather.3.cloned.1.call-done = bf16[640,2560]{1,0:T(8,128)(2,1)} async-done(((bf16[80,2560]{1,0:T(8,128)(2,1)}), bf16[640,2560]{1,0:T(8,128)(2,1)}) %all-gather.3.cloned.1.call-update) | async-done | bytes 3276816 | tf_op jit(solution)/shard_map/all_gather | solution.py:56
  74.2 4.4 %fusion = f32[256,640]{1,0:T(8,128)} fusion(bf16[640,2560]{1,0:T(8,128)(2,1)} %all-gather.3.cloned.1.call-done, bf16[256,2560]{1,0:T(8,128)(2,1)} %param.8, pred[256]{0:T(512)(128)(4,1)S(1)} %lt.47), kind=kOutput, calls=%fused_computation.3 | convolution fusion | flops 839516160 | bytes 5243136 | tf_op jit(solution)/shard_map/dot_general | solution.py:16
  78.6 127.3 %all-gather.5.cloned.1.call-done = bf16[640,6912]{1,0:T(8,128)(2,1)} async-done(((bf16[80,6912]{1,0:T(8,128)(2,1)}), bf16[640,6912]{1,0:T(8,128)(2,1)}) %all-gather.5.cloned.1.call-update) | async-done | bytes 8847376 | tf_op jit(solution)/shard_map/all_gather | solution.py:57
  205.9 6.4 %fusion.12 = f32[256,640]{1,0:T(8,128)} fusion(bf16[256,6912]{1,0:T(8,128)(2,1)S(1)} %copy-done, bf16[640,6912]{1,0:T(8,128)(2,1)} %all-gather.5.cloned.1.call-done), kind=kOutput, calls=%fused_computation.37 | convolution fusion | flops 2264924160 | bytes 13041664 | tf_op jit(solution)/shard_map/dot_general | solution.py:16
  212.4 0.7 fusion.7
  213.1 1.3 fusion.9
  214.4 1.4 fusion.10
  215.8 1.4 iota_reduce_fusion
  217.7 13.1 %all-reduce.3.cloned.1.call-done = (f32[256,640]{1,0:T(8,128)}, f32[256,640]{1,0:T(8,128)}) async-done(((f32[256,640]{1,0:T(8,128)}, f32[256,640]{1,0:T(8,128)}), (f32[256,640]{1,0:T(8,128)}, f32[256,640]{1,0:T(8,128)})) %all-reduce.3.cloned.1.call-update) | async-done | bytes 1310736 | tf_op jit(solution)/shard_map/psum | solution.py:60
  230.8 1.4 bitcast_reduce_fusion
  232.2 1.0 fusion.4
  233.2 0.6 gather_fusion.1
  234.3 0.7 broadcast_select_fusion
  235.0 4.5 %collective-permute-start.1 = (f32[2,20]{1,0:T(2,128)S(1)}, f32[2,20]{1,0:T(2,128)}, u32[]{:S(2)}, u32[]{:S(2)}) collective-permute-start(f32[2,20]{1,0:T(2,128)S(1)} %broadcast_select_fusion), channel_id=1, source_target_pairs={{0,14},{2,0},{4,2},{6,4},{8,6},{10,8},{12,10},{14,12},{1,15},{3,1}... | collective-permute-start | bytes 488 | tf_op jit(solution)/shard_map/ppermute | solution.py:12
  239.5 1.2 broadcast_select_fusion.1
  240.8 0.7 pad_clamp_fusion.2
  242.0 5.4 %collective-permute-done = f32[2,20]{1,0:T(2,128)} collective-permute-done((f32[2,20]{1,0:T(2,128)}, f32[2,20]{1,0:T(2,128)}, u32[]{:S(2)}, u32[]{:S(2)}) %collective-permute-start) | collective-permute-done | bytes 192 | tf_op jit(solution)/shard_map/ppermute | solution.py:12
  247.4 1.3 maximum_select_fusion
  (19 shorter events, 1.9 us)
Async XLA Ops:
  6.5 199.4 %copy-start = (bf16[256,6912]{1,0:T(8,128)(2,1)S(1)}, bf16[256,6912]{1,0:T(8,128)(2,1)}, u32[]{:S(2)}) copy-start(bf16[256,6912]{1,0:T(8,128)(2,1)} %param.7) | copy-start | bytes 10616836
  6.5 67.7 %all-gather.3.cloned.1.call-start = ((), (), s32[]{:S(2)}) async-start(), calls=%async_computation | async-start | bytes 3686400 | tf_op jit(solution)/shard_map/all_gather | solution.py:56
  7.3 198.6 %all-gather.5.cloned.1.call-start = ((), (), s32[]{:S(2)}) async-start(), calls=%async_computation.1 | async-start | bytes 9953280 | tf_op jit(solution)/shard_map/all_gather | solution.py:57
  8.0 222.8 %all-reduce.3.cloned.1.call-start = ((), (), s32[]{:S(2)}) async-start(), calls=%async_computation.2 | async-start | bytes 2621440 | tf_op jit(solution)/shard_map/psum | solution.py:60
  10.8 0.6 copy-start.1
  235.0 7.0 %collective-permute-start.1 = (f32[2,20]{1,0:T(2,128)S(1)}, f32[2,20]{1,0:T(2,128)}, u32[]{:S(2)}, u32[]{:S(2)}) collective-permute-start(f32[2,20]{1,0:T(2,128)S(1)} %broadcast_select_fusion), channel_id=1, source_target_pairs={{0,14},{2,0},{4,2},{6,4},{8,6},{10,8},{12,10},{14,12},{1,15},{3,1}... | collective-permute-start | bytes 488 | tf_op jit(solution)/shard_map/ppermute | solution.py:12
  240.8 6.6 %collective-permute-start = (f32[2,20]{1,0:T(2,128)}, f32[2,20]{1,0:T(2,128)}, u32[]{:S(2)}, u32[]{:S(2)}) collective-permute-start(f32[2,20]{1,0:T(2,128)} %broadcast_select_fusion.1), channel_id=1, source_target_pairs={{0,2},{2,4},{4,6},{6,8},{8,10},{10,12},{12,14},{14,0},{1,3},{3,5},... | collective-permute-start | bytes 488 | tf_op jit(solution)/shard_map/ppermute | solution.py:12
Sparse Core Ops, SparseCore 0:
  9.5 64.6 all-gather.2
  76.4 129.4 all-gather.4
  212.5 18.2 all-reduce.2
where the time goes:
time: 256 us; the launch traced here: 255 us
  waiting for transfers between devices  210 us (82%)
  other arithmetic  13.3 us (5%)
  between operations  13.2 us (5%)
  matrix products  11.8 us (5%)
  starting transfers between devices  4.59 us (2%)
    all_gather x1, waiting for transfers between devices, shards(): act_all = lax.all_gather(act_factor, 'dp', axis=0, tiled=True)  127 us
    all_gather x1, waiting for transfers between devices, shards(): grad_all = lax.all_gather(grad_factor, 'dp', axis=0, tiled=True)  62.8 us
    psum x1, waiting for transfers between devices, shards(): full_grad, full_act = lax.psum((proj_grad, proj_act), 'tensor')  13.1 us
    dot_general x2, matrix products, project_rows(): lax.dot_general(rows, factor, (((1,), (1,)), ((), ())), preferred_element...  10.8 us
    ppermute x2, waiting for transfers between devices, shifted(): return lax.ppermute(value, axis, pairs)  5.35 us
  transfers between devices with their start and end apart: 5, of which 4 were waited for; matrix products, arithmetic and copies ran while one was open for 6% of the time, Pallas kernels for 0%

commit v1 on v0

v1 whole, which is shorter than its diff:
```python
import jax
import jax.numpy as jnp
from jax import lax
from jax.sharding import PartitionSpec as P

QUERIES = 20


def shifted(value, axis, steps):
    count = lax.axis_size(axis)
    pairs = [(source, (source + steps) % count) for source in range(count)]
    return lax.ppermute(value, axis, pairs)


def project_rows(rows, factor):
    return lax.dot_general(
        rows, factor, (((1,), (1,)), ((), ())), preferred_element_type=jnp.float32
    )


def swapped(value, axis):
    return lax.ppermute(value, axis, [(0, 1), (1, 0)])


def one_hot_queries(query_of_row):
    ids = jnp.arange(QUERIES, dtype=jnp.int32)[None, :]
    return (query_of_row[:, None] == ids).astype(jnp.float32)


def query_sums(rows, onehot):
    return jnp.dot(rows, onehot, precision=lax.Precision.HIGHEST, preferred_element_type=jnp.float32)


def gathered(activations, out_grads, act_factor, grad_factor, query_of_row, live_tokens, move_plan):
    slots_in = live_tokens.shape[0]
    block_len = activations.shape[0] // slots_in
    slots_out = slots_in // 2
    half_slots = slots_out // 2
    my_rank = lax.axis_index("dp")
    dp_size = lax.axis_size("dp")
    offsets = jnp.arange(block_len, dtype=jnp.int32)
    live_mask = (offsets[None, :] < live_tokens[:, None]).reshape(-1)
    grad_rows = jnp.where(live_mask[:, None], out_grads, jnp.zeros_like(out_grads))
    grad_all = lax.all_gather(grad_factor, "dp", axis=0, tiled=True)
    act_all = lax.all_gather(act_factor, "dp", axis=0, tiled=True)
    proj_grad = project_rows(grad_rows, grad_all)
    proj_act = project_rows(activations, act_all)
    full_grad, full_act = lax.psum((proj_grad, proj_act), "tensor")
    per_block = (full_grad * full_act).reshape(slots_in, block_len, -1).sum(axis=1)
    slot_scores = query_sums(per_block, one_hot_queries(query_of_row))
    keep, right, left = plan_weights(move_plan, my_rank, dp_size, slots_out, half_slots)
    lower = shifted(pick(right, slot_scores), "dp", 1)
    upper = shifted(pick(left, slot_scores), "dp", -1)
    return pick(keep, slot_scores) + jnp.concatenate([lower, upper], axis=0)


def plan_weights(move_plan, my_rank, dp_size, slots_out, half_slots):
    dest_rank = move_plan[:, 0]
    dest_slot = move_plan[:, 1]
    out_ids = jnp.arange(slots_out, dtype=jnp.int32)[:, None]
    hand_ids = jnp.arange(half_slots, dtype=jnp.int32)[:, None]
    keep = (dest_rank == my_rank)[None, :] & (dest_slot[None, :] == out_ids)
    right = (dest_rank == (my_rank + 1) % dp_size)[None, :] & (dest_slot[None, :] == hand_ids)
    left = (dest_rank == (my_rank + dp_size - 1) % dp_size)[None, :] & (
        dest_slot[None, :] == hand_ids + half_slots
    )
    return keep, right, left


def pick(hits, scores):
    return jnp.where(hits[:, :, None], scores[None, :, :], 0.0).sum(axis=1)


def ring_place(index, count):
    return jnp.where(index % 2 == 0, index // 2, count - 1 - index // 2)


def ring_index(place, count):
    place = place % count
    return jnp.where(place < count // 2, 2 * place, 2 * (count - 1 - place) + 1)


def ringed(activations, out_grads, act_factor, grad_factor, query_of_row, live_tokens, move_plan):
    dp_size = lax.axis_size("dp")
    my_rank = lax.axis_index("dp")
    group = lax.axis_index("groups")
    core = lax.axis_index("tensor")
    slots_in = live_tokens.shape[0]
    tokens, act_width = activations.shape
    grad_width = out_grads.shape[1]
    factor_rows = act_factor.shape[0]
    block_len = tokens // slots_in
    slots_out = slots_in // 2
    half_slots = slots_out // 2
    half_tokens = tokens // 2
    my_slots = slots_in // 2
    act_half, grad_half = act_width // 2, grad_width // 2

    def halves(acts, grads, side):
        act_part = lax.dynamic_slice_in_dim(acts, side * act_half, act_half, 1)
        grad_part = lax.dynamic_slice_in_dim(grads, side * grad_half, grad_half, 1)
        return jnp.concatenate([act_part, grad_part], axis=1)

    order = list(range(0, dp_size, 2)) + list(range(dp_size - 1, 0, -2))
    ahead = [(order[i], order[(i + 1) % dp_size]) for i in range(dp_size)]
    back = [(b, a) for a, b in ahead]

    def send_ahead(value):
        return lax.ppermute(value, "dp", ahead)

    def send_back(value):
        return lax.ppermute(value, "dp", back)

    own_factor = halves(act_factor, grad_factor, group)
    from_back, from_ahead = [own_factor], [own_factor]
    steps = dp_size // 2
    for _ in range(steps - 1):
        from_back.append(send_ahead(from_back[-1]))
        from_ahead.append(send_back(from_ahead[-1]))
    cut = factor_rows // 2
    last_factor = jnp.concatenate(
        [send_ahead(from_back[-1][:cut]), send_back(from_ahead[-1][cut:])], axis=0
    )

    def of_core(value, side):
        return lax.dynamic_slice_in_dim(value, side * half_tokens, half_tokens, 0)

    acts_keep, acts_give = of_core(activations, core), of_core(activations, 1 - core)
    grads_keep, grads_give = of_core(out_grads, core), of_core(out_grads, 1 - core)
    other = jnp.concatenate(
        [halves(acts_keep, grads_keep, 1 - group), halves(acts_give, grads_give, 1 - group)], axis=0
    )
    other = swapped(other, "groups")
    keep = jnp.concatenate([halves(acts_keep, grads_keep, group), other[:half_tokens]], axis=0)
    give = jnp.concatenate([halves(acts_give, grads_give, group), other[half_tokens:]], axis=0)

    place = ring_place(my_rank, dp_size)

    def onehot_of(distance):
        start = ring_index(place + distance, dp_size) * factor_rows
        return one_hot_queries(lax.dynamic_slice_in_dim(query_of_row, start, factor_rows, 0))

    live = lax.dynamic_slice_in_dim(live_tokens, core * my_slots, my_slots, 0)
    offsets = jnp.arange(block_len, dtype=jnp.int32)
    live_mask = (offsets[None, :] < live[:, None])[:, :, None]

    def scores_of(act, grad, onehot):
        product = (act * grad).reshape(my_slots, block_len, -1)
        return query_sums(jnp.where(live_mask, product, 0.0).sum(axis=1), onehot)

    def project(rows, factor):
        return (
            project_rows(rows[:, :act_half], factor[:, :act_half]),
            project_rows(rows[:, act_half:], factor[:, act_half:]),
        )

    own_act = project_rows(acts_keep, act_factor) + swapped(project_rows(acts_give, act_factor), "tensor")
    own_grad = project_rows(grads_keep, grad_factor) + swapped(
        project_rows(grads_give, grad_factor), "tensor"
    )
    scores = scores_of(own_act, own_grad, onehot_of(0))

    def shared_scores(factor, onehot):
        given_act, given_grad = project(give, factor)
        got_act, got_grad = swapped(given_act, "tensor"), swapped(given_grad, "tensor")
        kept_act, kept_grad = project(keep, factor)
        act, grad = kept_act + got_act, kept_grad + got_grad
        act = act[:half_tokens] + swapped(act[half_tokens:], "groups")
        grad = grad[:half_tokens] + swapped(grad[half_tokens:], "groups")
        return scores_of(act, grad, onehot)

    early, early_onehot = [], []
    for distance in range(1, steps):
        early += [from_back[distance], from_ahead[distance]]
        early_onehot += [onehot_of(-distance), onehot_of(distance)]
    scores += shared_scores(jnp.concatenate(early, axis=0), jnp.concatenate(early_onehot, axis=0))
    scores += shared_scores(last_factor, onehot_of(steps))

    my_plan = lax.dynamic_slice_in_dim(move_plan, core * my_slots, my_slots, 0)
    keep_hits, right_hits, left_hits = plan_weights(my_plan, my_rank, dp_size, slots_out, half_slots)
    own, right, left = pick(keep_hits, scores), pick(right_hits, scores), pick(left_hits, scores)

    def across(value, steps):
        pairs = [
            (2 * source + side, 2 * ((source + steps) % dp_size) + 1 - side)
            for source in range(dp_size)
            for side in range(2)
        ]
        return lax.ppermute(value, ("dp", "tensor"), pairs)

    own += swapped(own, "tensor")
    lower = shifted(right, "dp", 1) + across(right, 1)
    upper = shifted(left, "dp", -1) + across(left, -1)
    return own + jnp.concatenate([lower, upper], axis=0)


def solution(mesh):
    paired = mesh.shape["groups"] == 2 and mesh.shape["tensor"] == 2
    short = mesh.shape["dp"] % 2 == 0 and 4 <= mesh.shape["dp"] <= 16
    return jax.shard_map(
        ringed if paired and short else gathered,
        mesh=mesh,
        in_specs=(
            P(("groups", "dp"), "tensor"),
            P(("groups", "dp"), "tensor"),
            P("dp", "tensor"),
            P("dp", "tensor"),
            P(),
            P(("groups", "dp")),
            P(("groups", "dp"), None),
        ),
        out_specs=P(("groups", "dp"), None),
        check_vma=False,
    )
```

time: 256 us -> 113 us (0.44)
  waiting for transfers between devices: 210 us -> 43.9 us
  starting transfers between devices: 4.59 us -> 23 us
  local copies, waits for them, and re-layouts: 2.47 us -> 17.8 us
  between operations: 13.2 us -> 0.43 us
  matrix products: 11.8 us -> 18.1 us
  other arithmetic: 13.3 us -> 8.91 us
    all_gather x2 -> x0, waiting for transfers between devices: 190 us -> none  [the longest x1 127 us: shards(): act_all = lax.all_gather(act_factor, 'dp', axis=0, tiled=True)]
    ppermute x0 -> x22, waiting for transfers between devices: none -> 43.9 us  [the longest x4 31.5 us: send_ahead(): return lax.ppermute(value, 'dp', ahead)]
    ppermute x0 -> x22, starting transfers between devices: none -> 18.5 us  [the longest x4 7.81 us: send_ahead(): return lax.ppermute(value, 'dp', ahead)]
    psum x1 -> x0, waiting for transfers between devices: 13.1 us -> none  [shards(): full_grad, full_act = lax.psum((proj_grad, proj_act), 'tensor')]
    dynamic_slice x0 -> x7, local copies, waits for them, and re-layouts: none -> 7.19 us  [the longest x2 4.05 us: halves(): act_part = lax.dynamic_slice_in_dim(acts, side * act_half, act_half, 1)]
    dot_general x2 -> x12, matrix products: 10.8 us -> 17.6 us  [project_rows(): lax.dot_general(rows, factor, (((1,), (1,)), ((), ())), preferred_element...]
    ppermute x2, waiting for transfers between devices: 5.35 us -> 0.01 us  [shifted(): return lax.ppermute(value, axis, pairs)]
    unnamed x4 -> x36, local copies, waits for them, and re-layouts: 0.01 us -> 3.96 us
  transfers between devices with their start and end apart: 5 -> 24, of which waited for: 4 -> 10; matrix products, arithmetic and copies ran while one was open for 6% -> 36% of each run, Pallas kernels for 0% -> 0%
where the time goes in v1:
time: 113 us; the launch traced here: 112 us
  waiting for transfers between devices  43.9 us (39%)
  starting transfers between devices  23 us (20%)
  matrix products  18.1 us (16%)
  local copies, waits for them, and re-layouts  17.8 us (16%)
  other arithmetic  8.91 us (8%)
    ppermute x4, waiting for transfers between devices, send_ahead(): return lax.ppermute(value, 'dp', ahead)  31.5 us
    dot_general x12, matrix products, project_rows(): lax.dot_general(rows, factor, (((1,), (1,)), ((), ())), preferred_element...  17.6 us
    ppermute x12, waiting for transfers between devices, swapped(): return lax.ppermute(value, axis, [(0, 1), (1, 0)])  9.63 us
    ppermute x4, starting transfers between devices, send_ahead(): return lax.ppermute(value, 'dp', ahead)  7.81 us
    ppermute x12, starting transfers between devices, swapped(): return lax.ppermute(value, axis, [(0, 1), (1, 0)])  7.51 us
    ppermute x2, starting transfers between devices, shifted(): return lax.ppermute(value, axis, pairs)  4.47 us
    dynamic_slice x2, local copies, waits for them, and re-layouts, halves(): act_part = lax.dynamic_slice_in_dim(acts, side * act_half, act_half, 1)  4.05 us
    unnamed x36, local copies, waits for them, and re-layouts  3.96 us
  transfers between devices with their start and end apart: 24, of which 10 were waited for; matrix products, arithmetic and copies ran while one was open for 36% of the time, Pallas kernels for 0%

profile of v1, /device:TPU:0, one launch (start us, length us, event | category | flops | bytes accessed | tf_op | source)
XLA Modules:
  0.0 112.1 jit_solution(16376257855276473857)
XLA Ops:
  3.2 3.0 %collective-permute-start.3 = (bf16[80,4736]{1,0:T(8,128)(2,1)}, bf16[80,4736]{1,0:T(8,128)(2,1)}, u32[]{:S(2)}, u32[]{:S(2)}) collective-permute-start(bf16[80,4736]{1,0:T(8,128)(2,1)} %pad_maximum_fusion.2), channel_id=1, source_target_pairs={{0,4},{4,8},{8,12},{12,14},{14,10},{10,6},{6,2},{2,0},{1,5},{5,9},... | collective-permute-start | bytes 2273288 | tf_op jit(solution)/shard_map/ppermute | solution.py:109
  6.2 4.0 %fusion.49 = (bf16[128,3456]{1,0:T(8,128)(2,1)S(1)}, bf16[128,3456]{1,0:T(8,128)(2,1)S(1)}, bf16[128,3456]{1,0:T(8,128)(2,1)S(1)}, bf16[128,3456]{1,0:T(8,128)(2,1)S(1)}) fusion(bf16[256,6912]{1,0:T(8,128)(2,1)} %param.7, s32[]{:T(128)S(6)} %select_n.177, s32[]{:T(128)S(6)} %select_n.179, s32[]{:T(128)S(6)} %select_n.183, s32[]{:T(128)S(6)} %select_n.186), kind=kLoop, calls=%fused_computation.89 | loop fusion | bytes 7077904 | tf_op jit(solution)/shard_map/dynamic_slice | solution.py:100
  11.0 1.6 %maximum_maximum_fusion = bf16[256,4736]{1,0:T(8,128)(2,1)} fusion(bf16[128,1280]{1,0:T(8,128)(2,1)S(1)} %get-tuple-element.18, bf16[128,3456]{1,0:T(8,128)(2,1)S(1)} %get-tuple-element.12, bf16[128,1280]{1,0:T(8,128)(2,1)S(1)} %get-tuple-element.16, bf16[128,3456]{1,0:T(8,128)(2,1)S(1)} %get-tuple-element.10), kind=kLoop, calls=%fused_computation.4 | loop fusion | flops 9699328 | bytes 4849664 | tf_op jit(solution)/shard_map/concatenate | solution.py:130
  12.6 2.0 %collective-permute-start.2 = (bf16[256,4736]{1,0:T(8,128)(2,1)}, bf16[256,4736]{1,0:T(8,128)(2,1)}, u32[]{:S(2)}, u32[]{:S(2)}) collective-permute-start(bf16[256,4736]{1,0:T(8,128)(2,1)} %maximum_maximum_fusion), channel_id=1, source_target_pairs={{0,16},{16,0},{1,17},{17,1},{2,18},{18,2},{3,19},{19,3},{4,20},{20... | collective-permute-start | bytes 7274504 | tf_op jit(solution)/shard_map/ppermute | solution.py:22
  25.1 1.6 %convolution_add_fusion.2 = f32[128,80]{0,1:T(8,128)S(1)} fusion(f32[128,80]{0,1:T(8,128)} %collective-permute-done.1, bf16[80,2560]{1,0:T(8,128)(2,1)} %param.10, bf16[256,2560]{1,0:T(8,128)(2,1)} %param.8, s32[]{:T(128)S(6)} %select_n.168), kind=kOutput, calls=%fused_computation.23 | convolution fusion | flops 52439040 | bytes 1146884 | tf_op jit(solution)/shard_map/dot_general | solution.py:16
  26.6 2.8 %fusion.25 = f32[128,80]{0,1:T(8,128)} fusion(f32[128,80]{0,1:T(8,128)S(1)} %convolution_add_fusion.2, f32[128,80]{0,1:T(8,128)} %collective-permute-done, bf16[80,6912]{1,0:T(8,128)(2,1)S(1)} %copy-done, bf16[256,6912]{1,0:T(8,128)(2,1)} %param.7, s32[]{:T(128)S(6)} %select_n.168), kind=kOutput, calls=%fused_computation.22 | convolution fusion | flops 141578240 | bytes 2998276 | tf_op jit(solution)/shard_map/dot_general | solution.py:16
  29.5 1.5 %copy.14 = f32[128,80]{1,0:T(8,128)} copy(f32[128,80]{0,1:T(8,128)} %fusion.25) | data formatting | bytes 81920 | tf_op jit(solution)/shard_map/mul | solution.py:148
  31.0 1.6 %collective-permute-start.5 = (bf16[80,4736]{1,0:T(8,128)(2,1)}, bf16[80,4736]{1,0:T(8,128)(2,1)S(1)}, u32[]{:S(2)}, u32[]{:S(2)}) collective-permute-start(bf16[80,4736]{1,0:T(8,128)(2,1)} %collective-permute-done.3), channel_id=1, source_target_pairs={{0,4},{4,8},{8,12},{12,14},{14,10},{10,6},{6,2},{2,0},{1,5},{5,9},... | collective-permute-start | bytes 2273288 | tf_op jit(solution)/shard_map/ppermute | solution.py:109
  35.4 14.6 %collective-permute-done.5 = bf16[80,4736]{1,0:T(8,128)(2,1)S(1)} collective-permute-done((bf16[80,4736]{1,0:T(8,128)(2,1)}, bf16[80,4736]{1,0:T(8,128)(2,1)S(1)}, u32[]{:S(2)}, u32[]{:S(2)}) %collective-permute-start.5) | collective-permute-done | bytes 757792 | tf_op jit(solution)/shard_map/ppermute | solution.py:109
  50.0 1.6 %collective-permute-start.7 = (bf16[80,4736]{1,0:T(8,128)(2,1)S(1)}, bf16[80,4736]{1,0:T(8,128)(2,1)S(1)}, u32[]{:S(2)}, u32[]{:S(2)}) collective-permute-start(bf16[80,4736]{1,0:T(8,128)(2,1)S(1)} %collective-permute-done.5), channel_id=1, source_target_pairs={{0,4},{4,8},{8,12},{12,14},{14,10},{10,6},{6,2},{2,0},{1,5},{5,9},... | collective-permute-start | bytes 2273288 | tf_op jit(solution)/shard_map/ppermute | solution.py:109
  52.2 15.9 %collective-permute-done.7 = bf16[80,4736]{1,0:T(8,128)(2,1)S(1)} collective-permute-done((bf16[80,4736]{1,0:T(8,128)(2,1)S(1)}, bf16[80,4736]{1,0:T(8,128)(2,1)S(1)}, u32[]{:S(2)}, u32[]{:S(2)}) %collective-permute-start.7) | collective-permute-done | bytes 757792 | tf_op jit(solution)/shard_map/ppermute | solution.py:109
  68.1 1.6 %collective-permute-start.13 = (bf16[40,4736]{1,0:T(8,128)(2,1)S(1)}, bf16[40,4736]{1,0:T(8,128)(2,1)S(1)}, u32[]{:S(2)}, u32[]{:S(2)}) collective-permute-start(bf16[40,4736]{1,0:T(8,128)(2,1)S(1)} %slice.106), channel_id=1, source_target_pairs={{0,4},{4,8},{8,12},{12,14},{14,10},{10,6},{6,2},{2,0},{1,5},{5,9},... | collective-permute-start | bytes 1136648 | tf_op jit(solution)/shard_map/ppermute | solution.py:109
  70.5 3.5 %fusion.50 = (bf16[128,4736]{1,0:T(8,128)(2,1)S(1)}, bf16[128,4736]{1,0:T(8,128)(2,1)S(1)}) fusion(bf16[256,4736]{1,0:T(8,128)(2,1)} %collective-permute-done.2), kind=kLoop, calls=%fused_computation.90 | loop fusion | bytes 4849664 | tf_op jit(solution)/shard_map/slice | solution.py:134
  74.1 1.9 %fusion = f32[256,480]{0,1:T(8,128)} fusion(bf16[480,4736]{1,0:T(8,128)(2,1)S(1)} %constant_dynamic-update-slice_fusion, bf16[256,4736]{1,0:T(8,128)(2,1)S(1)} %pad_maximum_fusion.1), kind=kOutput, calls=%fused_computation | convolution fusion | flops 849346560 | bytes 5578752 | tf_op jit(solution)/shard_map/dot_general | solution.py:16
  77.4 1.4 %collective-permute-done.14 = bf16[40,4736]{1,0:T(8,128)(2,1)S(1)} collective-permute-done((bf16[40,4736]{1,0:T(8,128)(2,1)S(1)}, bf16[40,4736]{1,0:T(8,128)(2,1)S(1)}, u32[]{:S(2)}, u32[]{:S(2)}) %collective-permute-start.14) | collective-permute-done | bytes 378912 | tf_op jit(solution)/shard_map/ppermute | solution.py:112
  82.4 1.6 %collective-permute-start.18 = (f32[128,80]{0,1:T(8,128)S(1)}, f32[128,80]{0,1:T(8,128)S(1)}, u32[]{:S(2)}, u32[]{:S(2)}) collective-permute-start(f32[128,80]{0,1:T(8,128)S(1)} %slice.113), channel_id=1, source_target_pairs={{0,16},{16,0},{1,17},{17,1},{2,18},{18,2},{3,19},{19,3},{4,20},{20... | collective-permute-start | bytes 122888 | tf_op jit(solution)/shard_map/ppermute | solution.py:22
  84.0 1.4 %fusion.28 = f32[256,480]{0,1:T(8,128)} fusion(bf16[256,1280]{1,0:T(8,128)(2,1)S(1)} %pad_maximum_fusion.3, bf16[480,4736]{1,0:T(8,128)(2,1)S(1)} %constant_dynamic-update-slice_fusion), kind=kOutput, calls=%fused_computation.26 | convolution fusion | flops 314572800 | bytes 2375680 | tf_op jit(solution)/shard_map/dot_general | solution.py:16
  86.6 3.6 %fusion.14 = f32[256,480]{0,1:T(8,128)S(1)} fusion(f32[256,480]{0,1:T(8,128)} %collective-permute-done.9, bf16[480,4736]{1,0:T(8,128)(2,1)} %copy-done.5, bf16[256,4736]{1,0:T(8,128)(2,1)} %copy-done.4), kind=kOutput, calls=%fused_computation.18 | convolution fusion | flops 849469440 | bytes 6070272 | tf_op jit(solution)/shard_map/dot_general | solution.py:16
  90.3 1.6 %collective-permute-start.10 = (f32[128,480]{0,1:T(8,128)S(1)}, f32[128,480]{0,1:T(8,128)S(1)}, u32[]{:S(2)}, u32[]{:S(2)}) collective-permute-start(f32[128,480]{0,1:T(8,128)S(1)} %slice.102), channel_id=1, source_target_pairs={{0,16},{16,0},{1,17},{17,1},{2,18},{18,2},{3,19},{19,3},{4,20},{20... | collective-permute-start | bytes 737288 | tf_op jit(solution)/shard_map/ppermute | solution.py:22
  91.9 1.9 %convolution_add_fusion = f32[256,480]{0,1:T(8,128)S(1)} fusion(f32[256,480]{0,1:T(8,128)} %collective-permute-done.11, bf16[256,1280]{1,0:T(8,128)(2,1)S(1)} %pad_maximum_fusion.4, bf16[480,4736]{1,0:T(8,128)(2,1)} %copy-done.5), kind=kOutput, calls=%fused_computation.17 | convolution fusion | flops 314695680 | bytes 2867200 | tf_op jit(solution)/shard_map/dot_general | solution.py:16
  94.8 4.5 %collective-permute-done.10 = f32[128,480]{0,1:T(8,128)S(1)} collective-permute-done((f32[128,480]{0,1:T(8,128)S(1)}, f32[128,480]{0,1:T(8,128)S(1)}, u32[]{:S(2)}, u32[]{:S(2)}) %collective-permute-start.10) | collective-permute-done | bytes 245792 | tf_op jit(solution)/shard_map/ppermute | solution.py:22
  99.3 3.6 %collective-permute-done.12 = f32[128,480]{0,1:T(8,128)S(1)} collective-permute-done((f32[128,480]{0,1:T(8,128)S(1)}, f32[128,480]{0,1:T(8,128)S(1)}, u32[]{:S(2)}, u32[]{:S(2)}) %collective-permute-start.12) | collective-permute-done | bytes 245792 | tf_op jit(solution)/shard_map/ppermute | solution.py:22
  104.6 3.9 %collective-permute-start.22 = (f32[2,20]{1,0:T(2,128)S(1)}, f32[2,20]{1,0:T(2,128)S(1)}, u32[]{:S(2)}, u32[]{:S(2)}) collective-permute-start(f32[2,20]{1,0:T(2,128)S(1)} %get-tuple-element.6), channel_id=1, source_target_pairs={{0,14},{2,0},{4,2},{6,4},{8,6},{10,8},{12,10},{14,12},{1,15},{3,1}... | collective-permute-start | bytes 488 | tf_op jit(solution)/shard_map/ppermute | solution.py:12
  108.5 1.5 %collective-permute-start.23 = (f32[2,20]{1,0:T(2,128)S(1)}, f32[2,20]{1,0:T(2,128)S(1)}, u32[]{:S(2)}, u32[]{:S(2)}) collective-permute-start(f32[2,20]{1,0:T(2,128)S(1)} %get-tuple-element.6), channel_id=1, source_target_pairs={{0,15},{1,14},{2,1},{3,0},{4,3},{5,2},{6,5},{7,4},{8,7},{9,6},{10,... | collective-permute-start | bytes 488 | tf_op jit(solution)/shard_map/ppermute | solution.py:189
  (119 shorter events, 29.5 us)
Async XLA Ops:
  3.2 27.8 %collective-permute-start.3 = (bf16[80,4736]{1,0:T(8,128)(2,1)}, bf16[80,4736]{1,0:T(8,128)(2,1)}, u32[]{:S(2)}, u32[]{:S(2)}) collective-permute-start(bf16[80,4736]{1,0:T(8,128)(2,1)} %pad_maximum_fusion.2), channel_id=1, source_target_pairs={{0,4},{4,8},{8,12},{12,14},{14,10},{10,6},{6,2},{2,0},{1,5},{5,9},... | collective-permute-start | bytes 2273288 | tf_op jit(solution)/shard_map/ppermute | solution.py:109
  6.2 26.3 %collective-permute-start.4 = (bf16[80,4736]{1,0:T(8,128)(2,1)}, bf16[80,4736]{1,0:T(8,128)(2,1)}, u32[]{:S(2)}, u32[]{:S(2)}) collective-permute-start(bf16[80,4736]{1,0:T(8,128)(2,1)} %pad_maximum_fusion.2), channel_id=1, source_target_pairs={{4,0},{8,4},{12,8},{14,12},{10,14},{6,10},{2,6},{0,2},{5,1},{9,5},... | collective-permute-start | bytes 2273288 | tf_op jit(solution)/shard_map/ppermute | solution.py:112
  12.6 57.9 %collective-permute-start.2 = (bf16[256,4736]{1,0:T(8,128)(2,1)}, bf16[256,4736]{1,0:T(8,128)(2,1)}, u32[]{:S(2)}, u32[]{:S(2)}) collective-permute-start(bf16[256,4736]{1,0:T(8,128)(2,1)} %maximum_maximum_fusion), channel_id=1, source_target_pairs={{0,16},{16,0},{1,17},{17,1},{2,18},{18,2},{3,19},{19,3},{4,20},{20... | collective-permute-start | bytes 7274504 | tf_op jit(solution)/shard_map/ppermute | solution.py:22
  15.6 9.5 %collective-permute-start.1 = (f32[128,80]{0,1:T(8,128)}, f32[128,80]{0,1:T(8,128)}, u32[]{:S(2)}, u32[]{:S(2)}) collective-permute-start(f32[128,80]{0,1:T(8,128)} %fusion.31), channel_id=1, source_target_pairs={{0,1},{1,0},{2,3},{3,2},{4,5},{5,4},{6,7},{7,6},{8,9},{9,8},{10,11... | collective-permute-start | bytes 122888 | tf_op jit(solution)/shard_map/ppermute | solution.py:22
  16.9 9.7 %collective-permute-start = (f32[128,80]{0,1:T(8,128)}, f32[128,80]{0,1:T(8,128)}, u32[]{:S(2)}, u32[]{:S(2)}) collective-permute-start(f32[128,80]{0,1:T(8,128)} %fusion.4), channel_id=1, source_target_pairs={{0,1},{1,0},{2,3},{3,2},{4,5},{5,4},{6,7},{7,6},{8,9},{9,8},{10,11... | collective-permute-start | bytes 122888 | tf_op jit(solution)/shard_map/ppermute | solution.py:22
  31.0 19.1 %collective-permute-start.5 = (bf16[80,4736]{1,0:T(8,128)(2,1)}, bf16[80,4736]{1,0:T(8,128)(2,1)S(1)}, u32[]{:S(2)}, u32[]{:S(2)}) collective-permute-start(bf16[80,4736]{1,0:T(8,128)(2,1)} %collective-permute-done.3), channel_id=1, source_target_pairs={{0,4},{4,8},{8,12},{12,14},{14,10},{10,6},{6,2},{2,0},{1,5},{5,9},... | collective-permute-start | bytes 2273288 | tf_op jit(solution)/shard_map/ppermute | solution.py:109
  32.5 19.1 %collective-permute-start.6 = (bf16[80,4736]{1,0:T(8,128)(2,1)}, bf16[80,4736]{1,0:T(8,128)(2,1)S(1)}, u32[]{:S(2)}, u32[]{:S(2)}) collective-permute-start(bf16[80,4736]{1,0:T(8,128)(2,1)} %collective-permute-done.4), channel_id=1, source_target_pairs={{4,0},{8,4},{12,8},{14,12},{10,14},{6,10},{2,6},{0,2},{5,1},{9,5},... | collective-permute-start | bytes 2273288 | tf_op jit(solution)/shard_map/ppermute | solution.py:112
  50.0 18.1 %collective-permute-start.7 = (bf16[80,4736]{1,0:T(8,128)(2,1)S(1)}, bf16[80,4736]{1,0:T(8,128)(2,1)S(1)}, u32[]{:S(2)}, u32[]{:S(2)}) collective-permute-start(bf16[80,4736]{1,0:T(8,128)(2,1)S(1)} %collective-permute-done.5), channel_id=1, source_target_pairs={{0,4},{4,8},{8,12},{12,14},{14,10},{10,6},{6,2},{2,0},{1,5},{5,9},... | collective-permute-start | bytes 2273288 | tf_op jit(solution)/shard_map/ppermute | solution.py:109
  51.6 18.2 %collective-permute-start.8 = (bf16[80,4736]{1,0:T(8,128)(2,1)S(1)}, bf16[80,4736]{1,0:T(8,128)(2,1)S(1)}, u32[]{:S(2)}, u32[]{:S(2)}) collective-permute-start(bf16[80,4736]{1,0:T(8,128)(2,1)S(1)} %collective-permute-done.6), channel_id=1, source_target_pairs={{4,0},{8,4},{12,8},{14,12},{10,14},{6,10},{2,6},{0,2},{5,1},{9,5},... | collective-permute-start | bytes 2273288 | tf_op jit(solution)/shard_map/ppermute | solution.py:112
  68.1 9.2 %collective-permute-start.13 = (bf16[40,4736]{1,0:T(8,128)(2,1)S(1)}, bf16[40,4736]{1,0:T(8,128)(2,1)S(1)}, u32[]{:S(2)}, u32[]{:S(2)}) collective-permute-start(bf16[40,4736]{1,0:T(8,128)(2,1)S(1)} %slice.106), channel_id=1, source_target_pairs={{0,4},{4,8},{8,12},{12,14},{14,10},{10,6},{6,2},{2,0},{1,5},{5,9},... | collective-permute-start | bytes 1136648 | tf_op jit(solution)/shard_map/ppermute | solution.py:109
  69.8 8.9 %collective-permute-start.14 = (bf16[40,4736]{1,0:T(8,128)(2,1)S(1)}, bf16[40,4736]{1,0:T(8,128)(2,1)S(1)}, u32[]{:S(2)}, u32[]{:S(2)}) collective-permute-start(bf16[40,4736]{1,0:T(8,128)(2,1)S(1)} %slice.107), channel_id=1, source_target_pairs={{4,0},{8,4},{12,8},{14,12},{10,14},{6,10},{2,6},{0,2},{5,1},{9,5},... | collective-permute-start | bytes 1136648 | tf_op jit(solution)/shard_map/ppermute | solution.py:112
  76.1 10.5 %collective-permute-start.9 = (f32[256,480]{0,1:T(8,128)}, f32[256,480]{0,1:T(8,128)}, u32[]{:S(2)}, u32[]{:S(2)}) collective-permute-start(f32[256,480]{0,1:T(8,128)} %fusion), channel_id=1, source_target_pairs={{0,1},{1,0},{2,3},{3,2},{4,5},{5,4},{6,7},{7,6},{8,9},{9,8},{10,11... | collective-permute-start | bytes 1474568 | tf_op jit(solution)/shard_map/ppermute | solution.py:22
  79.4 1.3 %collective-permute-start.15 = (f32[256,80]{0,1:T(8,128)S(1)}, f32[256,80]{0,1:T(8,128)S(1)}, u32[]{:S(2)}, u32[]{:S(2)}) collective-permute-start(f32[256,80]{0,1:T(8,128)S(1)} %fusion.8), channel_id=1, source_target_pairs={{0,1},{1,0},{2,3},{3,2},{4,5},{5,4},{6,7},{7,6},{8,9},{9,8},{10,11... | collective-permute-start | bytes 245768 | tf_op jit(solution)/shard_map/ppermute | solution.py:22
  79.9 2.2 %collective-permute-start.17 = (f32[256,80]{0,1:T(8,128)S(1)}, f32[256,80]{0,1:T(8,128)S(1)}, u32[]{:S(2)}, u32[]{:S(2)}) collective-permute-start(f32[256,80]{0,1:T(8,128)S(1)} %fusion.37), channel_id=1, source_target_pairs={{0,1},{1,0},{2,3},{3,2},{4,5},{5,4},{6,7},{7,6},{8,9},{9,8},{10,11... | collective-permute-start | bytes 245768 | tf_op jit(solution)/shard_map/ppermute | solution.py:22
  81.5 4.3 %collective-permute-start.16 = (f32[128,80]{0,1:T(8,128)S(1)}, f32[128,80]{0,1:T(8,128)S(1)}, u32[]{:S(2)}, u32[]{:S(2)}) collective-permute-start(f32[128,80]{0,1:T(8,128)S(1)} %slice.110), channel_id=1, source_target_pairs={{0,16},{16,0},{1,17},{17,1},{2,18},{18,2},{3,19},{19,3},{4,20},{20... | collective-permute-start | bytes 122888 | tf_op jit(solution)/shard_map/ppermute | solution.py:22
  82.4 4.1 %collective-permute-start.18 = (f32[128,80]{0,1:T(8,128)S(1)}, f32[128,80]{0,1:T(8,128)S(1)}, u32[]{:S(2)}, u32[]{:S(2)}) collective-permute-start(f32[128,80]{0,1:T(8,128)S(1)} %slice.113), channel_id=1, source_target_pairs={{0,16},{16,0},{1,17},{17,1},{2,18},{18,2},{3,19},{19,3},{4,20},{20... | collective-permute-start | bytes 122888 | tf_op jit(solution)/shard_map/ppermute | solution.py:22
  85.4 6.6 %collective-permute-start.11 = (f32[256,480]{0,1:T(8,128)}, f32[256,480]{0,1:T(8,128)}, u32[]{:S(2)}, u32[]{:S(2)}) collective-permute-start(f32[256,480]{0,1:T(8,128)} %fusion.28), channel_id=1, source_target_pairs={{0,1},{1,0},{2,3},{3,2},{4,5},{5,4},{6,7},{7,6},{8,9},{9,8},{10,11... | collective-permute-start | bytes 1474568 | tf_op jit(solution)/shard_map/ppermute | solution.py:22
  90.3 9.0 %collective-permute-start.10 = (f32[128,480]{0,1:T(8,128)S(1)}, f32[128,480]{0,1:T(8,128)S(1)}, u32[]{:S(2)}, u32[]{:S(2)}) collective-permute-start(f32[128,480]{0,1:T(8,128)S(1)} %slice.102), channel_id=1, source_target_pairs={{0,16},{16,0},{1,17},{17,1},{2,18},{18,2},{3,19},{19,3},{4,20},{20... | collective-permute-start | bytes 737288 | tf_op jit(solution)/shard_map/ppermute | solution.py:22
  93.9 9.0 %collective-permute-start.12 = (f32[128,480]{0,1:T(8,128)S(1)}, f32[128,480]{0,1:T(8,128)S(1)}, u32[]{:S(2)}, u32[]{:S(2)}) collective-permute-start(f32[128,480]{0,1:T(8,128)S(1)} %slice.105), channel_id=1, source_target_pairs={{0,16},{16,0},{1,17},{17,1},{2,18},{18,2},{3,19},{19,3},{4,20},{20... | collective-permute-start | bytes 737288 | tf_op jit(solution)/shard_map/ppermute | solution.py:22
  103.7 6.4 %collective-permute-start.20 = (f32[2,20]{1,0:T(2,128)S(1)}, f32[2,20]{1,0:T(2,128)S(1)}, u32[]{:S(2)}, u32[]{:S(2)}) collective-permute-start(f32[2,20]{1,0:T(2,128)S(1)} %get-tuple-element.5), channel_id=1, source_target_pairs={{0,2},{2,4},{4,6},{6,8},{8,10},{10,12},{12,14},{14,0},{1,3},{3,5},... | collective-permute-start | bytes 488 | tf_op jit(solution)/shard_map/ppermute | solution.py:12
  104.3 5.8 %collective-permute-start.21 = (f32[2,20]{1,0:T(2,128)S(1)}, f32[2,20]{1,0:T(2,128)S(1)}, u32[]{:S(2)}, u32[]{:S(2)}) collective-permute-start(f32[2,20]{1,0:T(2,128)S(1)} %get-tuple-element.5), channel_id=1, source_target_pairs={{0,3},{1,2},{2,5},{3,4},{4,7},{5,6},{6,9},{7,8},{8,11},{9,10},{10,... | collective-permute-start | bytes 488 | tf_op jit(solution)/shard_map/ppermute | solution.py:189
  104.6 5.5 %collective-permute-start.22 = (f32[2,20]{1,0:T(2,128)S(1)}, f32[2,20]{1,0:T(2,128)S(1)}, u32[]{:S(2)}, u32[]{:S(2)}) collective-permute-start(f32[2,20]{1,0:T(2,128)S(1)} %get-tuple-element.6), channel_id=1, source_target_pairs={{0,14},{2,0},{4,2},{6,4},{8,6},{10,8},{12,10},{14,12},{1,15},{3,1}... | collective-permute-start | bytes 488 | tf_op jit(solution)/shard_map/ppermute | solution.py:12
  108.5 3.0 %collective-permute-start.23 = (f32[2,20]{1,0:T(2,128)S(1)}, f32[2,20]{1,0:T(2,128)S(1)}, u32[]{:S(2)}, u32[]{:S(2)}) collective-permute-start(f32[2,20]{1,0:T(2,128)S(1)} %get-tuple-element.6), channel_id=1, source_target_pairs={{0,15},{1,14},{2,1},{3,0},{4,3},{5,2},{6,5},{7,4},{8,7},{9,6},{10,... | collective-permute-start | bytes 488 | tf_op jit(solution)/shard_map/ppermute | solution.py:189
  110.0 1.5 %collective-permute-start.19 = (f32[4,20]{1,0:T(4,128)S(1)}, f32[4,20]{1,0:T(4,128)S(1)}, u32[]{:S(2)}, u32[]{:S(2)}) collective-permute-start(f32[4,20]{1,0:T(4,128)S(1)} %select_reduce_fusion.3), channel_id=1, source_target_pairs={{0,1},{1,0},{2,3},{3,2},{4,5},{5,4},{6,7},{7,6},{8,9},{9,8},{10,11... | collective-permute-start | bytes 968 | tf_op jit(solution)/shard_map/ppermute | solution.py:22
  (15 other events, 114.9 us)

commit v2 on v0

v2 whole, which is shorter than its diff:
```python
import functools

import jax
import jax.numpy as jnp
from jax import lax
from jax.experimental import pallas as pl
from jax.experimental.pallas import tpu as pltpu
from jax.sharding import PartitionSpec as P

QUERIES = 20


def shifted(value, axis, steps):
    count = lax.axis_size(axis)
    pairs = [(source, (source + steps) % count) for source in range(count)]
    return lax.ppermute(value, axis, pairs)


def project_rows(rows, factor):
    return lax.dot_general(
        rows, factor, (((1,), (1,)), ((), ())), preferred_element_type=jnp.float32
    )


def swapped(value, axis):
    return lax.ppermute(value, axis, [(0, 1), (1, 0)])


def one_hot_queries(query_of_row):
    ids = jnp.arange(QUERIES, dtype=jnp.int32)[None, :]
    return (query_of_row[:, None] == ids).astype(jnp.float32)


def query_sums(rows, onehot):
    return jnp.dot(rows, onehot, precision=lax.Precision.HIGHEST, preferred_element_type=jnp.float32)


def gathered(activations, out_grads, act_factor, grad_factor, query_of_row, live_tokens, move_plan):
    slots_in = live_tokens.shape[0]
    block_len = activations.shape[0] // slots_in
    slots_out = slots_in // 2
    half_slots = slots_out // 2
    my_rank = lax.axis_index("dp")
    dp_size = lax.axis_size("dp")
    offsets = jnp.arange(block_len, dtype=jnp.int32)
    live_mask = (offsets[None, :] < live_tokens[:, None]).reshape(-1)
    grad_rows = jnp.where(live_mask[:, None], out_grads, jnp.zeros_like(out_grads))
    grad_all = lax.all_gather(grad_factor, "dp", axis=0, tiled=True)
    act_all = lax.all_gather(act_factor, "dp", axis=0, tiled=True)
    proj_grad = project_rows(grad_rows, grad_all)
    proj_act = project_rows(activations, act_all)
    full_grad, full_act = lax.psum((proj_grad, proj_act), "tensor")
    per_block = (full_grad * full_act).reshape(slots_in, block_len, -1).sum(axis=1)
    slot_scores = query_sums(per_block, one_hot_queries(query_of_row))
    keep, right, left = plan_weights(move_plan, my_rank, dp_size, slots_out, half_slots)
    lower = shifted(pick(right, slot_scores), "dp", 1)
    upper = shifted(pick(left, slot_scores), "dp", -1)
    return pick(keep, slot_scores) + jnp.concatenate([lower, upper], axis=0)


def plan_weights(move_plan, my_rank, dp_size, slots_out, half_slots):
    dest_rank = move_plan[:, 0]
    dest_slot = move_plan[:, 1]
    out_ids = jnp.arange(slots_out, dtype=jnp.int32)[:, None]
    hand_ids = jnp.arange(half_slots, dtype=jnp.int32)[:, None]
    keep = (dest_rank == my_rank)[None, :] & (dest_slot[None, :] == out_ids)
    right = (dest_rank == (my_rank + 1) % dp_size)[None, :] & (dest_slot[None, :] == hand_ids)
    left = (dest_rank == (my_rank + dp_size - 1) % dp_size)[None, :] & (
        dest_slot[None, :] == hand_ids + half_slots
    )
    return keep, right, left


def pick(hits, scores):
    return jnp.where(hits[:, :, None], scores[None, :, :], 0.0).sum(axis=1)


def ring_place(index, count):
    step = lax.div(index, 2)
    return jnp.where(lax.rem(index, 2) == 0, step, count - 1 - step)


def ring_index(place, count):
    place = lax.rem(place, count)
    return jnp.where(place < count // 2, 2 * place, 2 * (count - 1 - place) + 1)


LANES = 128
SUBLANES = 16
QUERY_LANES = 32
DEST_ROWS = 8


def after(value, *others):
    return lax.optimization_barrier((value, *others))[0]


def kernel_call(body, out_shape, in_specs, out_specs, operands, scratch=(), flops=0, limit=24):
    return pl.pallas_call(
        body,
        out_shape=out_shape,
        in_specs=in_specs,
        out_specs=out_specs,
        scratch_shapes=list(scratch),
        compiler_params=pltpu.CompilerParams(vmem_limit_bytes=limit * 1024 * 1024),
        cost_estimate=pl.CostEstimate(flops=flops, bytes_accessed=0, transcendentals=0),
    )(*operands)


def dot_rows(left, right):
    return lax.dot_general(
        left, right, (((1,), (1,)), ((), ())), preferred_element_type=jnp.float32
    )


def halves_kernel(acts, grads, act_factor, grad_factor, first, second, other, sems):
    act_half, grad_half = acts.shape[1] // 2, grads.shape[1] // 2
    cut = first.shape[1]
    group = lax.axis_index("groups")

    def columns(side, width, skip=0, size=None):
        return pl.ds(pl.multiple_of(side * width + skip, LANES), width if size is None else size)

    moves = [
        (act_factor.at[:, columns(group, act_half, 0, cut)], first),
        (act_factor.at[:, columns(group, act_half, cut, act_half - cut)], second.at[:, pl.ds(0, act_half - cut)]),
        (grad_factor.at[:, columns(group, grad_half)], second.at[:, pl.ds(act_half - cut, grad_half)]),
    ]
    size = acts.shape[0] // 4
    for part in range(4):
        some = pl.ds(part * size, size)
        moves += [
            (acts.at[some, columns(1 - group, act_half)], other.at[some, pl.ds(0, act_half)]),
            (grads.at[some, columns(1 - group, grad_half)], other.at[some, pl.ds(act_half, grad_half)]),
        ]
    copies = [pltpu.make_async_copy(src, dst, sems.at[i]) for i, (src, dst) in enumerate(moves)]
    for copy in copies:
        copy.start()
    for copy in copies:
        copy.wait()


def split_cores(act, grad, give, keep, sums, start):
    rows = act.shape[1]
    tokens = sums.shape[0]
    core = lax.axis_index("tensor")
    for i, value in enumerate((act, grad)):
        sums[:, :rows] = value
        for out, side in ((give, 1 - core), (keep, core)):
            some = sums[pl.ds(pl.multiple_of(side * (tokens // 2), LANES), tokens // 2), :]
            out[start + i * rows : start + (i + 1) * rows, :] = some.T[:rows]


def own_rows_kernel(acts, grads, act_factor, grad_factor, give, keep, own, sums):
    act_half, grad_half = acts.shape[1] // 2, grads.shape[1] // 2
    group = lax.axis_index("groups")
    act = dot_rows(acts[...], act_factor[...])
    grad = dot_rows(grads[...], grad_factor[...])
    split_cores(act, grad, give, keep, sums, 0)
    own[:, :act_half] = acts[:, pl.ds(pl.multiple_of(group * act_half, LANES), act_half)]
    own[:, act_half:] = grads[:, pl.ds(pl.multiple_of(group * grad_half, LANES), grad_half)]


def near_own_kernel(count, act_half, tokens, *refs):
    pieces, (factor, give, keep, sums, sems) = refs[:count], refs[count:]
    rows, cut = pieces[0].shape
    copies = []
    for i, piece in enumerate(pieces):
        columns = pl.ds(0, cut) if i % 2 == 0 else pl.ds(cut, factor.shape[1] - cut)
        copies.append(
            pltpu.make_async_copy(piece, factor.at[pl.ds(i // 2 * rows, rows), columns], sems.at[i])
        )
    for copy in copies:
        copy.start()
    for copy in copies:
        copy.wait()
    near_other_kernel(act_half, tokens, factor, give, keep, sums)


def near_other_kernel(act_half, tokens, factor, give, keep, sums):
    act = dot_rows(tokens[:, :act_half], factor[:, :act_half])
    grad = dot_rows(tokens[:, act_half:], factor[:, act_half:])
    split_cores(act, grad, give, keep, sums, 0)


def last_kernel(act_half, own, other, first, second, give, keep, sums):
    rows, cut = first.shape
    rest = act_half - cut
    for i, tokens in enumerate((own, other)):
        act = dot_rows(tokens[:, :cut], first[...]) + dot_rows(tokens[:, cut:act_half], second[:, :rest])
        grad = dot_rows(tokens[:, act_half:], second[:, rest:])
        split_cores(act, grad, give, keep, sums, 2 * rows * i)


def scores_kernel(block_len, dp_size, live_tokens, move_plan, query, *refs):
    exact = functools.partial(
        lax.dot_general, precision=lax.Precision.HIGHEST, preferred_element_type=jnp.float32
    )
    sets, out = refs[:-1], refs[-1]
    rows = sets[0].shape[0] // 2
    products = []
    for terms in (sets[:2], sets[2:5], sets[5:8], sets[8:]):
        size = terms[-1].shape[0]
        total = sum(term[:size, :] for term in terms)
        products.append(total[: size // 2] * total[size // 2 :])
    product = jnp.concatenate(products, axis=0)
    my_rank = lax.axis_index("dp")
    place = ring_place(my_rank, dp_size)
    distances = [0]
    for distance in range(1, dp_size // 2):
        distances += [-distance, distance]
    distances.append(dp_size // 2)
    ids = lax.broadcasted_iota(jnp.int32, (rows, QUERY_LANES), 1)
    onehots = []
    for distance in distances:
        start = ring_index(place + distance + dp_size, dp_size) * rows
        onehots.append((query[pl.ds(pl.multiple_of(start, 8), rows), :] == ids).astype(jnp.float32))
    sums = exact(jnp.concatenate(onehots, axis=0), product, (((0,), (0,)), ((), ())))
    tokens = sums.shape[1]
    slots = tokens // block_len
    token = lax.broadcasted_iota(jnp.int32, (3 * DEST_ROWS, tokens), 1)
    dest = lax.broadcasted_iota(jnp.int32, (3 * DEST_ROWS, tokens), 0)
    moves = jnp.zeros((3 * DEST_ROWS, tokens), jnp.float32)
    right = jnp.where(my_rank == dp_size - 1, 0, my_rank + 1)
    for slot in range(slots):
        mine = lax.axis_index("tensor") * slots + slot
        rank = move_plan[mine, 0]
        side = jnp.where(rank == my_rank, 0, jnp.where(rank == right, 1, 2))
        target = jnp.where(rank >= 0, side * DEST_ROWS + move_plan[mine, 1], -1)
        start = slot * block_len
        hit = (token >= start) & (token < start + live_tokens[mine]) & (dest == target)
        moves = moves + hit.astype(jnp.float32)
    out[...] = exact(moves, sums, (((1,), (1,)), ((), ())))


def ringed(activations, out_grads, act_factor, grad_factor, query_of_row, live_tokens, move_plan):
    dp_size = lax.axis_size("dp")
    slots_in = live_tokens.shape[0]
    tokens, act_width = activations.shape
    grad_width = out_grads.shape[1]
    rows = act_factor.shape[0]
    block_len = tokens // slots_in
    slots_out = slots_in // 2
    half = tokens // 2
    act_half, grad_half = act_width // 2, grad_width // 2
    width = act_half + grad_half
    cut = (width // 2) // LANES * LANES
    steps = dp_size // 2
    any_space = pl.BlockSpec(memory_space=pl.ANY)
    whole = pl.BlockSpec(memory_space=pltpu.VMEM)
    bf16, f32 = jnp.bfloat16, jnp.float32

    order = list(range(0, dp_size, 2)) + list(range(dp_size - 1, 0, -2))
    ahead = [(order[i], order[(i + 1) % dp_size]) for i in range(dp_size)]
    back = [(b, a) for a, b in ahead]
    smem = pl.BlockSpec(memory_space=pltpu.SMEM)

    first, second, other = kernel_call(
        halves_kernel,
        [
            jax.ShapeDtypeStruct((rows, cut), bf16),
            jax.ShapeDtypeStruct((rows, width - cut), bf16),
            jax.ShapeDtypeStruct((tokens, width), bf16),
        ],
        [any_space] * 4,
        [whole] * 3,
        (activations, out_grads, act_factor, grad_factor),
        scratch=[pltpu.SemaphoreType.DMA((11,))],
        limit=60,
    )
    other = swapped(other, "groups")

    def sent(pieces, pairs):
        return tuple(lax.ppermute(piece, "dp", pairs) for piece in pieces)

    start = (first, second)
    from_back, from_ahead = [start, sent(start, ahead)], [start, sent(start, back)]
    from_back.append(sent(from_back[1], ahead))
    from_ahead.append(sent(from_ahead[1], back))

    def work(factor_rows, features):
        return 2 * factor_rows * tokens * features

    halves = [jax.ShapeDtypeStruct((2 * rows, half), f32)] * 2
    sums = pltpu.VMEM((tokens, LANES), f32)
    own_give, own_keep, own = kernel_call(
        own_rows_kernel,
        halves + [jax.ShapeDtypeStruct((tokens, width), bf16)],
        [whole] * 4,
        [whole] * 3,
        lax.optimization_barrier(
            (activations, out_grads, act_factor, grad_factor, *from_back[1], *from_ahead[1])
        )[:4],
        scratch=[sums],
        flops=work(rows, 2 * width),
    )
    own_got = swapped(own_give, "tensor")

    def tied(pieces, *others):
        return lax.optimization_barrier((*pieces, *others))[: len(pieces)]

    def wide_sums(count):
        return pltpu.VMEM((tokens, -(-count // LANES) * LANES), f32)

    def against_own(pieces):
        count = rows * len(pieces) // 2
        factor, give, keep = kernel_call(
            functools.partial(near_own_kernel, len(pieces), act_half),
            [jax.ShapeDtypeStruct((count, width), bf16)] + [jax.ShapeDtypeStruct((2 * count, half), f32)] * 2,
            [whole] + [any_space] * len(pieces),
            [whole] * 3,
            (own, *pieces),
            scratch=[wide_sums(count), pltpu.SemaphoreType.DMA((len(pieces),))],
            flops=work(count, width),
        )
        return factor, give, keep, swapped(give, "tensor")

    def against_other(factor, other):
        count = factor.shape[0]
        give, keep = kernel_call(
            functools.partial(near_other_kernel, act_half),
            [jax.ShapeDtypeStruct((2 * count, half), f32)] * 2,
            [whole] * 2,
            [whole] * 2,
            (other, factor),
            scratch=[wide_sums(count)],
            flops=work(count, width),
        )
        return swapped(keep + swapped(give, "tensor"), "groups"), keep

    for distance in range(2, steps - 2):
        from_back.append(sent(from_back[distance], ahead))
        from_ahead.append(sent(from_ahead[distance], back))
    from_back.append(sent(tied(from_back[steps - 2], own_give), ahead))
    from_ahead.append(sent(tied(from_ahead[steps - 2], own_give), back))
    near_pieces = []
    for distance in range(1, steps - 1):
        near_pieces += [*from_back[distance], *from_ahead[distance]]
    near, near_give, near_keep, near_got = against_own(near_pieces)
    far_pieces = [*from_back[steps - 1], *from_ahead[steps - 1]]
    last_first, last_second = tied((from_back[-1][0], from_ahead[-1][1]), near_give)
    last = [lax.ppermute(last_first, "dp", ahead), lax.ppermute(last_second, "dp", back)]
    far, far_give, far_keep, far_got = against_own(far_pieces)
    other = after(other, far)
    near_other, near_done = against_other(near, other)
    far_other, _ = against_other(far, after(other, near_done))

    last_give, last_keep = kernel_call(
        functools.partial(last_kernel, act_half),
        [jax.ShapeDtypeStruct((4 * rows, half), f32)] * 2,
        [whole] * 4,
        [whole] * 2,
        (own, other, *last),
        scratch=[sums],
        flops=16 * 2 * work(rows, width),
    )
    last_got = swapped(last_give, "tensor")
    last_other = swapped(last_keep[2 * rows :] + last_got[2 * rows :], "groups")

    moved = kernel_call(
        functools.partial(scores_kernel, block_len, dp_size),
        jax.ShapeDtypeStruct((3 * DEST_ROWS, QUERY_LANES), f32),
        [smem, smem] + [whole] * 12,
        whole,
        (live_tokens, move_plan, query_of_row.reshape(-1, 1), own_keep, own_got, near_keep, near_got,
         near_other, far_keep, far_got, far_other, last_keep, last_got, last_other),
    )
    moved = moved + swapped(moved, "tensor")
    kept, right, left = (moved[i * DEST_ROWS : (i + 1) * DEST_ROWS] for i in range(3))
    total = kept + shifted(right, "dp", 1) + shifted(left, "dp", -1)
    return total[:slots_out, :QUERIES]


def shards(activations, out_grads, act_factor, grad_factor, query_of_row, live_tokens, move_plan):
    args = (activations, out_grads, act_factor, grad_factor, query_of_row, live_tokens, move_plan)
    dp_size = lax.axis_size("dp")
    tokens, act_width = activations.shape
    grad_width = out_grads.shape[1]
    rows = act_factor.shape[0]
    slots_in = live_tokens.shape[0]
    fits = (
        lax.axis_size("groups") == 2
        and lax.axis_size("tensor") == 2
        and dp_size % 2 == 0
        and 6 <= dp_size <= 16
        and act_width % (2 * LANES) == 0
        and grad_width % (2 * LANES) == 0
        and tokens == 2 * LANES
        and rows % SUBLANES == 0
        and slots_in % 4 == 0
        and slots_in <= 2 * DEST_ROWS
    )
    return ringed(*args) if fits else gathered(*args)


def solution(mesh):
    return jax.shard_map(
        shards,
        mesh=mesh,
        in_specs=(
            P(("groups", "dp"), "tensor"),
            P(("groups", "dp"), "tensor"),
            P("dp", "tensor"),
            P("dp", "tensor"),
            P(),
            P(("groups", "dp")),
            P(("groups", "dp"), None),
        ),
        out_specs=P(("groups", "dp"), None),
        check_vma=False,
    )
```

time: 256 us -> 98.9 us (0.39)
  waiting for transfers between devices: 210 us -> 54.8 us
  starting transfers between devices: 4.59 us -> 26.4 us
  Pallas kernels: 0 us -> 13.9 us
  other arithmetic: 13.3 us -> 0.08 us
  between operations: 13.2 us -> 0.18 us
  matrix products: 11.8 us -> 0 us
    all_gather x2 -> x0, waiting for transfers between devices: 190 us -> none  [the longest x1 127 us: shards(): act_all = lax.all_gather(act_factor, 'dp', axis=0, tiled=True)]
    ppermute x0 -> x25, waiting for transfers between devices: none -> 48.5 us  [the longest x12 35.9 us: sent(): return tuple((lax.ppermute(piece, 'dp', pairs) for piece in pieces))]
    ppermute x0 -> x25, starting transfers between devices: none -> 22.8 us  [the longest x12 13.2 us: sent(): return tuple((lax.ppermute(piece, 'dp', pairs) for piece in pieces))]
    pallas_call x0 -> x8, Pallas kernels: none -> 13.9 us  [kernel_call(): pl.pallas_call(body, out_shape=out_shape, in_specs=in_specs, out_specs=ou...]
    psum x1 -> x0, waiting for transfers between devices: 13.1 us -> none  [shards(): full_grad, full_act = lax.psum((proj_grad, proj_act), 'tensor')]
    dot_general x3 -> x0, matrix products: 11.8 us -> none  [the longest x2 10.8 us: project_rows(): lax.dot_general(rows, factor, (((1,), (1,)), ((), ())), preferred_element...]
    select_n x6 -> x0, other arithmetic: 3.9 us -> none  [the longest x1 1.33 us: shards(): jnp.where(keep_valid[:, None], own_scores, jnp.concatenate([lower_scores,...]
    reduce_or x2 -> x0, other arithmetic: 2.7 us -> none  [the longest x1 1.41 us: shards(): right_valid = jnp.any(right_hits, axis=1)]
  transfers between devices with their start and end apart: 5 -> 27, of which waited for: 4 -> 11; matrix products, arithmetic and copies ran while one was open for 6% -> 0% of each run, Pallas kernels for 0% -> 9%
where the time goes in v2:
time: 98.9 us; the launch traced here: 98.8 us
  waiting for transfers between devices  54.8 us (55%)
  starting transfers between devices  26.4 us (27%)
  Pallas kernels  13.9 us (14%)
  local copies, waits for them, and re-layouts  3.39 us (3%)
    ppermute x12, waiting for transfers between devices, sent(): return tuple((lax.ppermute(piece, 'dp', pairs) for piece in pieces))  35.9 us
    pallas_call x8, Pallas kernels, kernel_call(): pl.pallas_call(body, out_shape=out_shape, in_specs=in_specs, out_specs=ou...  13.9 us
    ppermute x12, starting transfers between devices, sent(): return tuple((lax.ppermute(piece, 'dp', pairs) for piece in pieces))  13.2 us
    ppermute x11, waiting for transfers between devices, swapped(): return lax.ppermute(value, axis, [(0, 1), (1, 0)])  12.6 us
    ppermute x11, starting transfers between devices, swapped(): return lax.ppermute(value, axis, [(0, 1), (1, 0)])  7.56 us
    ppermute x2, waiting for transfers between devices, shifted(): return lax.ppermute(value, axis, pairs)  6.3 us
    ppermute x2, starting transfers between devices, shifted(): return lax.ppermute(value, axis, pairs)  3.58 us
    unnamed x15, local copies, waits for them, and re-layouts  2.67 us
  transfers between devices with their start and end apart: 27, of which 11 were waited for; matrix products, arithmetic and copies ran while one was open for 0% of the time, Pallas kernels for 9%

profile of v2, /device:TPU:0, one launch (start us, length us, event | category | flops | bytes accessed | tf_op | source)
XLA Modules:
  0.0 98.8 jit_solution(14487568418858019527)
XLA Ops:
  0.0 3.8 %shard_map.73 = (bf16[80,2304]{1,0:T(8,128)(2,1)}, bf16[80,2432]{1,0:T(8,128)(2,1)}, bf16[256,4736]{1,0:T(8,128)(2,1)}) custom-call(bf16[256,6912]{1,0:T(8,128)(2,1)} %acts.2, bf16[256,2560]{1,0:T(8,128)(2,1)} %grads.2, bf16[80,6912]{1,0:T(8,128)(2,1)} %act_factor.2, bf16[80,2560]{1,0:T(8,128)(2,1)} %grad_factor.2), custom_call_target="tpu_custom_call" | custom-call | tf_op jit(solution)/shard_map/pallas_call | solution.py:99
  3.8 3.0 %collective-permute-start.10 = (bf16[256,4736]{1,0:T(8,128)(2,1)}, bf16[256,4736]{1,0:T(8,128)(2,1)S(1)}, u32[]{:S(2)}, u32[]{:S(2)}) collective-permute-start(bf16[256,4736]{1,0:T(8,128)(2,1)} %get-tuple-element.46), channel_id=1, source_target_pairs={{0,16},{16,0},{1,17},{17,1},{2,18},{18,2},{3,19},{19,3},{4,20},{20... | collective-permute-start | bytes 7274504 | tf_op jit(solution)/shard_map/ppermute | solution.py:26
  6.8 1.5 %collective-permute-start.3 = (bf16[80,2432]{1,0:T(8,128)(2,1)}, bf16[80,2432]{1,0:T(8,128)(2,1)S(1)}, u32[]{:S(2)}, u32[]{:S(2)}) collective-permute-start(bf16[80,2432]{1,0:T(8,128)(2,1)} %get-tuple-element.36), channel_id=1, source_target_pairs={{4,0},{8,4},{12,8},{14,12},{10,14},{6,10},{2,6},{0,2},{5,1},{9,5},... | collective-permute-start | bytes 1167368 | tf_op jit(solution)/shard_map/ppermute | solution.py:274
  8.9 1.5 %collective-permute-start.2 = (bf16[80,2304]{1,0:T(8,128)(2,1)}, bf16[80,2304]{1,0:T(8,128)(2,1)S(1)}, u32[]{:S(2)}, u32[]{:S(2)}) collective-permute-start(bf16[80,2304]{1,0:T(8,128)(2,1)} %get-tuple-element.35), channel_id=1, source_target_pairs={{4,0},{8,4},{12,8},{14,12},{10,14},{6,10},{2,6},{0,2},{5,1},{9,5},... | collective-permute-start | bytes 1105928 | tf_op jit(solution)/shard_map/ppermute | solution.py:274
  10.9 8.1 %collective-permute-done.3.refs_3_ = bf16[80,2432]{1,0:T(8,128)(2,1)S(1)} collective-permute-done((bf16[80,2432]{1,0:T(8,128)(2,1)}, bf16[80,2432]{1,0:T(8,128)(2,1)S(1)}, u32[]{:S(2)}, u32[]{:S(2)}) %collective-permute-start.3) | collective-permute-done | bytes 389152 | tf_op jit(solution)/shard_map/ppermute | solution.py:274
  19.0 1.5 %collective-permute-start.8 = (bf16[80,2432]{1,0:T(8,128)(2,1)S(1)}, bf16[80,2432]{1,0:T(8,128)(2,1)S(1)}, u32[]{:S(2)}, u32[]{:S(2)}) collective-permute-start(bf16[80,2432]{1,0:T(8,128)(2,1)S(1)} %collective-permute-done.3.refs_3_), channel_id=1, source_target_pairs={{4,0},{8,4},{12,8},{14,12},{10,14},{6,10},{2,6},{0,2},{5,1},{9,5},... | collective-permute-start | bytes 1167368 | tf_op jit(solution)/shard_map/ppermute | solution.py:274
  20.5 6.4 %collective-permute-done.2.refs_2_ = bf16[80,2304]{1,0:T(8,128)(2,1)S(1)} collective-permute-done((bf16[80,2304]{1,0:T(8,128)(2,1)}, bf16[80,2304]{1,0:T(8,128)(2,1)S(1)}, u32[]{:S(2)}, u32[]{:S(2)}) %collective-permute-start.2) | collective-permute-done | bytes 368672 | tf_op jit(solution)/shard_map/ppermute | solution.py:274
  26.9 1.5 %collective-permute-start.7 = (bf16[80,2304]{1,0:T(8,128)(2,1)S(1)}, bf16[80,2304]{1,0:T(8,128)(2,1)S(1)}, u32[]{:S(2)}, u32[]{:S(2)}) collective-permute-start(bf16[80,2304]{1,0:T(8,128)(2,1)S(1)} %collective-permute-done.2.refs_2_), channel_id=1, source_target_pairs={{4,0},{8,4},{12,8},{14,12},{10,14},{6,10},{2,6},{0,2},{5,1},{9,5},... | collective-permute-start | bytes 1105928 | tf_op jit(solution)/shard_map/ppermute | solution.py:274
  28.9 1.6 %collective-permute-start.5 = (bf16[80,2304]{1,0:T(8,128)(2,1)S(1)}, bf16[80,2304]{1,0:T(8,128)(2,1)S(1)}, u32[]{:S(2)}, u32[]{:S(2)}) collective-permute-start(bf16[80,2304]{1,0:T(8,128)(2,1)S(1)} %collective-permute-done.refs_0_), channel_id=1, source_target_pairs={{0,4},{4,8},{8,12},{12,14},{14,10},{10,6},{6,2},{2,0},{1,5},{5,9},... | collective-permute-start | bytes 1105928 | tf_op jit(solution)/shard_map/ppermute | solution.py:274
  33.1 1.5 %shard_map.74 = (f32[160,128]{1,0:T(8,128)S(1)}, f32[160,128]{1,0:T(8,128)S(1)}, bf16[256,4736]{1,0:T(8,128)(2,1)S(1)}) custom-call(bf16[256,6912]{1,0:T(8,128)(2,1)S(1)} %copy-done, bf16[256,2560]{1,0:T(8,128)(2,1)S(1)} %copy-done.1, bf16[80,6912]{1,0:T(8,128)(2,1)S(1)} %copy-done.2, bf16[80,2560]{1,0:T(8,128)(2,1)S(1)} %copy-done.3), custom_call_target="tpu_custom_call" | custom-call | flops 387973120 | tf_op jit(solution)/shard_map/pallas_call | solution.py:99
  34.6 7.0 %collective-permute-done.7.refs_6_ = bf16[80,2304]{1,0:T(8,128)(2,1)S(1)} collective-permute-done((bf16[80,2304]{1,0:T(8,128)(2,1)S(1)}, bf16[80,2304]{1,0:T(8,128)(2,1)S(1)}, u32[]{:S(2)}, u32[]{:S(2)}) %collective-permute-start.7) | collective-permute-done | bytes 368672 | tf_op jit(solution)/shard_map/ppermute | solution.py:274
  41.7 1.5 %collective-permute-start.14 = (bf16[80,2432]{1,0:T(8,128)(2,1)S(1)}, bf16[80,2432]{1,0:T(8,128)(2,1)S(1)}, u32[]{:S(2)}, u32[]{:S(2)}) collective-permute-start(bf16[80,2432]{1,0:T(8,128)(2,1)S(1)} %collective-permute-done.8.refs_7_), channel_id=1, source_target_pairs={{4,0},{8,4},{12,8},{14,12},{10,14},{6,10},{2,6},{0,2},{5,1},{9,5},... | collective-permute-start | bytes 1167368 | tf_op jit(solution)/shard_map/ppermute | solution.py:274
  44.7 1.6 %collective-permute-start.12 = (bf16[80,2432]{1,0:T(8,128)(2,1)S(1)}, bf16[80,2432]{1,0:T(8,128)(2,1)S(1)}, u32[]{:S(2)}, u32[]{:S(2)}) collective-permute-start(bf16[80,2432]{1,0:T(8,128)(2,1)S(1)} %collective-permute-done.6.refs_5_), channel_id=1, source_target_pairs={{0,4},{4,8},{8,12},{12,14},{14,10},{10,6},{6,2},{2,0},{1,5},{5,9},... | collective-permute-start | bytes 1167368 | tf_op jit(solution)/shard_map/ppermute | solution.py:274
  46.7 1.9 %shard_map.75 = (bf16[320,4736]{1,0:T(8,128)(2,1)S(1)}, f32[640,128]{1,0:T(8,128)S(1)}, f32[640,128]{1,0:T(8,128)S(1)}) custom-call(bf16[256,4736]{1,0:T(8,128)(2,1)S(1)} %get-tuple-element.43.tokens.own, bf16[80,2304]{1,0:T(8,128)(2,1)S(1)} %collective-permute-done.refs_0_, bf16[80,2432]{1,0:T(8,128)(2,1)S(1)} %collective-permute-done.1.refs_1_, ...), custom_call_target="tpu_custom_call" | custom-call | flops 775946240 | tf_op jit(solution)/shard_map/pallas_call | solution.py:99
  48.6 7.0 %collective-permute-done.11.refs_0_ = bf16[80,2304]{1,0:T(8,128)(2,1)S(1)} collective-permute-done((bf16[80,2304]{1,0:T(8,128)(2,1)S(1)}, bf16[80,2304]{1,0:T(8,128)(2,1)S(1)}, u32[]{:S(2)}, u32[]{:S(2)}) %collective-permute-start.11) | collective-permute-done | bytes 368672 | tf_op jit(solution)/shard_map/ppermute | solution.py:274
  55.7 1.6 %collective-permute-start.21 = (bf16[80,2432]{1,0:T(8,128)(2,1)S(1)}, bf16[80,2432]{1,0:T(8,128)(2,1)S(1)}, u32[]{:S(2)}, u32[]{:S(2)}) collective-permute-start(bf16[80,2432]{1,0:T(8,128)(2,1)S(1)} %collective-permute-done.14.refs_3_), channel_id=1, source_target_pairs={{4,0},{8,4},{12,8},{14,12},{10,14},{6,10},{2,6},{0,2},{5,1},{9,5},... | collective-permute-start | bytes 1167368 | tf_op jit(solution)/shard_map/ppermute | solution.py:342
  57.7 3.9 %collective-permute-done.13.refs_2_ = bf16[80,2304]{1,0:T(8,128)(2,1)S(1)} collective-permute-done((bf16[80,2304]{1,0:T(8,128)(2,1)S(1)}, bf16[80,2304]{1,0:T(8,128)(2,1)S(1)}, u32[]{:S(2)}, u32[]{:S(2)}) %collective-permute-start.13) | collective-permute-done | bytes 368672 | tf_op jit(solution)/shard_map/ppermute | solution.py:274
  61.5 2.5 %collective-permute-done.12.refs_1_ = bf16[80,2432]{1,0:T(8,128)(2,1)S(1)} collective-permute-done((bf16[80,2432]{1,0:T(8,128)(2,1)S(1)}, bf16[80,2432]{1,0:T(8,128)(2,1)S(1)}, u32[]{:S(2)}, u32[]{:S(2)}) %collective-permute-start.12) | collective-permute-done | bytes 389152 | tf_op jit(solution)/shard_map/ppermute | solution.py:274
  65.2 1.6 %shard_map.77 = (f32[640,128]{1,0:T(8,128)S(1)}, f32[640,128]{1,0:T(8,128)S(1)}) custom-call(bf16[256,4736]{1,0:T(8,128)(2,1)S(1)} %collective-permute-done.10.tokens.other, bf16[320,4736]{1,0:T(8,128)(2,1)S(1)} %get-tuple-element.53.factor), custom_call_target="tpu_custom_call" | custom-call | flops 775946240 | tf_op jit(solution)/shard_map/pallas_call | solution.py:99
  68.5 1.6 %shard_map.79 = (f32[320,128]{1,0:T(8,128)S(1)}, f32[320,128]{1,0:T(8,128)S(1)}) custom-call(bf16[256,4736]{1,0:T(8,128)(2,1)S(1)} %get-tuple-element.43.tokens.own, bf16[256,4736]{1,0:T(8,128)(2,1)S(1)} %collective-permute-done.10.tokens.other, bf16[80,2304]{1,0:T(8,128)(2,1)S(1)} %collective-permute-done.20.first, ...), custom_call_target="tpu_custom_call" | custom-call | flops 6207569920 | tf_op jit(solution)/shard_map/pallas_call | solution.py:99
  71.9 1.6 %collective-permute-start.19 = (f32[320,128]{1,0:T(8,128)S(1)}, f32[320,128]{1,0:T(8,128)S(1)}, u32[]{:S(2)}, u32[]{:S(2)}) collective-permute-start(f32[320,128]{1,0:T(8,128)S(1)} %add.19), channel_id=1, source_target_pairs={{0,16},{16,0},{1,17},{17,1},{2,18},{18,2},{3,19},{19,3},{4,20},{20... | collective-permute-start | bytes 491528 | tf_op jit(solution)/shard_map/ppermute | solution.py:26
  74.4 11.4 %collective-permute-done.23.refs_10_ = f32[160,128]{1,0:T(8,128)S(1)} collective-permute-done((f32[160,128]{1,0:T(8,128)S(1)}, f32[160,128]{1,0:T(8,128)S(1)}, u32[]{:S(2)}, u32[]{:S(2)}) %collective-permute-start.23) | collective-permute-done | bytes 81952 | tf_op jit(solution)/shard_map/ppermute | solution.py:26
  88.3 3.6 %collective-permute-start.26 = (f32[8,32]{1,0:T(8,128)S(1)}, f32[8,32]{1,0:T(8,128)S(1)}, u32[]{:S(2)}, u32[]{:S(2)}) collective-permute-start(f32[8,32]{1,0:T(8,128)S(1)} %get-tuple-element.66), channel_id=1, source_target_pairs={{0,14},{2,0},{4,2},{6,4},{8,6},{10,8},{12,10},{14,12},{1,15},{3,1}... | collective-permute-start | bytes 3080 | tf_op jit(solution)/shard_map/ppermute | solution.py:16
  93.2 5.0 %collective-permute-done.25 = f32[8,32]{1,0:T(8,128)S(1)} collective-permute-done((f32[8,32]{1,0:T(8,128)S(1)}, f32[8,32]{1,0:T(8,128)S(1)}, u32[]{:S(2)}, u32[]{:S(2)}) %collective-permute-start.25) | collective-permute-done | bytes 1056 | tf_op jit(solution)/shard_map/ppermute | solution.py:16
  (61 shorter events, 16.5 us)
Async XLA Ops:
  3.8 61.4 %collective-permute-start.10 = (bf16[256,4736]{1,0:T(8,128)(2,1)}, bf16[256,4736]{1,0:T(8,128)(2,1)S(1)}, u32[]{:S(2)}, u32[]{:S(2)}) collective-permute-start(bf16[256,4736]{1,0:T(8,128)(2,1)} %get-tuple-element.46), channel_id=1, source_target_pairs={{0,16},{16,0},{1,17},{17,1},{2,18},{18,2},{3,19},{19,3},{4,20},{20... | collective-permute-start | bytes 7274504 | tf_op jit(solution)/shard_map/ppermute | solution.py:26
  6.8 12.2 %collective-permute-start.3 = (bf16[80,2432]{1,0:T(8,128)(2,1)}, bf16[80,2432]{1,0:T(8,128)(2,1)S(1)}, u32[]{:S(2)}, u32[]{:S(2)}) collective-permute-start(bf16[80,2432]{1,0:T(8,128)(2,1)} %get-tuple-element.36), channel_id=1, source_target_pairs={{4,0},{8,4},{12,8},{14,12},{10,14},{6,10},{2,6},{0,2},{5,1},{9,5},... | collective-permute-start | bytes 1167368 | tf_op jit(solution)/shard_map/ppermute | solution.py:274
  8.3 20.1 %collective-permute-start.1 = (bf16[80,2432]{1,0:T(8,128)(2,1)}, bf16[80,2432]{1,0:T(8,128)(2,1)S(1)}, u32[]{:S(2)}, u32[]{:S(2)}) collective-permute-start(bf16[80,2432]{1,0:T(8,128)(2,1)} %get-tuple-element.36), channel_id=1, source_target_pairs={{0,4},{4,8},{8,12},{12,14},{14,10},{10,6},{6,2},{2,0},{1,5},{5,9},... | collective-permute-start | bytes 1167368 | tf_op jit(solution)/shard_map/ppermute | solution.py:274
  8.9 18.0 %collective-permute-start.2 = (bf16[80,2304]{1,0:T(8,128)(2,1)}, bf16[80,2304]{1,0:T(8,128)(2,1)S(1)}, u32[]{:S(2)}, u32[]{:S(2)}) collective-permute-start(bf16[80,2304]{1,0:T(8,128)(2,1)} %get-tuple-element.35), channel_id=1, source_target_pairs={{4,0},{8,4},{12,8},{14,12},{10,14},{6,10},{2,6},{0,2},{5,1},{9,5},... | collective-permute-start | bytes 1105928 | tf_op jit(solution)/shard_map/ppermute | solution.py:274
  10.4 18.6 %collective-permute-start = (bf16[80,2304]{1,0:T(8,128)(2,1)}, bf16[80,2304]{1,0:T(8,128)(2,1)S(1)}, u32[]{:S(2)}, u32[]{:S(2)}) collective-permute-start(bf16[80,2304]{1,0:T(8,128)(2,1)} %get-tuple-element.35), channel_id=1, source_target_pairs={{0,4},{4,8},{8,12},{12,14},{14,10},{10,6},{6,2},{2,0},{1,5},{5,9},... | collective-permute-start | bytes 1105928 | tf_op jit(solution)/shard_map/ppermute | solution.py:274
  19.0 22.7 %collective-permute-start.8 = (bf16[80,2432]{1,0:T(8,128)(2,1)S(1)}, bf16[80,2432]{1,0:T(8,128)(2,1)S(1)}, u32[]{:S(2)}, u32[]{:S(2)}) collective-permute-start(bf16[80,2432]{1,0:T(8,128)(2,1)S(1)} %collective-permute-done.3.refs_3_), channel_id=1, source_target_pairs={{4,0},{8,4},{12,8},{14,12},{10,14},{6,10},{2,6},{0,2},{5,1},{9,5},... | collective-permute-start | bytes 1167368 | tf_op jit(solution)/shard_map/ppermute | solution.py:274
  26.9 14.8 %collective-permute-start.7 = (bf16[80,2304]{1,0:T(8,128)(2,1)S(1)}, bf16[80,2304]{1,0:T(8,128)(2,1)S(1)}, u32[]{:S(2)}, u32[]{:S(2)}) collective-permute-start(bf16[80,2304]{1,0:T(8,128)(2,1)S(1)} %collective-permute-done.2.refs_2_), channel_id=1, source_target_pairs={{4,0},{8,4},{12,8},{14,12},{10,14},{6,10},{2,6},{0,2},{5,1},{9,5},... | collective-permute-start | bytes 1105928 | tf_op jit(solution)/shard_map/ppermute | solution.py:274
  28.4 15.7 %collective-permute-start.6 = (bf16[80,2432]{1,0:T(8,128)(2,1)S(1)}, bf16[80,2432]{1,0:T(8,128)(2,1)S(1)}, u32[]{:S(2)}, u32[]{:S(2)}) collective-permute-start(bf16[80,2432]{1,0:T(8,128)(2,1)S(1)} %collective-permute-done.1.refs_1_), channel_id=1, source_target_pairs={{0,4},{4,8},{8,12},{12,14},{14,10},{10,6},{6,2},{2,0},{1,5},{5,9},... | collective-permute-start | bytes 1167368 | tf_op jit(solution)/shard_map/ppermute | solution.py:274
  28.9 15.2 %collective-permute-start.5 = (bf16[80,2304]{1,0:T(8,128)(2,1)S(1)}, bf16[80,2304]{1,0:T(8,128)(2,1)S(1)}, u32[]{:S(2)}, u32[]{:S(2)}) collective-permute-start(bf16[80,2304]{1,0:T(8,128)(2,1)S(1)} %collective-permute-done.refs_0_), channel_id=1, source_target_pairs={{0,4},{4,8},{8,12},{12,14},{14,10},{10,6},{6,2},{2,0},{1,5},{5,9},... | collective-permute-start | bytes 1105928 | tf_op jit(solution)/shard_map/ppermute | solution.py:274
  41.7 14.0 %collective-permute-start.14 = (bf16[80,2432]{1,0:T(8,128)(2,1)S(1)}, bf16[80,2432]{1,0:T(8,128)(2,1)S(1)}, u32[]{:S(2)}, u32[]{:S(2)}) collective-permute-start(bf16[80,2432]{1,0:T(8,128)(2,1)S(1)} %collective-permute-done.8.refs_7_), channel_id=1, source_target_pairs={{4,0},{8,4},{12,8},{14,12},{10,14},{6,10},{2,6},{0,2},{5,1},{9,5},... | collective-permute-start | bytes 1167368 | tf_op jit(solution)/shard_map/ppermute | solution.py:274
  44.1 11.5 %collective-permute-start.11 = (bf16[80,2304]{1,0:T(8,128)(2,1)S(1)}, bf16[80,2304]{1,0:T(8,128)(2,1)S(1)}, u32[]{:S(2)}, u32[]{:S(2)}) collective-permute-start(bf16[80,2304]{1,0:T(8,128)(2,1)S(1)} %collective-permute-done.5.refs_4_), channel_id=1, source_target_pairs={{0,4},{4,8},{8,12},{12,14},{14,10},{10,6},{6,2},{2,0},{1,5},{5,9},... | collective-permute-start | bytes 1105928 | tf_op jit(solution)/shard_map/ppermute | solution.py:274
  44.7 19.3 %collective-permute-start.12 = (bf16[80,2432]{1,0:T(8,128)(2,1)S(1)}, bf16[80,2432]{1,0:T(8,128)(2,1)S(1)}, u32[]{:S(2)}, u32[]{:S(2)}) collective-permute-start(bf16[80,2432]{1,0:T(8,128)(2,1)S(1)} %collective-permute-done.6.refs_5_), channel_id=1, source_target_pairs={{0,4},{4,8},{8,12},{12,14},{14,10},{10,6},{6,2},{2,0},{1,5},{5,9},... | collective-permute-start | bytes 1167368 | tf_op jit(solution)/shard_map/ppermute | solution.py:274
  46.2 15.3 %collective-permute-start.13 = (bf16[80,2304]{1,0:T(8,128)(2,1)S(1)}, bf16[80,2304]{1,0:T(8,128)(2,1)S(1)}, u32[]{:S(2)}, u32[]{:S(2)}) collective-permute-start(bf16[80,2304]{1,0:T(8,128)(2,1)S(1)} %collective-permute-done.7.refs_6_), channel_id=1, source_target_pairs={{4,0},{8,4},{12,8},{14,12},{10,14},{6,10},{2,6},{0,2},{5,1},{9,5},... | collective-permute-start | bytes 1105928 | tf_op jit(solution)/shard_map/ppermute | solution.py:274
  55.7 12.9 %collective-permute-start.21 = (bf16[80,2432]{1,0:T(8,128)(2,1)S(1)}, bf16[80,2432]{1,0:T(8,128)(2,1)S(1)}, u32[]{:S(2)}, u32[]{:S(2)}) collective-permute-start(bf16[80,2432]{1,0:T(8,128)(2,1)S(1)} %collective-permute-done.14.refs_3_), channel_id=1, source_target_pairs={{4,0},{8,4},{12,8},{14,12},{10,14},{6,10},{2,6},{0,2},{5,1},{9,5},... | collective-permute-start | bytes 1167368 | tf_op jit(solution)/shard_map/ppermute | solution.py:342
  57.2 11.3 %collective-permute-start.20 = (bf16[80,2304]{1,0:T(8,128)(2,1)S(1)}, bf16[80,2304]{1,0:T(8,128)(2,1)S(1)}, u32[]{:S(2)}, u32[]{:S(2)}) collective-permute-start(bf16[80,2304]{1,0:T(8,128)(2,1)S(1)} %collective-permute-done.11.refs_0_), channel_id=1, source_target_pairs={{0,4},{4,8},{8,12},{12,14},{14,10},{10,6},{6,2},{2,0},{1,5},{5,9},... | collective-permute-start | bytes 1105928 | tf_op jit(solution)/shard_map/ppermute | solution.py:342
  66.8 3.9 %collective-permute-start.15 = (f32[640,128]{1,0:T(8,128)S(1)}, f32[640,128]{1,0:T(8,128)S(1)}, u32[]{:S(2)}, u32[]{:S(2)}) collective-permute-start(f32[640,128]{1,0:T(8,128)S(1)} %get-tuple-element.55), channel_id=1, source_target_pairs={{0,1},{1,0},{2,3},{3,2},{4,5},{5,4},{6,7},{7,6},{8,9},{9,8},{10,11... | collective-permute-start | bytes 983048 | tf_op jit(solution)/shard_map/ppermute | solution.py:26
  68.0 3.4 %collective-permute-start.18 = (f32[320,128]{1,0:T(8,128)S(1)}, f32[320,128]{1,0:T(8,128)S(1)}, u32[]{:S(2)}, u32[]{:S(2)}) collective-permute-start(f32[320,128]{1,0:T(8,128)S(1)} %get-tuple-element.60), channel_id=1, source_target_pairs={{0,1},{1,0},{2,3},{3,2},{4,5},{5,4},{6,7},{7,6},{8,9},{9,8},{10,11... | collective-permute-start | bytes 491528 | tf_op jit(solution)/shard_map/ppermute | solution.py:26
  70.2 4.1 %collective-permute-start.9 = (f32[640,128]{1,0:T(8,128)S(1)}, f32[640,128]{1,0:T(8,128)S(1)}, u32[]{:S(2)}, u32[]{:S(2)}) collective-permute-start(f32[640,128]{1,0:T(8,128)S(1)} %get-tuple-element.45), channel_id=1, source_target_pairs={{0,1},{1,0},{2,3},{3,2},{4,5},{5,4},{6,7},{7,6},{8,9},{9,8},{10,11... | collective-permute-start | bytes 983048 | tf_op jit(solution)/shard_map/ppermute | solution.py:26
  70.8 15.0 %collective-permute-start.16 = (f32[640,128]{1,0:T(8,128)S(1)}, f32[640,128]{1,0:T(8,128)S(1)}, u32[]{:S(2)}, u32[]{:S(2)}) collective-permute-start(f32[640,128]{1,0:T(8,128)S(1)} %add.18), channel_id=1, source_target_pairs={{0,16},{16,0},{1,17},{17,1},{2,18},{18,2},{3,19},{19,3},{4,20},{20... | collective-permute-start | bytes 983048 | tf_op jit(solution)/shard_map/ppermute | solution.py:26
  71.3 3.0 %collective-permute-start.17 = (f32[320,128]{1,0:T(8,128)S(1)}, f32[320,128]{1,0:T(8,128)S(1)}, u32[]{:S(2)}, u32[]{:S(2)}) collective-permute-start(f32[320,128]{1,0:T(8,128)S(1)} %get-tuple-element.57), channel_id=1, source_target_pairs={{0,1},{1,0},{2,3},{3,2},{4,5},{5,4},{6,7},{7,6},{8,9},{9,8},{10,11... | collective-permute-start | bytes 491528 | tf_op jit(solution)/shard_map/ppermute | solution.py:26
  71.9 13.9 %collective-permute-start.19 = (f32[320,128]{1,0:T(8,128)S(1)}, f32[320,128]{1,0:T(8,128)S(1)}, u32[]{:S(2)}, u32[]{:S(2)}) collective-permute-start(f32[320,128]{1,0:T(8,128)S(1)} %add.19), channel_id=1, source_target_pairs={{0,16},{16,0},{1,17},{17,1},{2,18},{18,2},{3,19},{19,3},{4,20},{20... | collective-permute-start | bytes 491528 | tf_op jit(solution)/shard_map/ppermute | solution.py:26
  73.5 12.3 %collective-permute-start.23 = (f32[160,128]{1,0:T(8,128)S(1)}, f32[160,128]{1,0:T(8,128)S(1)}, u32[]{:S(2)}, u32[]{:S(2)}) collective-permute-start(f32[160,128]{1,0:T(8,128)S(1)} %slice_add_fusion), channel_id=1, source_target_pairs={{0,16},{16,0},{1,17},{17,1},{2,18},{18,2},{3,19},{19,3},{4,20},{20... | collective-permute-start | bytes 245768 | tf_op jit(solution)/shard_map/ppermute | solution.py:26
  88.3 4.9 %collective-permute-start.26 = (f32[8,32]{1,0:T(8,128)S(1)}, f32[8,32]{1,0:T(8,128)S(1)}, u32[]{:S(2)}, u32[]{:S(2)}) collective-permute-start(f32[8,32]{1,0:T(8,128)S(1)} %get-tuple-element.66), channel_id=1, source_target_pairs={{0,14},{2,0},{4,2},{6,4},{8,6},{10,8},{12,10},{14,12},{1,15},{3,1}... | collective-permute-start | bytes 3080 | tf_op jit(solution)/shard_map/ppermute | solution.py:16
  91.9 6.3 %collective-permute-start.25 = (f32[8,32]{1,0:T(8,128)S(1)}, f32[8,32]{1,0:T(8,128)S(1)}, u32[]{:S(2)}, u32[]{:S(2)}) collective-permute-start(f32[8,32]{1,0:T(8,128)S(1)} %get-tuple-element.65), channel_id=1, source_target_pairs={{0,2},{2,4},{4,6},{6,8},{8,10},{10,12},{12,14},{14,0},{1,3},{3,5},... | collective-permute-start | bytes 3080 | tf_op jit(solution)/shard_map/ppermute | solution.py:16
  (10 other events, 99.0 us)

commit v3 on v2

--- a/solution.py
+++ b/solution.py
@@ -221,11 +221,13 @@
     token = lax.broadcasted_iota(jnp.int32, (3 * DEST_ROWS, tokens), 1)
     dest = lax.broadcasted_iota(jnp.int32, (3 * DEST_ROWS, tokens), 0)
     moves = jnp.zeros((3 * DEST_ROWS, tokens), jnp.float32)
-    right = jnp.where(my_rank == dp_size - 1, 0, my_rank + 1)
+    odd = lax.rem(my_rank, 2)
+    partner = jnp.where(odd == 1, my_rank + 1, my_rank - 1 + dp_size)
+    partner = lax.rem(partner, dp_size)
     for slot in range(slots):
         mine = lax.axis_index("tensor") * slots + slot
         rank = move_plan[mine, 0]
-        side = jnp.where(rank == my_rank, 0, jnp.where(rank == right, 1, 2))
+        side = jnp.where(rank == my_rank, 0, jnp.where(rank == partner, 1, 2))
         target = jnp.where(rank >= 0, side * DEST_ROWS + move_plan[mine, 1], -1)
         start = slot * block_len
         hit = (token >= start) & (token < start + live_tokens[mine]) & (dest == target)
@@ -296,8 +298,8 @@
     )
     own_got = swapped(own_give, "tensor")
 
-    def tied(pieces, *others):
-        return lax.optimization_barrier((*pieces, *others))[: len(pieces)]
+    def tied(pieces, other):
+        return [after(piece, other) for piece in pieces]
 
     def wide_sums(count):
         return pltpu.VMEM((tokens, -(-count // LANES) * LANES), f32)
@@ -366,8 +368,10 @@
          near_other, far_keep, far_got, far_other, last_keep, last_got, last_other),
     )
     moved = moved + swapped(moved, "tensor")
-    kept, right, left = (moved[i * DEST_ROWS : (i + 1) * DEST_ROWS] for i in range(3))
-    total = kept + shifted(right, "dp", 1) + shifted(left, "dp", -1)
+    kept, outer, inner = (moved[i * DEST_ROWS : (i + 1) * DEST_ROWS] for i in range(3))
+    outer_pairs = [(d, (d + 1 if d % 2 else d - 1) % dp_size) for d in range(dp_size)]
+    inner_pairs = [(d, d - 1 if d % 2 else d + 1) for d in range(dp_size)]
+    total = kept + lax.ppermute(outer, "dp", outer_pairs) + lax.ppermute(inner, "dp", inner_pairs)
     return total[:slots_out, :QUERIES]
 
 

time: 98.9 us -> 95.4 us (0.965)
  waiting for transfers between devices: 54.8 us -> 51.6 us
    ppermute x2, waiting for transfers between devices: 6.3 us -> 3.6 us  [the longest x1 3.6 us: ringed(): lax.ppermute(outer, 'dp', outer_pairs)]
    ppermute x12, waiting for transfers between devices: 35.9 us -> 33.8 us  [sent(): return tuple((lax.ppermute(piece, 'dp', pairs) for piece in pieces))]
    ppermute x1, waiting for transfers between devices: 0.01 us -> 1.6 us  [ringed(): lax.ppermute(last_first, 'dp', ahead)]
    ppermute x12, starting transfers between devices: 13.2 us -> 12.2 us  [sent(): return tuple((lax.ppermute(piece, 'dp', pairs) for piece in pieces))]
where the time goes in v3:
time: 95.4 us; the launch traced here: 95.3 us
  waiting for transfers between devices  51.6 us (54%)
  starting transfers between devices  26 us (27%)
  Pallas kernels  14 us (15%)
  local copies, waits for them, and re-layouts  3.39 us (4%)
    ppermute x12, waiting for transfers between devices, sent(): return tuple((lax.ppermute(piece, 'dp', pairs) for piece in pieces))  33.8 us
    pallas_call x8, Pallas kernels, kernel_call(): pl.pallas_call(body, out_shape=out_shape, in_specs=in_specs, out_specs=ou...  14 us
    ppermute x11, waiting for transfers between devices, swapped(): return lax.ppermute(value, axis, [(0, 1), (1, 0)])  12.6 us
    ppermute x12, starting transfers between devices, sent(): return tuple((lax.ppermute(piece, 'dp', pairs) for piece in pieces))  12.2 us
    ppermute x11, starting transfers between devices, swapped(): return lax.ppermute(value, axis, [(0, 1), (1, 0)])  7.55 us
    ppermute x1, waiting for transfers between devices, ringed(): lax.ppermute(outer, 'dp', outer_pairs)  3.6 us
    ppermute x1, starting transfers between devices, ringed(): lax.ppermute(outer, 'dp', outer_pairs)  2.7 us
    unnamed x15, local copies, waits for them, and re-layouts  2.67 us
  transfers between devices with their start and end apart: 27, of which 11 were waited for; matrix products, arithmetic and copies ran while one was open for 0% of the time, Pallas kernels for 9%

profile of v3, /device:TPU:0, one launch (start us, length us, event | category | flops | bytes accessed | tf_op | source)
XLA Modules:
  0.0 95.3 jit_solution(2364791035268712299)
XLA Ops:
  0.0 3.8 %shard_map.73 = (bf16[80,2304]{1,0:T(8,128)(2,1)}, bf16[80,2432]{1,0:T(8,128)(2,1)}, bf16[256,4736]{1,0:T(8,128)(2,1)}) custom-call(bf16[256,6912]{1,0:T(8,128)(2,1)} %acts.2, bf16[256,2560]{1,0:T(8,128)(2,1)} %grads.2, bf16[80,6912]{1,0:T(8,128)(2,1)} %act_factor.2, bf16[80,2560]{1,0:T(8,128)(2,1)} %grad_factor.2), custom_call_target="tpu_custom_call" | custom-call | tf_op jit(solution)/shard_map/pallas_call | solution.py:99
  3.8 3.0 %collective-permute-start.10 = (bf16[256,4736]{1,0:T(8,128)(2,1)}, bf16[256,4736]{1,0:T(8,128)(2,1)S(1)}, u32[]{:S(2)}, u32[]{:S(2)}) collective-permute-start(bf16[256,4736]{1,0:T(8,128)(2,1)} %get-tuple-element.46), channel_id=1, source_target_pairs={{0,16},{16,0},{1,17},{17,1},{2,18},{18,2},{3,19},{19,3},{4,20},{20... | collective-permute-start | bytes 7274504 | tf_op jit(solution)/shard_map/ppermute | solution.py:26
  6.8 1.5 %collective-permute-start.3 = (bf16[80,2432]{1,0:T(8,128)(2,1)}, bf16[80,2432]{1,0:T(8,128)(2,1)S(1)}, u32[]{:S(2)}, u32[]{:S(2)}) collective-permute-start(bf16[80,2432]{1,0:T(8,128)(2,1)} %get-tuple-element.36), channel_id=1, source_target_pairs={{4,0},{8,4},{12,8},{14,12},{10,14},{6,10},{2,6},{0,2},{5,1},{9,5},... | collective-permute-start | bytes 1167368 | tf_op jit(solution)/shard_map/ppermute | solution.py:276
  8.9 1.6 %collective-permute-start.1 = (bf16[80,2432]{1,0:T(8,128)(2,1)}, bf16[80,2432]{1,0:T(8,128)(2,1)S(1)}, u32[]{:S(2)}, u32[]{:S(2)}) collective-permute-start(bf16[80,2432]{1,0:T(8,128)(2,1)} %get-tuple-element.36), channel_id=1, source_target_pairs={{0,4},{4,8},{8,12},{12,14},{14,10},{10,6},{6,2},{2,0},{1,5},{5,9},... | collective-permute-start | bytes 1167368 | tf_op jit(solution)/shard_map/ppermute | solution.py:276
  10.9 8.1 %collective-permute-done.3.refs_3_ = bf16[80,2432]{1,0:T(8,128)(2,1)S(1)} collective-permute-done((bf16[80,2432]{1,0:T(8,128)(2,1)}, bf16[80,2432]{1,0:T(8,128)(2,1)S(1)}, u32[]{:S(2)}, u32[]{:S(2)}) %collective-permute-start.3) | collective-permute-done | bytes 389152 | tf_op jit(solution)/shard_map/ppermute | solution.py:276
  19.0 1.5 %collective-permute-start.8 = (bf16[80,2432]{1,0:T(8,128)(2,1)S(1)}, bf16[80,2432]{1,0:T(8,128)(2,1)S(1)}, u32[]{:S(2)}, u32[]{:S(2)}) collective-permute-start(bf16[80,2432]{1,0:T(8,128)(2,1)S(1)} %collective-permute-done.3.refs_3_), channel_id=1, source_target_pairs={{4,0},{8,4},{12,8},{14,12},{10,14},{6,10},{2,6},{0,2},{5,1},{9,5},... | collective-permute-start | bytes 1167368 | tf_op jit(solution)/shard_map/ppermute | solution.py:276
  21.0 7.4 %collective-permute-done.1.refs_1_ = bf16[80,2432]{1,0:T(8,128)(2,1)S(1)} collective-permute-done((bf16[80,2432]{1,0:T(8,128)(2,1)}, bf16[80,2432]{1,0:T(8,128)(2,1)S(1)}, u32[]{:S(2)}, u32[]{:S(2)}) %collective-permute-start.1) | collective-permute-done | bytes 389152 | tf_op jit(solution)/shard_map/ppermute | solution.py:276
  28.9 1.5 %collective-permute-start.7 = (bf16[80,2304]{1,0:T(8,128)(2,1)S(1)}, bf16[80,2304]{1,0:T(8,128)(2,1)S(1)}, u32[]{:S(2)}, u32[]{:S(2)}) collective-permute-start(bf16[80,2304]{1,0:T(8,128)(2,1)S(1)} %collective-permute-done.2.refs_2_), channel_id=1, source_target_pairs={{4,0},{8,4},{12,8},{14,12},{10,14},{6,10},{2,6},{0,2},{5,1},{9,5},... | collective-permute-start | bytes 1105928 | tf_op jit(solution)/shard_map/ppermute | solution.py:276
  33.0 1.6 %shard_map.74 = (f32[160,128]{1,0:T(8,128)S(1)}, f32[160,128]{1,0:T(8,128)S(1)}, bf16[256,4736]{1,0:T(8,128)(2,1)S(1)}) custom-call(bf16[256,6912]{1,0:T(8,128)(2,1)S(1)} %copy-done, bf16[256,2560]{1,0:T(8,128)(2,1)S(1)} %copy-done.1, bf16[80,6912]{1,0:T(8,128)(2,1)S(1)} %copy-done.2, bf16[80,2560]{1,0:T(8,128)(2,1)S(1)} %copy-done.3), custom_call_target="tpu_custom_call" | custom-call | flops 387973120 | tf_op jit(solution)/shard_map/pallas_call | solution.py:99
  35.2 1.5 %collective-permute-start.14 = (bf16[80,2432]{1,0:T(8,128)(2,1)S(1)}, bf16[80,2432]{1,0:T(8,128)(2,1)S(1)}, u32[]{:S(2)}, u32[]{:S(2)}) collective-permute-start(bf16[80,2432]{1,0:T(8,128)(2,1)S(1)} %collective-permute-done.8.refs_7_), channel_id=1, source_target_pairs={{4,0},{8,4},{12,8},{14,12},{10,14},{6,10},{2,6},{0,2},{5,1},{9,5},... | collective-permute-start | bytes 1167368 | tf_op jit(solution)/shard_map/ppermute | solution.py:276
  37.3 7.4 %collective-permute-done.6.refs_5_ = bf16[80,2432]{1,0:T(8,128)(2,1)S(1)} collective-permute-done((bf16[80,2432]{1,0:T(8,128)(2,1)S(1)}, bf16[80,2432]{1,0:T(8,128)(2,1)S(1)}, u32[]{:S(2)}, u32[]{:S(2)}) %collective-permute-start.6) | collective-permute-done | bytes 389152 | tf_op jit(solution)/shard_map/ppermute | solution.py:276
  45.2 1.5 %collective-permute-start.13 = (bf16[80,2304]{1,0:T(8,128)(2,1)S(1)}, bf16[80,2304]{1,0:T(8,128)(2,1)S(1)}, u32[]{:S(2)}, u32[]{:S(2)}) collective-permute-start(bf16[80,2304]{1,0:T(8,128)(2,1)S(1)} %collective-permute-done.7.refs_6_), channel_id=1, source_target_pairs={{4,0},{8,4},{12,8},{14,12},{10,14},{6,10},{2,6},{0,2},{5,1},{9,5},... | collective-permute-start | bytes 1105928 | tf_op jit(solution)/shard_map/ppermute | solution.py:276
  46.7 1.9 %shard_map.75 = (bf16[320,4736]{1,0:T(8,128)(2,1)S(1)}, f32[640,128]{1,0:T(8,128)S(1)}, f32[640,128]{1,0:T(8,128)S(1)}) custom-call(bf16[256,4736]{1,0:T(8,128)(2,1)S(1)} %get-tuple-element.43.tokens.own, bf16[80,2304]{1,0:T(8,128)(2,1)S(1)} %collective-permute-done.refs_0_, bf16[80,2432]{1,0:T(8,128)(2,1)S(1)} %collective-permute-done.1.refs_1_, ...), custom_call_target="tpu_custom_call" | custom-call | flops 775946240 | tf_op jit(solution)/shard_map/pallas_call | solution.py:99
  48.6 2.9 %collective-permute-done.14.refs_3_ = bf16[80,2432]{1,0:T(8,128)(2,1)S(1)} collective-permute-done((bf16[80,2432]{1,0:T(8,128)(2,1)S(1)}, bf16[80,2432]{1,0:T(8,128)(2,1)S(1)}, u32[]{:S(2)}, u32[]{:S(2)}) %collective-permute-start.14) | collective-permute-done | bytes 389152 | tf_op jit(solution)/shard_map/ppermute | solution.py:276
  53.5 5.9 %collective-permute-done.13.refs_2_ = bf16[80,2304]{1,0:T(8,128)(2,1)S(1)} collective-permute-done((bf16[80,2304]{1,0:T(8,128)(2,1)S(1)}, bf16[80,2304]{1,0:T(8,128)(2,1)S(1)}, u32[]{:S(2)}, u32[]{:S(2)}) %collective-permute-start.13) | collective-permute-done | bytes 368672 | tf_op jit(solution)/shard_map/ppermute | solution.py:276
  59.4 1.5 %collective-permute-done.12.refs_1_ = bf16[80,2432]{1,0:T(8,128)(2,1)S(1)} collective-permute-done((bf16[80,2432]{1,0:T(8,128)(2,1)S(1)}, bf16[80,2432]{1,0:T(8,128)(2,1)S(1)}, u32[]{:S(2)}, u32[]{:S(2)}) %collective-permute-start.12) | collective-permute-done | bytes 389152 | tf_op jit(solution)/shard_map/ppermute | solution.py:276
  62.1 1.6 %shard_map.77 = (f32[640,128]{1,0:T(8,128)S(1)}, f32[640,128]{1,0:T(8,128)S(1)}) custom-call(bf16[256,4736]{1,0:T(8,128)(2,1)S(1)} %collective-permute-done.10.tokens.other, bf16[320,4736]{1,0:T(8,128)(2,1)S(1)} %get-tuple-element.53.factor), custom_call_target="tpu_custom_call" | custom-call | flops 775946240 | tf_op jit(solution)/shard_map/pallas_call | solution.py:99
  65.4 1.6 %collective-permute-done.20.first = bf16[80,2304]{1,0:T(8,128)(2,1)S(1)} collective-permute-done((bf16[80,2304]{1,0:T(8,128)(2,1)S(1)}, bf16[80,2304]{1,0:T(8,128)(2,1)S(1)}, u32[]{:S(2)}, u32[]{:S(2)}) %collective-permute-start.20) | collective-permute-done | bytes 368672 | tf_op jit(solution)/shard_map/ppermute | solution.py:344
  67.0 1.6 %shard_map.79 = (f32[320,128]{1,0:T(8,128)S(1)}, f32[320,128]{1,0:T(8,128)S(1)}) custom-call(bf16[256,4736]{1,0:T(8,128)(2,1)S(1)} %get-tuple-element.43.tokens.own, bf16[256,4736]{1,0:T(8,128)(2,1)S(1)} %collective-permute-done.10.tokens.other, bf16[80,2304]{1,0:T(8,128)(2,1)S(1)} %collective-permute-done.20.first, ...), custom_call_target="tpu_custom_call" | custom-call | flops 6207569920 | tf_op jit(solution)/shard_map/pallas_call | solution.py:99
  70.4 1.6 %collective-permute-start.19 = (f32[320,128]{1,0:T(8,128)S(1)}, f32[320,128]{1,0:T(8,128)S(1)}, u32[]{:S(2)}, u32[]{:S(2)}) collective-permute-start(f32[320,128]{1,0:T(8,128)S(1)} %add.19), channel_id=1, source_target_pairs={{0,16},{16,0},{1,17},{17,1},{2,18},{18,2},{3,19},{19,3},{4,20},{20... | collective-permute-start | bytes 491528 | tf_op jit(solution)/shard_map/ppermute | solution.py:26
  72.9 11.4 %collective-permute-done.23.refs_10_ = f32[160,128]{1,0:T(8,128)S(1)} collective-permute-done((f32[160,128]{1,0:T(8,128)S(1)}, f32[160,128]{1,0:T(8,128)S(1)}, u32[]{:S(2)}, u32[]{:S(2)}) %collective-permute-start.23) | collective-permute-done | bytes 81952 | tf_op jit(solution)/shard_map/ppermute | solution.py:26
  86.8 1.6 %collective-permute-start.26 = (f32[8,32]{1,0:T(8,128)S(1)}, f32[8,32]{1,0:T(8,128)S(1)}, u32[]{:S(2)}, u32[]{:S(2)}) collective-permute-start(f32[8,32]{1,0:T(8,128)S(1)} %get-tuple-element.66), channel_id=1, source_target_pairs={{0,2},{2,0},{4,6},{6,4},{8,10},{10,8},{12,14},{14,12},{1,3},{3,1},... | collective-permute-start | bytes 3080 | tf_op jit(solution)/shard_map/ppermute | solution.py:374
  88.4 2.7 %collective-permute-start.25 = (f32[8,32]{1,0:T(8,128)S(1)}, f32[8,32]{1,0:T(8,128)S(1)}, u32[]{:S(2)}, u32[]{:S(2)}) collective-permute-start(f32[8,32]{1,0:T(8,128)S(1)} %get-tuple-element.65), channel_id=1, source_target_pairs={{0,14},{2,4},{4,2},{6,8},{8,6},{10,12},{12,10},{14,0},{1,15},{3,5}... | collective-permute-start | bytes 3080 | tf_op jit(solution)/shard_map/ppermute | solution.py:374
  91.1 3.6 %collective-permute-done.25 = f32[8,32]{1,0:T(8,128)S(1)} collective-permute-done((f32[8,32]{1,0:T(8,128)S(1)}, f32[8,32]{1,0:T(8,128)S(1)}, u32[]{:S(2)}, u32[]{:S(2)}) %collective-permute-start.25) | collective-permute-done | bytes 1056 | tf_op jit(solution)/shard_map/ppermute | solution.py:374
  (61 shorter events, 17.0 us)
Async XLA Ops:
  3.8 58.3 %collective-permute-start.10 = (bf16[256,4736]{1,0:T(8,128)(2,1)}, bf16[256,4736]{1,0:T(8,128)(2,1)S(1)}, u32[]{:S(2)}, u32[]{:S(2)}) collective-permute-start(bf16[256,4736]{1,0:T(8,128)(2,1)} %get-tuple-element.46), channel_id=1, source_target_pairs={{0,16},{16,0},{1,17},{17,1},{2,18},{18,2},{3,19},{19,3},{4,20},{20... | collective-permute-start | bytes 7274504 | tf_op jit(solution)/shard_map/ppermute | solution.py:26
  6.8 12.2 %collective-permute-start.3 = (bf16[80,2432]{1,0:T(8,128)(2,1)}, bf16[80,2432]{1,0:T(8,128)(2,1)S(1)}, u32[]{:S(2)}, u32[]{:S(2)}) collective-permute-start(bf16[80,2432]{1,0:T(8,128)(2,1)} %get-tuple-element.36), channel_id=1, source_target_pairs={{4,0},{8,4},{12,8},{14,12},{10,14},{6,10},{2,6},{0,2},{5,1},{9,5},... | collective-permute-start | bytes 1167368 | tf_op jit(solution)/shard_map/ppermute | solution.py:276
  8.3 12.2 %collective-permute-start = (bf16[80,2304]{1,0:T(8,128)(2,1)}, bf16[80,2304]{1,0:T(8,128)(2,1)S(1)}, u32[]{:S(2)}, u32[]{:S(2)}) collective-permute-start(bf16[80,2304]{1,0:T(8,128)(2,1)} %get-tuple-element.35), channel_id=1, source_target_pairs={{0,4},{4,8},{8,12},{12,14},{14,10},{10,6},{6,2},{2,0},{1,5},{5,9},... | collective-permute-start | bytes 1105928 | tf_op jit(solution)/shard_map/ppermute | solution.py:276
  8.9 19.5 %collective-permute-start.1 = (bf16[80,2432]{1,0:T(8,128)(2,1)}, bf16[80,2432]{1,0:T(8,128)(2,1)S(1)}, u32[]{:S(2)}, u32[]{:S(2)}) collective-permute-start(bf16[80,2432]{1,0:T(8,128)(2,1)} %get-tuple-element.36), channel_id=1, source_target_pairs={{0,4},{4,8},{8,12},{12,14},{14,10},{10,6},{6,2},{2,0},{1,5},{5,9},... | collective-permute-start | bytes 1167368 | tf_op jit(solution)/shard_map/ppermute | solution.py:276
  10.4 18.5 %collective-permute-start.2 = (bf16[80,2304]{1,0:T(8,128)(2,1)}, bf16[80,2304]{1,0:T(8,128)(2,1)S(1)}, u32[]{:S(2)}, u32[]{:S(2)}) collective-permute-start(bf16[80,2304]{1,0:T(8,128)(2,1)} %get-tuple-element.35), channel_id=1, source_target_pairs={{4,0},{8,4},{12,8},{14,12},{10,14},{6,10},{2,6},{0,2},{5,1},{9,5},... | collective-permute-start | bytes 1105928 | tf_op jit(solution)/shard_map/ppermute | solution.py:276
  19.0 16.2 %collective-permute-start.8 = (bf16[80,2432]{1,0:T(8,128)(2,1)S(1)}, bf16[80,2432]{1,0:T(8,128)(2,1)S(1)}, u32[]{:S(2)}, u32[]{:S(2)}) collective-permute-start(bf16[80,2432]{1,0:T(8,128)(2,1)S(1)} %collective-permute-done.3.refs_3_), channel_id=1, source_target_pairs={{4,0},{8,4},{12,8},{14,12},{10,14},{6,10},{2,6},{0,2},{5,1},{9,5},... | collective-permute-start | bytes 1167368 | tf_op jit(solution)/shard_map/ppermute | solution.py:276
  20.5 16.2 %collective-permute-start.5 = (bf16[80,2304]{1,0:T(8,128)(2,1)S(1)}, bf16[80,2304]{1,0:T(8,128)(2,1)S(1)}, u32[]{:S(2)}, u32[]{:S(2)}) collective-permute-start(bf16[80,2304]{1,0:T(8,128)(2,1)S(1)} %collective-permute-done.refs_0_), channel_id=1, source_target_pairs={{0,4},{4,8},{8,12},{12,14},{14,10},{10,6},{6,2},{2,0},{1,5},{5,9},... | collective-permute-start | bytes 1105928 | tf_op jit(solution)/shard_map/ppermute | solution.py:276
  28.4 16.2 %collective-permute-start.6 = (bf16[80,2432]{1,0:T(8,128)(2,1)S(1)}, bf16[80,2432]{1,0:T(8,128)(2,1)S(1)}, u32[]{:S(2)}, u32[]{:S(2)}) collective-permute-start(bf16[80,2432]{1,0:T(8,128)(2,1)S(1)} %collective-permute-done.1.refs_1_), channel_id=1, source_target_pairs={{0,4},{4,8},{8,12},{12,14},{14,10},{10,6},{6,2},{2,0},{1,5},{5,9},... | collective-permute-start | bytes 1167368 | tf_op jit(solution)/shard_map/ppermute | solution.py:276
  28.9 16.2 %collective-permute-start.7 = (bf16[80,2304]{1,0:T(8,128)(2,1)S(1)}, bf16[80,2304]{1,0:T(8,128)(2,1)S(1)}, u32[]{:S(2)}, u32[]{:S(2)}) collective-permute-start(bf16[80,2304]{1,0:T(8,128)(2,1)S(1)} %collective-permute-done.2.refs_2_), channel_id=1, source_target_pairs={{4,0},{8,4},{12,8},{14,12},{10,14},{6,10},{2,6},{0,2},{5,1},{9,5},... | collective-permute-start | bytes 1105928 | tf_op jit(solution)/shard_map/ppermute | solution.py:276
  35.2 16.2 %collective-permute-start.14 = (bf16[80,2432]{1,0:T(8,128)(2,1)S(1)}, bf16[80,2432]{1,0:T(8,128)(2,1)S(1)}, u32[]{:S(2)}, u32[]{:S(2)}) collective-permute-start(bf16[80,2432]{1,0:T(8,128)(2,1)S(1)} %collective-permute-done.8.refs_7_), channel_id=1, source_target_pairs={{4,0},{8,4},{12,8},{14,12},{10,14},{6,10},{2,6},{0,2},{5,1},{9,5},... | collective-permute-start | bytes 1167368 | tf_op jit(solution)/shard_map/ppermute | solution.py:276
  36.7 16.2 %collective-permute-start.11 = (bf16[80,2304]{1,0:T(8,128)(2,1)S(1)}, bf16[80,2304]{1,0:T(8,128)(2,1)S(1)}, u32[]{:S(2)}, u32[]{:S(2)}) collective-permute-start(bf16[80,2304]{1,0:T(8,128)(2,1)S(1)} %collective-permute-done.5.refs_4_), channel_id=1, source_target_pairs={{0,4},{4,8},{8,12},{12,14},{14,10},{10,6},{6,2},{2,0},{1,5},{5,9},... | collective-permute-start | bytes 1105928 | tf_op jit(solution)/shard_map/ppermute | solution.py:276
  44.6 16.2 %collective-permute-start.12 = (bf16[80,2432]{1,0:T(8,128)(2,1)S(1)}, bf16[80,2432]{1,0:T(8,128)(2,1)S(1)}, u32[]{:S(2)}, u32[]{:S(2)}) collective-permute-start(bf16[80,2432]{1,0:T(8,128)(2,1)S(1)} %collective-permute-done.6.refs_5_), channel_id=1, source_target_pairs={{0,4},{4,8},{8,12},{12,14},{14,10},{10,6},{6,2},{2,0},{1,5},{5,9},... | collective-permute-start | bytes 1167368 | tf_op jit(solution)/shard_map/ppermute | solution.py:276
  45.2 14.2 %collective-permute-start.13 = (bf16[80,2304]{1,0:T(8,128)(2,1)S(1)}, bf16[80,2304]{1,0:T(8,128)(2,1)S(1)}, u32[]{:S(2)}, u32[]{:S(2)}) collective-permute-start(bf16[80,2304]{1,0:T(8,128)(2,1)S(1)} %collective-permute-done.7.refs_6_), channel_id=1, source_target_pairs={{4,0},{8,4},{12,8},{14,12},{10,14},{6,10},{2,6},{0,2},{5,1},{9,5},... | collective-permute-start | bytes 1105928 | tf_op jit(solution)/shard_map/ppermute | solution.py:276
  51.5 15.5 %collective-permute-start.21 = (bf16[80,2432]{1,0:T(8,128)(2,1)S(1)}, bf16[80,2432]{1,0:T(8,128)(2,1)S(1)}, u32[]{:S(2)}, u32[]{:S(2)}) collective-permute-start(bf16[80,2432]{1,0:T(8,128)(2,1)S(1)} %collective-permute-done.14.refs_3_), channel_id=1, source_target_pairs={{4,0},{8,4},{12,8},{14,12},{10,14},{6,10},{2,6},{0,2},{5,1},{9,5},... | collective-permute-start | bytes 1167368 | tf_op jit(solution)/shard_map/ppermute | solution.py:344
  53.0 14.1 %collective-permute-start.20 = (bf16[80,2304]{1,0:T(8,128)(2,1)S(1)}, bf16[80,2304]{1,0:T(8,128)(2,1)S(1)}, u32[]{:S(2)}, u32[]{:S(2)}) collective-permute-start(bf16[80,2304]{1,0:T(8,128)(2,1)S(1)} %collective-permute-done.11.refs_0_), channel_id=1, source_target_pairs={{0,4},{4,8},{8,12},{12,14},{14,10},{10,6},{6,2},{2,0},{1,5},{5,9},... | collective-permute-start | bytes 1105928 | tf_op jit(solution)/shard_map/ppermute | solution.py:344
  63.7 5.5 %collective-permute-start.15 = (f32[640,128]{1,0:T(8,128)S(1)}, f32[640,128]{1,0:T(8,128)S(1)}, u32[]{:S(2)}, u32[]{:S(2)}) collective-permute-start(f32[640,128]{1,0:T(8,128)S(1)} %get-tuple-element.55), channel_id=1, source_target_pairs={{0,1},{1,0},{2,3},{3,2},{4,5},{5,4},{6,7},{7,6},{8,9},{9,8},{10,11... | collective-permute-start | bytes 983048 | tf_op jit(solution)/shard_map/ppermute | solution.py:26
  64.9 5.0 %collective-permute-start.18 = (f32[320,128]{1,0:T(8,128)S(1)}, f32[320,128]{1,0:T(8,128)S(1)}, u32[]{:S(2)}, u32[]{:S(2)}) collective-permute-start(f32[320,128]{1,0:T(8,128)S(1)} %get-tuple-element.60), channel_id=1, source_target_pairs={{0,1},{1,0},{2,3},{3,2},{4,5},{5,4},{6,7},{7,6},{8,9},{9,8},{10,11... | collective-permute-start | bytes 491528 | tf_op jit(solution)/shard_map/ppermute | solution.py:26
  68.7 4.2 %collective-permute-start.9 = (f32[640,128]{1,0:T(8,128)S(1)}, f32[640,128]{1,0:T(8,128)S(1)}, u32[]{:S(2)}, u32[]{:S(2)}) collective-permute-start(f32[640,128]{1,0:T(8,128)S(1)} %get-tuple-element.45), channel_id=1, source_target_pairs={{0,1},{1,0},{2,3},{3,2},{4,5},{5,4},{6,7},{7,6},{8,9},{9,8},{10,11... | collective-permute-start | bytes 983048 | tf_op jit(solution)/shard_map/ppermute | solution.py:26
  69.3 15.0 %collective-permute-start.16 = (f32[640,128]{1,0:T(8,128)S(1)}, f32[640,128]{1,0:T(8,128)S(1)}, u32[]{:S(2)}, u32[]{:S(2)}) collective-permute-start(f32[640,128]{1,0:T(8,128)S(1)} %add.18), channel_id=1, source_target_pairs={{0,16},{16,0},{1,17},{17,1},{2,18},{18,2},{3,19},{19,3},{4,20},{20... | collective-permute-start | bytes 983048 | tf_op jit(solution)/shard_map/ppermute | solution.py:26
  69.8 3.0 %collective-permute-start.17 = (f32[320,128]{1,0:T(8,128)S(1)}, f32[320,128]{1,0:T(8,128)S(1)}, u32[]{:S(2)}, u32[]{:S(2)}) collective-permute-start(f32[320,128]{1,0:T(8,128)S(1)} %get-tuple-element.57), channel_id=1, source_target_pairs={{0,1},{1,0},{2,3},{3,2},{4,5},{5,4},{6,7},{7,6},{8,9},{9,8},{10,11... | collective-permute-start | bytes 491528 | tf_op jit(solution)/shard_map/ppermute | solution.py:26
  70.4 13.9 %collective-permute-start.19 = (f32[320,128]{1,0:T(8,128)S(1)}, f32[320,128]{1,0:T(8,128)S(1)}, u32[]{:S(2)}, u32[]{:S(2)}) collective-permute-start(f32[320,128]{1,0:T(8,128)S(1)} %add.19), channel_id=1, source_target_pairs={{0,16},{16,0},{1,17},{17,1},{2,18},{18,2},{3,19},{19,3},{4,20},{20... | collective-permute-start | bytes 491528 | tf_op jit(solution)/shard_map/ppermute | solution.py:26
  72.0 12.3 %collective-permute-start.23 = (f32[160,128]{1,0:T(8,128)S(1)}, f32[160,128]{1,0:T(8,128)S(1)}, u32[]{:S(2)}, u32[]{:S(2)}) collective-permute-start(f32[160,128]{1,0:T(8,128)S(1)} %slice_add_fusion), channel_id=1, source_target_pairs={{0,16},{16,0},{1,17},{17,1},{2,18},{18,2},{3,19},{19,3},{4,20},{20... | collective-permute-start | bytes 245768 | tf_op jit(solution)/shard_map/ppermute | solution.py:26
  86.8 4.3 %collective-permute-start.26 = (f32[8,32]{1,0:T(8,128)S(1)}, f32[8,32]{1,0:T(8,128)S(1)}, u32[]{:S(2)}, u32[]{:S(2)}) collective-permute-start(f32[8,32]{1,0:T(8,128)S(1)} %get-tuple-element.66), channel_id=1, source_target_pairs={{0,2},{2,0},{4,6},{6,4},{8,10},{10,8},{12,14},{14,12},{1,3},{3,1},... | collective-permute-start | bytes 3080 | tf_op jit(solution)/shard_map/ppermute | solution.py:374
  88.4 6.3 %collective-permute-start.25 = (f32[8,32]{1,0:T(8,128)S(1)}, f32[8,32]{1,0:T(8,128)S(1)}, u32[]{:S(2)}, u32[]{:S(2)}) collective-permute-start(f32[8,32]{1,0:T(8,128)S(1)} %get-tuple-element.65), channel_id=1, source_target_pairs={{0,14},{2,4},{4,2},{6,8},{8,6},{10,12},{12,10},{14,0},{1,15},{3,5}... | collective-permute-start | bytes 3080 | tf_op jit(solution)/shard_map/ppermute | solution.py:374
  (10 other events, 103.6 us)

commit v4 on v3

--- a/solution.py
+++ b/solution.py
@@ -183,13 +183,14 @@
     split_cores(act, grad, give, keep, sums, 0)
 
 
-def last_kernel(act_half, own, other, first, second, give, keep, sums):
+def last_kernel(act_half, own, other, first, second, own_give, own_keep, give, keep, sums):
     rows, cut = first.shape
     rest = act_half - cut
     for i, tokens in enumerate((own, other)):
         act = dot_rows(tokens[:, :cut], first[...]) + dot_rows(tokens[:, cut:act_half], second[:, :rest])
         grad = dot_rows(tokens[:, act_half:], second[:, rest:])
-        split_cores(act, grad, give, keep, sums, 2 * rows * i)
+        outs = (own_give, own_keep) if i == 0 else (give, keep)
+        split_cores(act, grad, *outs, sums, 0)
 
 
 def scores_kernel(block_len, dp_size, live_tokens, move_plan, query, *refs):
@@ -294,7 +295,7 @@
             (activations, out_grads, act_factor, grad_factor, *from_back[1], *from_ahead[1])
         )[:4],
         scratch=[sums],
-        flops=work(rows, 2 * width),
+        flops=0 * work(rows, 2 * width),
     )
     own_got = swapped(own_give, "tensor")
 
@@ -328,7 +329,8 @@
             scratch=[wide_sums(count)],
             flops=work(count, width),
         )
-        return swapped(keep + swapped(give, "tensor"), "groups"), keep
+        total = keep + swapped(give, "tensor")
+        return swapped(total, "groups"), total
 
     for distance in range(2, steps - 2):
         from_back.append(sent(from_back[distance], ahead))
@@ -344,20 +346,20 @@
     last = [lax.ppermute(last_first, "dp", ahead), lax.ppermute(last_second, "dp", back)]
     far, far_give, far_keep, far_got = against_own(far_pieces)
     other = after(other, far)
-    near_other, near_done = against_other(near, other)
-    far_other, _ = against_other(far, after(other, near_done))
-
-    last_give, last_keep = kernel_call(
+    far_other, far_total = against_other(far, other)
+    near_other, near_total = against_other(near, other)
+
+    last_give, last_keep, shared_give, shared_keep = kernel_call(
         functools.partial(last_kernel, act_half),
-        [jax.ShapeDtypeStruct((4 * rows, half), f32)] * 2,
+        [jax.ShapeDtypeStruct((2 * rows, half), f32)] * 4,
         [whole] * 4,
-        [whole] * 2,
-        (own, other, *last),
+        [whole] * 4,
+        (own, after(other, far_other), *last),
         scratch=[sums],
-        flops=16 * 2 * work(rows, width),
+        flops=0,
     )
     last_got = swapped(last_give, "tensor")
-    last_other = swapped(last_keep[2 * rows :] + last_got[2 * rows :], "groups")
+    last_other = swapped(shared_keep + swapped(shared_give, "tensor"), "groups")
 
     moved = kernel_call(
         functools.partial(scores_kernel, block_len, dp_size),

time: 95.4 us -> 92.8 us (0.973)
  waiting for transfers between devices: 51.6 us -> 50.1 us
  starting transfers between devices: 26 us -> 24.9 us
    ppermute x1, starting transfers between devices: 1.58 us -> 0.01 us  [ringed(): lax.ppermute(inner, 'dp', inner_pairs)]
    ppermute x1, waiting for transfers between devices: 1.6 us -> 0.57 us  [ringed(): lax.ppermute(last_first, 'dp', ahead)]
    ppermute x11 -> x12, waiting for transfers between devices: 12.6 us -> 11.8 us  [swapped(): return lax.ppermute(value, axis, [(0, 1), (1, 0)])]
    ppermute x11 -> x12, starting transfers between devices: 7.55 us -> 7.14 us  [swapped(): return lax.ppermute(value, axis, [(0, 1), (1, 0)])]
  transfers between devices with their start and end apart: 27 -> 28, of which waited for: 11 -> 16; matrix products, arithmetic and copies ran while one was open for 0% -> 0% of each run, Pallas kernels for 9% -> 8%
where the time goes in v4:
time: 92.8 us; the launch traced here: 92.6 us
  waiting for transfers between devices  50.1 us (54%)
  starting transfers between devices  24.9 us (27%)
  Pallas kernels  14 us (15%)
  local copies, waits for them, and re-layouts  3.39 us (4%)
    ppermute x12, waiting for transfers between devices, sent(): return tuple((lax.ppermute(piece, 'dp', pairs) for piece in pieces))  34.1 us
    pallas_call x8, Pallas kernels, kernel_call(): pl.pallas_call(body, out_shape=out_shape, in_specs=in_specs, out_specs=ou...  14 us
    ppermute x12, starting transfers between devices, sent(): return tuple((lax.ppermute(piece, 'dp', pairs) for piece in pieces))  12.2 us
    ppermute x12, waiting for transfers between devices, swapped(): return lax.ppermute(value, axis, [(0, 1), (1, 0)])  11.8 us
    ppermute x12, starting transfers between devices, swapped(): return lax.ppermute(value, axis, [(0, 1), (1, 0)])  7.14 us
    ppermute x1, starting transfers between devices, ringed(): lax.ppermute(outer, 'dp', outer_pairs)  3.52 us
    ppermute x1, waiting for transfers between devices, ringed(): lax.ppermute(outer, 'dp', outer_pairs)  2.78 us
    unnamed x15, local copies, waits for them, and re-layouts  2.67 us
  transfers between devices with their start and end apart: 28, of which 16 were waited for; matrix products, arithmetic and copies ran while one was open for 0% of the time, Pallas kernels for 8%

profile of v4, /device:TPU:0, one launch (start us, length us, event | category | flops | bytes accessed | tf_op | source)
XLA Modules:
  0.0 92.6 jit_solution(12556186917061108055)
XLA Ops:
  0.0 3.8 %shard_map.73 = (bf16[80,2304]{1,0:T(8,128)(2,1)}, bf16[80,2432]{1,0:T(8,128)(2,1)}, bf16[256,4736]{1,0:T(8,128)(2,1)}) custom-call(bf16[256,6912]{1,0:T(8,128)(2,1)} %acts.2, bf16[256,2560]{1,0:T(8,128)(2,1)} %grads.2, bf16[80,6912]{1,0:T(8,128)(2,1)} %act_factor.2, bf16[80,2560]{1,0:T(8,128)(2,1)} %grad_factor.2), custom_call_target="tpu_custom_call" | custom-call | tf_op jit(solution)/shard_map/pallas_call | solution.py:99
  3.8 3.0 %collective-permute-start.10 = (bf16[256,4736]{1,0:T(8,128)(2,1)}, bf16[256,4736]{1,0:T(8,128)(2,1)S(1)}, u32[]{:S(2)}, u32[]{:S(2)}) collective-permute-start(bf16[256,4736]{1,0:T(8,128)(2,1)} %get-tuple-element.48), channel_id=1, source_target_pairs={{0,16},{16,0},{1,17},{17,1},{2,18},{18,2},{3,19},{19,3},{4,20},{20... | collective-permute-start | bytes 7274504 | tf_op jit(solution)/shard_map/ppermute | solution.py:26
  6.8 1.5 %collective-permute-start.3 = (bf16[80,2432]{1,0:T(8,128)(2,1)}, bf16[80,2432]{1,0:T(8,128)(2,1)S(1)}, u32[]{:S(2)}, u32[]{:S(2)}) collective-permute-start(bf16[80,2432]{1,0:T(8,128)(2,1)} %get-tuple-element.38), channel_id=1, source_target_pairs={{4,0},{8,4},{12,8},{14,12},{10,14},{6,10},{2,6},{0,2},{5,1},{9,5},... | collective-permute-start | bytes 1167368 | tf_op jit(solution)/shard_map/ppermute | solution.py:277
  8.9 1.5 %collective-permute-start.2 = (bf16[80,2304]{1,0:T(8,128)(2,1)}, bf16[80,2304]{1,0:T(8,128)(2,1)S(1)}, u32[]{:S(2)}, u32[]{:S(2)}) collective-permute-start(bf16[80,2304]{1,0:T(8,128)(2,1)} %get-tuple-element.37), channel_id=1, source_target_pairs={{4,0},{8,4},{12,8},{14,12},{10,14},{6,10},{2,6},{0,2},{5,1},{9,5},... | collective-permute-start | bytes 1105928 | tf_op jit(solution)/shard_map/ppermute | solution.py:277
  10.9 8.1 %collective-permute-done.3.refs_3_ = bf16[80,2432]{1,0:T(8,128)(2,1)S(1)} collective-permute-done((bf16[80,2432]{1,0:T(8,128)(2,1)}, bf16[80,2432]{1,0:T(8,128)(2,1)S(1)}, u32[]{:S(2)}, u32[]{:S(2)}) %collective-permute-start.3) | collective-permute-done | bytes 389152 | tf_op jit(solution)/shard_map/ppermute | solution.py:277
  19.0 1.5 %collective-permute-start.8 = (bf16[80,2432]{1,0:T(8,128)(2,1)S(1)}, bf16[80,2432]{1,0:T(8,128)(2,1)S(1)}, u32[]{:S(2)}, u32[]{:S(2)}) collective-permute-start(bf16[80,2432]{1,0:T(8,128)(2,1)S(1)} %collective-permute-done.3.refs_3_), channel_id=1, source_target_pairs={{4,0},{8,4},{12,8},{14,12},{10,14},{6,10},{2,6},{0,2},{5,1},{9,5},... | collective-permute-start | bytes 1167368 | tf_op jit(solution)/shard_map/ppermute | solution.py:277
  21.0 5.9 %collective-permute-done.2.refs_2_ = bf16[80,2304]{1,0:T(8,128)(2,1)S(1)} collective-permute-done((bf16[80,2304]{1,0:T(8,128)(2,1)}, bf16[80,2304]{1,0:T(8,128)(2,1)S(1)}, u32[]{:S(2)}, u32[]{:S(2)}) %collective-permute-start.2) | collective-permute-done | bytes 368672 | tf_op jit(solution)/shard_map/ppermute | solution.py:277
  26.9 1.5 %collective-permute-start.7 = (bf16[80,2304]{1,0:T(8,128)(2,1)S(1)}, bf16[80,2304]{1,0:T(8,128)(2,1)S(1)}, u32[]{:S(2)}, u32[]{:S(2)}) collective-permute-start(bf16[80,2304]{1,0:T(8,128)(2,1)S(1)} %collective-permute-done.2.refs_2_), channel_id=1, source_target_pairs={{4,0},{8,4},{12,8},{14,12},{10,14},{6,10},{2,6},{0,2},{5,1},{9,5},... | collective-permute-start | bytes 1105928 | tf_op jit(solution)/shard_map/ppermute | solution.py:277
  31.5 1.5 %shard_map.74 = (f32[160,128]{1,0:T(8,128)S(1)}, f32[160,128]{1,0:T(8,128)S(1)}, bf16[256,4736]{1,0:T(8,128)(2,1)S(1)}) custom-call(bf16[256,6912]{1,0:T(8,128)(2,1)S(1)} %copy-done, bf16[256,2560]{1,0:T(8,128)(2,1)S(1)} %copy-done.1, bf16[80,6912]{1,0:T(8,128)(2,1)S(1)} %copy-done.2, bf16[80,2560]{1,0:T(8,128)(2,1)S(1)} %copy-done.3), custom_call_target="tpu_custom_call" | custom-call | tf_op jit(solution)/shard_map/pallas_call | solution.py:99
  33.1 2.2 %collective-permute-done.8.refs_7_ = bf16[80,2432]{1,0:T(8,128)(2,1)S(1)} collective-permute-done((bf16[80,2432]{1,0:T(8,128)(2,1)S(1)}, bf16[80,2432]{1,0:T(8,128)(2,1)S(1)}, u32[]{:S(2)}, u32[]{:S(2)}) %collective-permute-start.8) | collective-permute-done | bytes 389152 | tf_op jit(solution)/shard_map/ppermute | solution.py:277
  35.2 1.5 %collective-permute-done.6.refs_5_ = bf16[80,2432]{1,0:T(8,128)(2,1)S(1)} collective-permute-done((bf16[80,2432]{1,0:T(8,128)(2,1)S(1)}, bf16[80,2432]{1,0:T(8,128)(2,1)S(1)}, u32[]{:S(2)}, u32[]{:S(2)}) %collective-permute-start.6) | collective-permute-done | bytes 389152 | tf_op jit(solution)/shard_map/ppermute | solution.py:277
  37.3 1.5 %collective-permute-start.14 = (bf16[80,2432]{1,0:T(8,128)(2,1)S(1)}, bf16[80,2432]{1,0:T(8,128)(2,1)S(1)}, u32[]{:S(2)}, u32[]{:S(2)}) collective-permute-start(bf16[80,2432]{1,0:T(8,128)(2,1)S(1)} %collective-permute-done.8.refs_7_), channel_id=1, source_target_pairs={{4,0},{8,4},{12,8},{14,12},{10,14},{6,10},{2,6},{0,2},{5,1},{9,5},... | collective-permute-start | bytes 1167368 | tf_op jit(solution)/shard_map/ppermute | solution.py:277
  38.8 4.4 %collective-permute-done.7.refs_6_ = bf16[80,2304]{1,0:T(8,128)(2,1)S(1)} collective-permute-done((bf16[80,2304]{1,0:T(8,128)(2,1)S(1)}, bf16[80,2304]{1,0:T(8,128)(2,1)S(1)}, u32[]{:S(2)}, u32[]{:S(2)}) %collective-permute-start.7) | collective-permute-done | bytes 368672 | tf_op jit(solution)/shard_map/ppermute | solution.py:277
  43.1 1.5 %collective-permute-done.5.refs_4_ = bf16[80,2304]{1,0:T(8,128)(2,1)S(1)} collective-permute-done((bf16[80,2304]{1,0:T(8,128)(2,1)S(1)}, bf16[80,2304]{1,0:T(8,128)(2,1)S(1)}, u32[]{:S(2)}, u32[]{:S(2)}) %collective-permute-start.5) | collective-permute-done | bytes 368672 | tf_op jit(solution)/shard_map/ppermute | solution.py:277
  45.2 1.5 %collective-permute-start.13 = (bf16[80,2304]{1,0:T(8,128)(2,1)S(1)}, bf16[80,2304]{1,0:T(8,128)(2,1)S(1)}, u32[]{:S(2)}, u32[]{:S(2)}) collective-permute-start(bf16[80,2304]{1,0:T(8,128)(2,1)S(1)} %collective-permute-done.7.refs_6_), channel_id=1, source_target_pairs={{4,0},{8,4},{12,8},{14,12},{10,14},{6,10},{2,6},{0,2},{5,1},{9,5},... | collective-permute-start | bytes 1105928 | tf_op jit(solution)/shard_map/ppermute | solution.py:277
  46.7 1.9 %shard_map.75 = (bf16[320,4736]{1,0:T(8,128)(2,1)S(1)}, f32[640,128]{1,0:T(8,128)S(1)}, f32[640,128]{1,0:T(8,128)S(1)}) custom-call(bf16[256,4736]{1,0:T(8,128)(2,1)S(1)} %get-tuple-element.45.tokens.own, bf16[80,2304]{1,0:T(8,128)(2,1)S(1)} %collective-permute-done.refs_0_, bf16[80,2432]{1,0:T(8,128)(2,1)S(1)} %collective-permute-done.1.refs_1_, ...), custom_call_target="tpu_custom_call" | custom-call | flops 775946240 | tf_op jit(solution)/shard_map/pallas_call | solution.py:99
  48.6 10.5 %collective-permute-done.11.refs_0_ = bf16[80,2304]{1,0:T(8,128)(2,1)S(1)} collective-permute-done((bf16[80,2304]{1,0:T(8,128)(2,1)S(1)}, bf16[80,2304]{1,0:T(8,128)(2,1)S(1)}, u32[]{:S(2)}, u32[]{:S(2)}) %collective-permute-start.11) | collective-permute-done | bytes 368672 | tf_op jit(solution)/shard_map/ppermute | solution.py:277
  60.4 1.6 %shard_map.77 = (f32[640,128]{1,0:T(8,128)S(1)}, f32[640,128]{1,0:T(8,128)S(1)}) custom-call(bf16[256,4736]{1,0:T(8,128)(2,1)S(1)} %collective-permute-done.10.tokens.other, bf16[320,4736]{1,0:T(8,128)(2,1)S(1)} %get-tuple-element.55.factor), custom_call_target="tpu_custom_call" | custom-call | flops 775946240 | tf_op jit(solution)/shard_map/pallas_call | solution.py:99
  62.0 1.6 %collective-permute-start.21 = (bf16[80,2432]{1,0:T(8,128)(2,1)S(1)}, bf16[80,2432]{1,0:T(8,128)(2,1)S(1)}, u32[]{:S(2)}, u32[]{:S(2)}) collective-permute-start(bf16[80,2432]{1,0:T(8,128)(2,1)S(1)} %collective-permute-done.14.refs_3_), channel_id=1, source_target_pairs={{4,0},{8,4},{12,8},{14,12},{10,14},{6,10},{2,6},{0,2},{5,1},{9,5},... | collective-permute-start | bytes 1167368 | tf_op jit(solution)/shard_map/ppermute | solution.py:346
  68.9 4.9 %collective-permute-done.19.refs_7_ = f32[320,128]{1,0:T(8,128)S(1)} collective-permute-done((f32[320,128]{1,0:T(8,128)S(1)}, f32[320,128]{1,0:T(8,128)S(1)}, u32[]{:S(2)}, u32[]{:S(2)}) %collective-permute-start.19) | collective-permute-done | bytes 163872 | tf_op jit(solution)/shard_map/ppermute | solution.py:26
  74.3 1.6 %shard_map.79 = (f32[160,128]{1,0:T(8,128)S(1)}, f32[160,128]{1,0:T(8,128)S(1)}, f32[160,128]{1,0:T(8,128)S(1)}, f32[160,128]{1,0:T(8,128)S(1)}) custom-call(bf16[256,4736]{1,0:T(8,128)(2,1)S(1)} %get-tuple-element.45.tokens.own, bf16[256,4736]{1,0:T(8,128)(2,1)S(1)} %collective-permute-done.10.tokens.other, ...), custom_call_target="tpu_custom_call" | custom-call | tf_op jit(solution)/shard_map/pallas_call | solution.py:99
  79.1 3.3 %collective-permute-done.24.refs_10_ = f32[160,128]{1,0:T(8,128)S(1)} collective-permute-done((f32[160,128]{1,0:T(8,128)S(1)}, f32[160,128]{1,0:T(8,128)S(1)}, u32[]{:S(2)}, u32[]{:S(2)}) %collective-permute-start.24) | collective-permute-done | bytes 81952 | tf_op jit(solution)/shard_map/ppermute | solution.py:26
  84.9 3.5 %collective-permute-start.26 = (f32[8,32]{1,0:T(8,128)S(1)}, f32[8,32]{1,0:T(8,128)S(1)}, u32[]{:S(2)}, u32[]{:S(2)}) collective-permute-start(f32[8,32]{1,0:T(8,128)S(1)} %get-tuple-element.69), channel_id=1, source_target_pairs={{0,14},{2,4},{4,2},{6,8},{8,6},{10,12},{12,10},{14,0},{1,15},{3,5}... | collective-permute-start | bytes 3080 | tf_op jit(solution)/shard_map/ppermute | solution.py:376
  88.4 2.8 %collective-permute-done.26 = f32[8,32]{1,0:T(8,128)S(1)} collective-permute-done((f32[8,32]{1,0:T(8,128)S(1)}, f32[8,32]{1,0:T(8,128)S(1)}, u32[]{:S(2)}, u32[]{:S(2)}) %collective-permute-start.26) | collective-permute-done | bytes 1056 | tf_op jit(solution)/shard_map/ppermute | solution.py:376
  (63 shorter events, 19.8 us)
Async XLA Ops:
  3.8 56.6 %collective-permute-start.10 = (bf16[256,4736]{1,0:T(8,128)(2,1)}, bf16[256,4736]{1,0:T(8,128)(2,1)S(1)}, u32[]{:S(2)}, u32[]{:S(2)}) collective-permute-start(bf16[256,4736]{1,0:T(8,128)(2,1)} %get-tuple-element.48), channel_id=1, source_target_pairs={{0,16},{16,0},{1,17},{17,1},{2,18},{18,2},{3,19},{19,3},{4,20},{20... | collective-permute-start | bytes 7274504 | tf_op jit(solution)/shard_map/ppermute | solution.py:26
  6.8 12.2 %collective-permute-start.3 = (bf16[80,2432]{1,0:T(8,128)(2,1)}, bf16[80,2432]{1,0:T(8,128)(2,1)S(1)}, u32[]{:S(2)}, u32[]{:S(2)}) collective-permute-start(bf16[80,2432]{1,0:T(8,128)(2,1)} %get-tuple-element.38), channel_id=1, source_target_pairs={{4,0},{8,4},{12,8},{14,12},{10,14},{6,10},{2,6},{0,2},{5,1},{9,5},... | collective-permute-start | bytes 1167368 | tf_op jit(solution)/shard_map/ppermute | solution.py:277
  8.3 12.2 %collective-permute-start.1 = (bf16[80,2432]{1,0:T(8,128)(2,1)}, bf16[80,2432]{1,0:T(8,128)(2,1)S(1)}, u32[]{:S(2)}, u32[]{:S(2)}) collective-permute-start(bf16[80,2432]{1,0:T(8,128)(2,1)} %get-tuple-element.38), channel_id=1, source_target_pairs={{0,4},{4,8},{8,12},{12,14},{14,10},{10,6},{6,2},{2,0},{1,5},{5,9},... | collective-permute-start | bytes 1167368 | tf_op jit(solution)/shard_map/ppermute | solution.py:277
  8.9 18.0 %collective-permute-start.2 = (bf16[80,2304]{1,0:T(8,128)(2,1)}, bf16[80,2304]{1,0:T(8,128)(2,1)S(1)}, u32[]{:S(2)}, u32[]{:S(2)}) collective-permute-start(bf16[80,2304]{1,0:T(8,128)(2,1)} %get-tuple-element.37), channel_id=1, source_target_pairs={{4,0},{8,4},{12,8},{14,12},{10,14},{6,10},{2,6},{0,2},{5,1},{9,5},... | collective-permute-start | bytes 1105928 | tf_op jit(solution)/shard_map/ppermute | solution.py:277
  10.4 18.1 %collective-permute-start = (bf16[80,2304]{1,0:T(8,128)(2,1)}, bf16[80,2304]{1,0:T(8,128)(2,1)S(1)}, u32[]{:S(2)}, u32[]{:S(2)}) collective-permute-start(bf16[80,2304]{1,0:T(8,128)(2,1)} %get-tuple-element.37), channel_id=1, source_target_pairs={{0,4},{4,8},{8,12},{12,14},{14,10},{10,6},{6,2},{2,0},{1,5},{5,9},... | collective-permute-start | bytes 1105928 | tf_op jit(solution)/shard_map/ppermute | solution.py:277
  19.0 16.2 %collective-permute-start.8 = (bf16[80,2432]{1,0:T(8,128)(2,1)S(1)}, bf16[80,2432]{1,0:T(8,128)(2,1)S(1)}, u32[]{:S(2)}, u32[]{:S(2)}) collective-permute-start(bf16[80,2432]{1,0:T(8,128)(2,1)S(1)} %collective-permute-done.3.refs_3_), channel_id=1, source_target_pairs={{4,0},{8,4},{12,8},{14,12},{10,14},{6,10},{2,6},{0,2},{5,1},{9,5},... | collective-permute-start | bytes 1167368 | tf_op jit(solution)/shard_map/ppermute | solution.py:277
  20.5 16.2 %collective-permute-start.6 = (bf16[80,2432]{1,0:T(8,128)(2,1)S(1)}, bf16[80,2432]{1,0:T(8,128)(2,1)S(1)}, u32[]{:S(2)}, u32[]{:S(2)}) collective-permute-start(bf16[80,2432]{1,0:T(8,128)(2,1)S(1)} %collective-permute-done.1.refs_1_), channel_id=1, source_target_pairs={{0,4},{4,8},{8,12},{12,14},{14,10},{10,6},{6,2},{2,0},{1,5},{5,9},... | collective-permute-start | bytes 1167368 | tf_op jit(solution)/shard_map/ppermute | solution.py:277
  26.9 16.2 %collective-permute-start.7 = (bf16[80,2304]{1,0:T(8,128)(2,1)S(1)}, bf16[80,2304]{1,0:T(8,128)(2,1)S(1)}, u32[]{:S(2)}, u32[]{:S(2)}) collective-permute-start(bf16[80,2304]{1,0:T(8,128)(2,1)S(1)} %collective-permute-done.2.refs_2_), channel_id=1, source_target_pairs={{4,0},{8,4},{12,8},{14,12},{10,14},{6,10},{2,6},{0,2},{5,1},{9,5},... | collective-permute-start | bytes 1105928 | tf_op jit(solution)/shard_map/ppermute | solution.py:277
  28.4 16.2 %collective-permute-start.5 = (bf16[80,2304]{1,0:T(8,128)(2,1)S(1)}, bf16[80,2304]{1,0:T(8,128)(2,1)S(1)}, u32[]{:S(2)}, u32[]{:S(2)}) collective-permute-start(bf16[80,2304]{1,0:T(8,128)(2,1)S(1)} %collective-permute-done.refs_0_), channel_id=1, source_target_pairs={{0,4},{4,8},{8,12},{12,14},{14,10},{10,6},{6,2},{2,0},{1,5},{5,9},... | collective-permute-start | bytes 1105928 | tf_op jit(solution)/shard_map/ppermute | solution.py:277
  36.7 22.4 %collective-permute-start.12 = (bf16[80,2432]{1,0:T(8,128)(2,1)S(1)}, bf16[80,2432]{1,0:T(8,128)(2,1)S(1)}, u32[]{:S(2)}, u32[]{:S(2)}) collective-permute-start(bf16[80,2432]{1,0:T(8,128)(2,1)S(1)} %collective-permute-done.6.refs_5_), channel_id=1, source_target_pairs={{0,4},{4,8},{8,12},{12,14},{14,10},{10,6},{6,2},{2,0},{1,5},{5,9},... | collective-permute-start | bytes 1167368 | tf_op jit(solution)/shard_map/ppermute | solution.py:277
  37.3 21.9 %collective-permute-start.14 = (bf16[80,2432]{1,0:T(8,128)(2,1)S(1)}, bf16[80,2432]{1,0:T(8,128)(2,1)S(1)}, u32[]{:S(2)}, u32[]{:S(2)}) collective-permute-start(bf16[80,2432]{1,0:T(8,128)(2,1)S(1)} %collective-permute-done.8.refs_7_), channel_id=1, source_target_pairs={{4,0},{8,4},{12,8},{14,12},{10,14},{6,10},{2,6},{0,2},{5,1},{9,5},... | collective-permute-start | bytes 1167368 | tf_op jit(solution)/shard_map/ppermute | solution.py:277
  44.6 14.5 %collective-permute-start.11 = (bf16[80,2304]{1,0:T(8,128)(2,1)S(1)}, bf16[80,2304]{1,0:T(8,128)(2,1)S(1)}, u32[]{:S(2)}, u32[]{:S(2)}) collective-permute-start(bf16[80,2304]{1,0:T(8,128)(2,1)S(1)} %collective-permute-done.5.refs_4_), channel_id=1, source_target_pairs={{0,4},{4,8},{8,12},{12,14},{14,10},{10,6},{6,2},{2,0},{1,5},{5,9},... | collective-permute-start | bytes 1105928 | tf_op jit(solution)/shard_map/ppermute | solution.py:277
  45.2 13.9 %collective-permute-start.13 = (bf16[80,2304]{1,0:T(8,128)(2,1)S(1)}, bf16[80,2304]{1,0:T(8,128)(2,1)S(1)}, u32[]{:S(2)}, u32[]{:S(2)}) collective-permute-start(bf16[80,2304]{1,0:T(8,128)(2,1)S(1)} %collective-permute-done.7.refs_6_), channel_id=1, source_target_pairs={{4,0},{8,4},{12,8},{14,12},{10,14},{6,10},{2,6},{0,2},{5,1},{9,5},... | collective-permute-start | bytes 1105928 | tf_op jit(solution)/shard_map/ppermute | solution.py:277
  62.0 5.8 %collective-permute-start.15 = (f32[640,128]{1,0:T(8,128)S(1)}, f32[640,128]{1,0:T(8,128)S(1)}, u32[]{:S(2)}, u32[]{:S(2)}) collective-permute-start(f32[640,128]{1,0:T(8,128)S(1)} %get-tuple-element.57), channel_id=1, source_target_pairs={{0,1},{1,0},{2,3},{3,2},{4,5},{5,4},{6,7},{7,6},{8,9},{9,8},{10,11... | collective-permute-start | bytes 983048 | tf_op jit(solution)/shard_map/ppermute | solution.py:26
  62.0 12.3 %collective-permute-start.21 = (bf16[80,2432]{1,0:T(8,128)(2,1)S(1)}, bf16[80,2432]{1,0:T(8,128)(2,1)S(1)}, u32[]{:S(2)}, u32[]{:S(2)}) collective-permute-start(bf16[80,2432]{1,0:T(8,128)(2,1)S(1)} %collective-permute-done.14.refs_3_), channel_id=1, source_target_pairs={{4,0},{8,4},{12,8},{14,12},{10,14},{6,10},{2,6},{0,2},{5,1},{9,5},... | collective-permute-start | bytes 1167368 | tf_op jit(solution)/shard_map/ppermute | solution.py:346
  63.7 10.7 %collective-permute-start.20 = (bf16[80,2304]{1,0:T(8,128)(2,1)S(1)}, bf16[80,2304]{1,0:T(8,128)(2,1)S(1)}, u32[]{:S(2)}, u32[]{:S(2)}) collective-permute-start(bf16[80,2304]{1,0:T(8,128)(2,1)S(1)} %collective-permute-done.11.refs_0_), channel_id=1, source_target_pairs={{0,4},{4,8},{8,12},{12,14},{14,10},{10,6},{6,2},{2,0},{1,5},{5,9},... | collective-permute-start | bytes 1105928 | tf_op jit(solution)/shard_map/ppermute | solution.py:346
  66.6 7.1 %collective-permute-start.19 = (f32[320,128]{1,0:T(8,128)S(1)}, f32[320,128]{1,0:T(8,128)S(1)}, u32[]{:S(2)}, u32[]{:S(2)}) collective-permute-start(f32[320,128]{1,0:T(8,128)S(1)} %add.19), channel_id=1, source_target_pairs={{0,16},{16,0},{1,17},{17,1},{2,18},{18,2},{3,19},{19,3},{4,20},{20... | collective-permute-start | bytes 491528 | tf_op jit(solution)/shard_map/ppermute | solution.py:26
  67.8 11.2 %collective-permute-start.9 = (f32[640,128]{1,0:T(8,128)S(1)}, f32[640,128]{1,0:T(8,128)S(1)}, u32[]{:S(2)}, u32[]{:S(2)}) collective-permute-start(f32[640,128]{1,0:T(8,128)S(1)} %get-tuple-element.47), channel_id=1, source_target_pairs={{0,1},{1,0},{2,3},{3,2},{4,5},{5,4},{6,7},{7,6},{8,9},{9,8},{10,11... | collective-permute-start | bytes 983048 | tf_op jit(solution)/shard_map/ppermute | solution.py:26
  67.9 14.5 %collective-permute-start.16 = (f32[640,128]{1,0:T(8,128)S(1)}, f32[640,128]{1,0:T(8,128)S(1)}, u32[]{:S(2)}, u32[]{:S(2)}) collective-permute-start(f32[640,128]{1,0:T(8,128)S(1)} %add.18), channel_id=1, source_target_pairs={{0,16},{16,0},{1,17},{17,1},{2,18},{18,2},{3,19},{19,3},{4,20},{20... | collective-permute-start | bytes 983048 | tf_op jit(solution)/shard_map/ppermute | solution.py:26
  76.0 3.0 %collective-permute-start.17 = (f32[320,128]{1,0:T(8,128)S(1)}, f32[320,128]{1,0:T(8,128)S(1)}, u32[]{:S(2)}, u32[]{:S(2)}) collective-permute-start(f32[320,128]{1,0:T(8,128)S(1)} %get-tuple-element.59), channel_id=1, source_target_pairs={{0,1},{1,0},{2,3},{3,2},{4,5},{5,4},{6,7},{7,6},{8,9},{9,8},{10,11... | collective-permute-start | bytes 491528 | tf_op jit(solution)/shard_map/ppermute | solution.py:26
  77.3 1.8 %collective-permute-start.22 = (f32[160,128]{1,0:T(8,128)S(1)}, f32[160,128]{1,0:T(8,128)S(1)}, u32[]{:S(2)}, u32[]{:S(2)}) collective-permute-start(f32[160,128]{1,0:T(8,128)S(1)} %get-tuple-element.66), channel_id=1, source_target_pairs={{0,1},{1,0},{2,3},{3,2},{4,5},{5,4},{6,7},{7,6},{8,9},{9,8},{10,11... | collective-permute-start | bytes 245768 | tf_op jit(solution)/shard_map/ppermute | solution.py:26
  77.8 4.6 %collective-permute-start.24 = (f32[160,128]{1,0:T(8,128)S(1)}, f32[160,128]{1,0:T(8,128)S(1)}, u32[]{:S(2)}, u32[]{:S(2)}) collective-permute-start(f32[160,128]{1,0:T(8,128)S(1)} %add.20), channel_id=1, source_target_pairs={{0,16},{16,0},{1,17},{17,1},{2,18},{18,2},{3,19},{19,3},{4,20},{20... | collective-permute-start | bytes 245768 | tf_op jit(solution)/shard_map/ppermute | solution.py:26
  84.9 6.3 %collective-permute-start.26 = (f32[8,32]{1,0:T(8,128)S(1)}, f32[8,32]{1,0:T(8,128)S(1)}, u32[]{:S(2)}, u32[]{:S(2)}) collective-permute-start(f32[8,32]{1,0:T(8,128)S(1)} %get-tuple-element.69), channel_id=1, source_target_pairs={{0,14},{2,4},{4,2},{6,8},{8,6},{10,12},{12,10},{14,0},{1,15},{3,5}... | collective-permute-start | bytes 3080 | tf_op jit(solution)/shard_map/ppermute | solution.py:376
  88.4 3.6 %collective-permute-start.27 = (f32[8,32]{1,0:T(8,128)S(1)}, f32[8,32]{1,0:T(8,128)S(1)}, u32[]{:S(2)}, u32[]{:S(2)}) collective-permute-start(f32[8,32]{1,0:T(8,128)S(1)} %get-tuple-element.70), channel_id=1, source_target_pairs={{0,2},{2,0},{4,6},{6,4},{8,10},{10,8},{12,14},{14,12},{1,3},{3,1},... | collective-permute-start | bytes 3080 | tf_op jit(solution)/shard_map/ppermute | solution.py:376
  (11 other events, 102.2 us)

commit v5 on v4

--- a/solution.py
+++ b/solution.py
@@ -193,24 +193,21 @@
         split_cores(act, grad, *outs, sums, 0)
 
 
-def scores_kernel(block_len, dp_size, live_tokens, move_plan, query, *refs):
+def scores_kernel(block_len, dp_size, distances, counts, live_tokens, move_plan, query, *refs):
     exact = functools.partial(
         lax.dot_general, precision=lax.Precision.HIGHEST, preferred_element_type=jnp.float32
     )
-    sets, out = refs[:-1], refs[-1]
-    rows = sets[0].shape[0] // 2
+    sets, before, out = refs[: sum(counts)], refs[sum(counts) : -1], refs[-1]
     products = []
-    for terms in (sets[:2], sets[2:5], sets[5:8], sets[8:]):
+    for count in counts:
+        terms, sets = sets[:count], sets[count:]
         size = terms[-1].shape[0]
         total = sum(term[:size, :] for term in terms)
         products.append(total[: size // 2] * total[size // 2 :])
+    rows = sum(value.shape[0] for value in products) // len(distances)
     product = jnp.concatenate(products, axis=0)
     my_rank = lax.axis_index("dp")
     place = ring_place(my_rank, dp_size)
-    distances = [0]
-    for distance in range(1, dp_size // 2):
-        distances += [-distance, distance]
-    distances.append(dp_size // 2)
     ids = lax.broadcasted_iota(jnp.int32, (rows, QUERY_LANES), 1)
     onehots = []
     for distance in distances:
@@ -233,7 +230,10 @@
         start = slot * block_len
         hit = (token >= start) & (token < start + live_tokens[mine]) & (dest == target)
         moves = moves + hit.astype(jnp.float32)
-    out[...] = exact(moves, sums, (((1,), (1,)), ((), ())))
+    total = exact(moves, sums, (((1,), (1,)), ((), ())))
+    for value in before:
+        total = total + value[...]
+    out[...] = total
 
 
 def ringed(activations, out_grads, act_factor, grad_factor, query_of_row, live_tokens, move_plan):
@@ -361,14 +361,27 @@
     last_got = swapped(last_give, "tensor")
     last_other = swapped(shared_keep + swapped(shared_give, "tensor"), "groups")
 
-    moved = kernel_call(
-        functools.partial(scores_kernel, block_len, dp_size),
-        jax.ShapeDtypeStruct((3 * DEST_ROWS, QUERY_LANES), f32),
-        [smem, smem] + [whole] * 12,
-        whole,
-        (live_tokens, move_plan, query_of_row.reshape(-1, 1), own_keep, own_got, near_keep, near_got,
-         near_other, far_keep, far_got, far_other, last_keep, last_got, last_other),
-    )
+    distances = [0]
+    for distance in range(1, steps):
+        distances += [-distance, distance]
+
+    def scores(distances, counts, terms, flops=0):
+        return kernel_call(
+            functools.partial(scores_kernel, block_len, dp_size, distances, counts),
+            jax.ShapeDtypeStruct((3 * DEST_ROWS, QUERY_LANES), f32),
+            [smem, smem] + [whole] * (1 + len(terms)),
+            whole,
+            (live_tokens, move_plan, query_of_row.reshape(-1, 1), *terms),
+            flops=flops,
+        )
+
+    moved = scores(
+        distances,
+        (2, 3, 3),
+        (own_keep, own_got, near_keep, near_got, near_other, far_keep, far_got, far_other),
+        flops=work(rows, width),
+    )
+    moved = scores([steps], (3,), (last_keep, last_got, last_other, moved))
     moved = moved + swapped(moved, "tensor")
     kept, outer, inner = (moved[i * DEST_ROWS : (i + 1) * DEST_ROWS] for i in range(3))
     outer_pairs = [(d, (d + 1 if d % 2 else d - 1) % dp_size) for d in range(dp_size)]

time: 92.8 us -> 92.6 us (level)
  waiting for transfers between devices: 50.1 us -> 48.2 us
  Pallas kernels: 14 us -> 15 us
    ppermute x12, waiting for transfers between devices: 11.8 us -> 10 us  [swapped(): return lax.ppermute(value, axis, [(0, 1), (1, 0)])]
    pallas_call x8 -> x9, Pallas kernels: 14 us -> 15 us  [kernel_call(): pl.pallas_call(body, out_shape=out_shape, in_specs=in_specs, out_specs=ou...]
  transfers between devices with their start and end apart: 28 -> 28, of which waited for: 16 -> 16; matrix products, arithmetic and copies ran while one was open for 0% -> 0% of each run, Pallas kernels for 8% -> 9%
where the time goes in v5:
time: 92.6 us; the launch traced here: 92.4 us
  waiting for transfers between devices  48.2 us (52%)
  starting transfers between devices  25.5 us (28%)
  Pallas kernels  15 us (16%)
  local copies, waits for them, and re-layouts  3.39 us (4%)
    ppermute x12, waiting for transfers between devices, sent(): return tuple((lax.ppermute(piece, 'dp', pairs) for piece in pieces))  34.1 us
    pallas_call x9, Pallas kernels, kernel_call(): pl.pallas_call(body, out_shape=out_shape, in_specs=in_specs, out_specs=ou...  15 us
    ppermute x12, starting transfers between devices, sent(): return tuple((lax.ppermute(piece, 'dp', pairs) for piece in pieces))  12.2 us
    ppermute x12, waiting for transfers between devices, swapped(): return lax.ppermute(value, axis, [(0, 1), (1, 0)])  10 us
    ppermute x12, starting transfers between devices, swapped(): return lax.ppermute(value, axis, [(0, 1), (1, 0)])  7.62 us
    ppermute x1, starting transfers between devices, ringed(): lax.ppermute(outer, 'dp', outer_pairs)  3.68 us
    unnamed x15, local copies, waits for them, and re-layouts  2.66 us
    ppermute x1, waiting for transfers between devices, ringed(): lax.ppermute(outer, 'dp', outer_pairs)  2.62 us
  transfers between devices with their start and end apart: 28, of which 16 were waited for; matrix products, arithmetic and copies ran while one was open for 0% of the time, Pallas kernels for 9%

profile of v5, /device:TPU:0, one launch (start us, length us, event | category | flops | bytes accessed | tf_op | source)
XLA Modules:
  0.0 92.4 jit_solution(5373940755083808702)
XLA Ops:
  0.0 3.8 %shard_map.73 = (bf16[80,2304]{1,0:T(8,128)(2,1)}, bf16[80,2432]{1,0:T(8,128)(2,1)}, bf16[256,4736]{1,0:T(8,128)(2,1)}) custom-call(bf16[256,6912]{1,0:T(8,128)(2,1)} %acts.2, bf16[256,2560]{1,0:T(8,128)(2,1)} %grads.2, bf16[80,6912]{1,0:T(8,128)(2,1)} %act_factor.2, bf16[80,2560]{1,0:T(8,128)(2,1)} %grad_factor.2), custom_call_target="tpu_custom_call" | custom-call | tf_op jit(solution)/shard_map/pallas_call | solution.py:99
  3.8 3.0 %collective-permute-start.4 = (bf16[256,4736]{1,0:T(8,128)(2,1)}, bf16[256,4736]{1,0:T(8,128)(2,1)S(1)}, u32[]{:S(2)}, u32[]{:S(2)}) collective-permute-start(bf16[256,4736]{1,0:T(8,128)(2,1)} %get-tuple-element.44), channel_id=1, source_target_pairs={{0,16},{16,0},{1,17},{17,1},{2,18},{18,2},{3,19},{19,3},{4,20},{20... | collective-permute-start | bytes 7274504 | tf_op jit(solution)/shard_map/ppermute | solution.py:26
  6.8 1.5 %collective-permute-start.3 = (bf16[80,2432]{1,0:T(8,128)(2,1)}, bf16[80,2432]{1,0:T(8,128)(2,1)S(1)}, u32[]{:S(2)}, u32[]{:S(2)}) collective-permute-start(bf16[80,2432]{1,0:T(8,128)(2,1)} %get-tuple-element.38), channel_id=1, source_target_pairs={{4,0},{8,4},{12,8},{14,12},{10,14},{6,10},{2,6},{0,2},{5,1},{9,5},... | collective-permute-start | bytes 1167368 | tf_op jit(solution)/shard_map/ppermute | solution.py:277
  8.9 1.5 %collective-permute-start.2 = (bf16[80,2304]{1,0:T(8,128)(2,1)}, bf16[80,2304]{1,0:T(8,128)(2,1)S(1)}, u32[]{:S(2)}, u32[]{:S(2)}) collective-permute-start(bf16[80,2304]{1,0:T(8,128)(2,1)} %get-tuple-element.37), channel_id=1, source_target_pairs={{4,0},{8,4},{12,8},{14,12},{10,14},{6,10},{2,6},{0,2},{5,1},{9,5},... | collective-permute-start | bytes 1105928 | tf_op jit(solution)/shard_map/ppermute | solution.py:277
  10.9 8.1 %collective-permute-done.3.refs_3_ = bf16[80,2432]{1,0:T(8,128)(2,1)S(1)} collective-permute-done((bf16[80,2432]{1,0:T(8,128)(2,1)}, bf16[80,2432]{1,0:T(8,128)(2,1)S(1)}, u32[]{:S(2)}, u32[]{:S(2)}) %collective-permute-start.3) | collective-permute-done | bytes 389152 | tf_op jit(solution)/shard_map/ppermute | solution.py:277
  19.0 1.5 %collective-permute-start.11 = (bf16[80,2432]{1,0:T(8,128)(2,1)S(1)}, bf16[80,2432]{1,0:T(8,128)(2,1)S(1)}, u32[]{:S(2)}, u32[]{:S(2)}) collective-permute-start(bf16[80,2432]{1,0:T(8,128)(2,1)S(1)} %collective-permute-done.3.refs_3_), channel_id=1, source_target_pairs={{4,0},{8,4},{12,8},{14,12},{10,14},{6,10},{2,6},{0,2},{5,1},{9,5},... | collective-permute-start | bytes 1167368 | tf_op jit(solution)/shard_map/ppermute | solution.py:277
  21.0 5.9 %collective-permute-done.2.refs_2_ = bf16[80,2304]{1,0:T(8,128)(2,1)S(1)} collective-permute-done((bf16[80,2304]{1,0:T(8,128)(2,1)}, bf16[80,2304]{1,0:T(8,128)(2,1)S(1)}, u32[]{:S(2)}, u32[]{:S(2)}) %collective-permute-start.2) | collective-permute-done | bytes 368672 | tf_op jit(solution)/shard_map/ppermute | solution.py:277
  26.9 1.5 %collective-permute-start.9 = (bf16[80,2304]{1,0:T(8,128)(2,1)S(1)}, bf16[80,2304]{1,0:T(8,128)(2,1)S(1)}, u32[]{:S(2)}, u32[]{:S(2)}) collective-permute-start(bf16[80,2304]{1,0:T(8,128)(2,1)S(1)} %collective-permute-done.2.refs_2_), channel_id=1, source_target_pairs={{4,0},{8,4},{12,8},{14,12},{10,14},{6,10},{2,6},{0,2},{5,1},{9,5},... | collective-permute-start | bytes 1105928 | tf_op jit(solution)/shard_map/ppermute | solution.py:277
  28.9 1.3 %copy-done.1 = bf16[256,2560]{1,0:T(8,128)(2,1)S(1)} copy-done((bf16[256,2560]{1,0:T(8,128)(2,1)S(1)}, bf16[256,2560]{1,0:T(8,128)(2,1)}, u32[]{:S(2)}) %copy-start.1) | copy-done | bytes 1310744
  31.5 1.5 %shard_map.74 = (f32[160,128]{1,0:T(8,128)S(1)}, f32[160,128]{1,0:T(8,128)S(1)}, bf16[256,4736]{1,0:T(8,128)(2,1)S(1)}) custom-call(bf16[256,6912]{1,0:T(8,128)(2,1)S(1)} %copy-done, bf16[256,2560]{1,0:T(8,128)(2,1)S(1)} %copy-done.1, bf16[80,6912]{1,0:T(8,128)(2,1)S(1)} %copy-done.2, bf16[80,2560]{1,0:T(8,128)(2,1)S(1)} %copy-done.3), custom_call_target="tpu_custom_call" | custom-call | tf_op jit(solution)/shard_map/pallas_call | solution.py:99
  33.1 2.2 %collective-permute-done.11.refs_7_ = bf16[80,2432]{1,0:T(8,128)(2,1)S(1)} collective-permute-done((bf16[80,2432]{1,0:T(8,128)(2,1)S(1)}, bf16[80,2432]{1,0:T(8,128)(2,1)S(1)}, u32[]{:S(2)}, u32[]{:S(2)}) %collective-permute-start.11) | collective-permute-done | bytes 389152 | tf_op jit(solution)/shard_map/ppermute | solution.py:277
  35.2 1.5 %collective-permute-done.7.refs_5_ = bf16[80,2432]{1,0:T(8,128)(2,1)S(1)} collective-permute-done((bf16[80,2432]{1,0:T(8,128)(2,1)S(1)}, bf16[80,2432]{1,0:T(8,128)(2,1)S(1)}, u32[]{:S(2)}, u32[]{:S(2)}) %collective-permute-start.7) | collective-permute-done | bytes 389152 | tf_op jit(solution)/shard_map/ppermute | solution.py:277
  37.3 1.5 %collective-permute-start.12 = (bf16[80,2432]{1,0:T(8,128)(2,1)S(1)}, bf16[80,2432]{1,0:T(8,128)(2,1)S(1)}, u32[]{:S(2)}, u32[]{:S(2)}) collective-permute-start(bf16[80,2432]{1,0:T(8,128)(2,1)S(1)} %collective-permute-done.11.refs_7_), channel_id=1, source_target_pairs={{4,0},{8,4},{12,8},{14,12},{10,14},{6,10},{2,6},{0,2},{5,1},{9,5},... | collective-permute-start | bytes 1167368 | tf_op jit(solution)/shard_map/ppermute | solution.py:277
  38.8 4.4 %collective-permute-done.9.refs_6_ = bf16[80,2304]{1,0:T(8,128)(2,1)S(1)} collective-permute-done((bf16[80,2304]{1,0:T(8,128)(2,1)S(1)}, bf16[80,2304]{1,0:T(8,128)(2,1)S(1)}, u32[]{:S(2)}, u32[]{:S(2)}) %collective-permute-start.9) | collective-permute-done | bytes 368672 | tf_op jit(solution)/shard_map/ppermute | solution.py:277
  43.1 1.5 %collective-permute-done.5.refs_4_ = bf16[80,2304]{1,0:T(8,128)(2,1)S(1)} collective-permute-done((bf16[80,2304]{1,0:T(8,128)(2,1)S(1)}, bf16[80,2304]{1,0:T(8,128)(2,1)S(1)}, u32[]{:S(2)}, u32[]{:S(2)}) %collective-permute-start.5) | collective-permute-done | bytes 368672 | tf_op jit(solution)/shard_map/ppermute | solution.py:277
  45.2 1.5 %collective-permute-start.10 = (bf16[80,2304]{1,0:T(8,128)(2,1)S(1)}, bf16[80,2304]{1,0:T(8,128)(2,1)S(1)}, u32[]{:S(2)}, u32[]{:S(2)}) collective-permute-start(bf16[80,2304]{1,0:T(8,128)(2,1)S(1)} %collective-permute-done.9.refs_6_), channel_id=1, source_target_pairs={{4,0},{8,4},{12,8},{14,12},{10,14},{6,10},{2,6},{0,2},{5,1},{9,5},... | collective-permute-start | bytes 1105928 | tf_op jit(solution)/shard_map/ppermute | solution.py:277
  46.7 1.9 %shard_map.77 = (bf16[320,4736]{1,0:T(8,128)(2,1)S(1)}, f32[640,128]{1,0:T(8,128)S(1)}, f32[640,128]{1,0:T(8,128)S(1)}) custom-call(bf16[256,4736]{1,0:T(8,128)(2,1)S(1)} %get-tuple-element.43.tokens.own, bf16[80,2304]{1,0:T(8,128)(2,1)S(1)} %collective-permute-done.refs_0_, bf16[80,2432]{1,0:T(8,128)(2,1)S(1)} %collective-permute-done.1.refs_1_, ...), custom_call_target="tpu_custom_call" | custom-call | flops 775946240 | tf_op jit(solution)/shard_map/pallas_call | solution.py:99
  48.6 10.5 %collective-permute-done.6.refs_0_ = bf16[80,2304]{1,0:T(8,128)(2,1)S(1)} collective-permute-done((bf16[80,2304]{1,0:T(8,128)(2,1)S(1)}, bf16[80,2304]{1,0:T(8,128)(2,1)S(1)}, u32[]{:S(2)}, u32[]{:S(2)}) %collective-permute-start.6) | collective-permute-done | bytes 368672 | tf_op jit(solution)/shard_map/ppermute | solution.py:277
  60.4 1.6 %shard_map.79 = (f32[640,128]{1,0:T(8,128)S(1)}, f32[640,128]{1,0:T(8,128)S(1)}) custom-call(bf16[256,4736]{1,0:T(8,128)(2,1)S(1)} %collective-permute-done.4.tokens.other, bf16[320,4736]{1,0:T(8,128)(2,1)S(1)} %get-tuple-element.64.factor), custom_call_target="tpu_custom_call" | custom-call | flops 775946240 | tf_op jit(solution)/shard_map/pallas_call | solution.py:99
  62.0 1.6 %collective-permute-start.16 = (bf16[80,2432]{1,0:T(8,128)(2,1)S(1)}, bf16[80,2432]{1,0:T(8,128)(2,1)S(1)}, u32[]{:S(2)}, u32[]{:S(2)}) collective-permute-start(bf16[80,2432]{1,0:T(8,128)(2,1)S(1)} %collective-permute-done.12.refs_3_), channel_id=1, source_target_pairs={{4,0},{8,4},{12,8},{14,12},{10,14},{6,10},{2,6},{0,2},{5,1},{9,5},... | collective-permute-start | bytes 1167368 | tf_op jit(solution)/shard_map/ppermute | solution.py:346
  68.8 4.9 %collective-permute-done.14.refs_7_ = f32[320,128]{1,0:T(8,128)S(1)} collective-permute-done((f32[320,128]{1,0:T(8,128)S(1)}, f32[320,128]{1,0:T(8,128)S(1)}, u32[]{:S(2)}, u32[]{:S(2)}) %collective-permute-start.14) | collective-permute-done | bytes 163872 | tf_op jit(solution)/shard_map/ppermute | solution.py:26
  74.3 1.6 %shard_map.78 = (f32[160,128]{1,0:T(8,128)S(1)}, f32[160,128]{1,0:T(8,128)S(1)}, f32[160,128]{1,0:T(8,128)S(1)}, f32[160,128]{1,0:T(8,128)S(1)}) custom-call(bf16[256,4736]{1,0:T(8,128)(2,1)S(1)} %get-tuple-element.43.tokens.own, bf16[256,4736]{1,0:T(8,128)(2,1)S(1)} %collective-permute-done.4.tokens.other, ...), custom_call_target="tpu_custom_call" | custom-call | tf_op jit(solution)/shard_map/pallas_call | solution.py:99
  84.5 3.7 %collective-permute-start.26 = (f32[8,32]{1,0:T(8,128)S(1)}, f32[8,32]{1,0:T(8,128)S(1)}, u32[]{:S(2)}, u32[]{:S(2)}) collective-permute-start(f32[8,32]{1,0:T(8,128)S(1)} %get-tuple-element.69), channel_id=1, source_target_pairs={{0,14},{2,4},{4,2},{6,8},{8,6},{10,12},{12,10},{14,0},{1,15},{3,5}... | collective-permute-start | bytes 3080 | tf_op jit(solution)/shard_map/ppermute | solution.py:389
  88.2 2.6 %collective-permute-done.26 = f32[8,32]{1,0:T(8,128)S(1)} collective-permute-done((f32[8,32]{1,0:T(8,128)S(1)}, f32[8,32]{1,0:T(8,128)S(1)}, u32[]{:S(2)}, u32[]{:S(2)}) %collective-permute-start.26) | collective-permute-done | bytes 1056 | tf_op jit(solution)/shard_map/ppermute | solution.py:389
  (64 shorter events, 21.6 us)
Async XLA Ops:
  3.8 56.6 %collective-permute-start.4 = (bf16[256,4736]{1,0:T(8,128)(2,1)}, bf16[256,4736]{1,0:T(8,128)(2,1)S(1)}, u32[]{:S(2)}, u32[]{:S(2)}) collective-permute-start(bf16[256,4736]{1,0:T(8,128)(2,1)} %get-tuple-element.44), channel_id=1, source_target_pairs={{0,16},{16,0},{1,17},{17,1},{2,18},{18,2},{3,19},{19,3},{4,20},{20... | collective-permute-start | bytes 7274504 | tf_op jit(solution)/shard_map/ppermute | solution.py:26
  6.8 12.2 %collective-permute-start.3 = (bf16[80,2432]{1,0:T(8,128)(2,1)}, bf16[80,2432]{1,0:T(8,128)(2,1)S(1)}, u32[]{:S(2)}, u32[]{:S(2)}) collective-permute-start(bf16[80,2432]{1,0:T(8,128)(2,1)} %get-tuple-element.38), channel_id=1, source_target_pairs={{4,0},{8,4},{12,8},{14,12},{10,14},{6,10},{2,6},{0,2},{5,1},{9,5},... | collective-permute-start | bytes 1167368 | tf_op jit(solution)/shard_map/ppermute | solution.py:277
  8.3 12.2 %collective-permute-start.1 = (bf16[80,2432]{1,0:T(8,128)(2,1)}, bf16[80,2432]{1,0:T(8,128)(2,1)S(1)}, u32[]{:S(2)}, u32[]{:S(2)}) collective-permute-start(bf16[80,2432]{1,0:T(8,128)(2,1)} %get-tuple-element.38), channel_id=1, source_target_pairs={{0,4},{4,8},{8,12},{12,14},{14,10},{10,6},{6,2},{2,0},{1,5},{5,9},... | collective-permute-start | bytes 1167368 | tf_op jit(solution)/shard_map/ppermute | solution.py:277
  8.9 18.0 %collective-permute-start.2 = (bf16[80,2304]{1,0:T(8,128)(2,1)}, bf16[80,2304]{1,0:T(8,128)(2,1)S(1)}, u32[]{:S(2)}, u32[]{:S(2)}) collective-permute-start(bf16[80,2304]{1,0:T(8,128)(2,1)} %get-tuple-element.37), channel_id=1, source_target_pairs={{4,0},{8,4},{12,8},{14,12},{10,14},{6,10},{2,6},{0,2},{5,1},{9,5},... | collective-permute-start | bytes 1105928 | tf_op jit(solution)/shard_map/ppermute | solution.py:277
  10.4 18.1 %collective-permute-start = (bf16[80,2304]{1,0:T(8,128)(2,1)}, bf16[80,2304]{1,0:T(8,128)(2,1)S(1)}, u32[]{:S(2)}, u32[]{:S(2)}) collective-permute-start(bf16[80,2304]{1,0:T(8,128)(2,1)} %get-tuple-element.37), channel_id=1, source_target_pairs={{0,4},{4,8},{8,12},{12,14},{14,10},{10,6},{6,2},{2,0},{1,5},{5,9},... | collective-permute-start | bytes 1105928 | tf_op jit(solution)/shard_map/ppermute | solution.py:277
  19.0 16.2 %collective-permute-start.11 = (bf16[80,2432]{1,0:T(8,128)(2,1)S(1)}, bf16[80,2432]{1,0:T(8,128)(2,1)S(1)}, u32[]{:S(2)}, u32[]{:S(2)}) collective-permute-start(bf16[80,2432]{1,0:T(8,128)(2,1)S(1)} %collective-permute-done.3.refs_3_), channel_id=1, source_target_pairs={{4,0},{8,4},{12,8},{14,12},{10,14},{6,10},{2,6},{0,2},{5,1},{9,5},... | collective-permute-start | bytes 1167368 | tf_op jit(solution)/shard_map/ppermute | solution.py:277
  20.5 16.2 %collective-permute-start.7 = (bf16[80,2432]{1,0:T(8,128)(2,1)S(1)}, bf16[80,2432]{1,0:T(8,128)(2,1)S(1)}, u32[]{:S(2)}, u32[]{:S(2)}) collective-permute-start(bf16[80,2432]{1,0:T(8,128)(2,1)S(1)} %collective-permute-done.1.refs_1_), channel_id=1, source_target_pairs={{0,4},{4,8},{8,12},{12,14},{14,10},{10,6},{6,2},{2,0},{1,5},{5,9},... | collective-permute-start | bytes 1167368 | tf_op jit(solution)/shard_map/ppermute | solution.py:277
  26.9 16.2 %collective-permute-start.9 = (bf16[80,2304]{1,0:T(8,128)(2,1)S(1)}, bf16[80,2304]{1,0:T(8,128)(2,1)S(1)}, u32[]{:S(2)}, u32[]{:S(2)}) collective-permute-start(bf16[80,2304]{1,0:T(8,128)(2,1)S(1)} %collective-permute-done.2.refs_2_), channel_id=1, source_target_pairs={{4,0},{8,4},{12,8},{14,12},{10,14},{6,10},{2,6},{0,2},{5,1},{9,5},... | collective-permute-start | bytes 1105928 | tf_op jit(solution)/shard_map/ppermute | solution.py:277
  28.4 16.2 %collective-permute-start.5 = (bf16[80,2304]{1,0:T(8,128)(2,1)S(1)}, bf16[80,2304]{1,0:T(8,128)(2,1)S(1)}, u32[]{:S(2)}, u32[]{:S(2)}) collective-permute-start(bf16[80,2304]{1,0:T(8,128)(2,1)S(1)} %collective-permute-done.refs_0_), channel_id=1, source_target_pairs={{0,4},{4,8},{8,12},{12,14},{14,10},{10,6},{6,2},{2,0},{1,5},{5,9},... | collective-permute-start | bytes 1105928 | tf_op jit(solution)/shard_map/ppermute | solution.py:277
  36.7 22.4 %collective-permute-start.8 = (bf16[80,2432]{1,0:T(8,128)(2,1)S(1)}, bf16[80,2432]{1,0:T(8,128)(2,1)S(1)}, u32[]{:S(2)}, u32[]{:S(2)}) collective-permute-start(bf16[80,2432]{1,0:T(8,128)(2,1)S(1)} %collective-permute-done.7.refs_5_), channel_id=1, source_target_pairs={{0,4},{4,8},{8,12},{12,14},{14,10},{10,6},{6,2},{2,0},{1,5},{5,9},... | collective-permute-start | bytes 1167368 | tf_op jit(solution)/shard_map/ppermute | solution.py:277
  37.3 21.9 %collective-permute-start.12 = (bf16[80,2432]{1,0:T(8,128)(2,1)S(1)}, bf16[80,2432]{1,0:T(8,128)(2,1)S(1)}, u32[]{:S(2)}, u32[]{:S(2)}) collective-permute-start(bf16[80,2432]{1,0:T(8,128)(2,1)S(1)} %collective-permute-done.11.refs_7_), channel_id=1, source_target_pairs={{4,0},{8,4},{12,8},{14,12},{10,14},{6,10},{2,6},{0,2},{5,1},{9,5},... | collective-permute-start | bytes 1167368 | tf_op jit(solution)/shard_map/ppermute | solution.py:277
  44.6 14.5 %collective-permute-start.6 = (bf16[80,2304]{1,0:T(8,128)(2,1)S(1)}, bf16[80,2304]{1,0:T(8,128)(2,1)S(1)}, u32[]{:S(2)}, u32[]{:S(2)}) collective-permute-start(bf16[80,2304]{1,0:T(8,128)(2,1)S(1)} %collective-permute-done.5.refs_4_), channel_id=1, source_target_pairs={{0,4},{4,8},{8,12},{12,14},{14,10},{10,6},{6,2},{2,0},{1,5},{5,9},... | collective-permute-start | bytes 1105928 | tf_op jit(solution)/shard_map/ppermute | solution.py:277
  45.2 13.9 %collective-permute-start.10 = (bf16[80,2304]{1,0:T(8,128)(2,1)S(1)}, bf16[80,2304]{1,0:T(8,128)(2,1)S(1)}, u32[]{:S(2)}, u32[]{:S(2)}) collective-permute-start(bf16[80,2304]{1,0:T(8,128)(2,1)S(1)} %collective-permute-done.9.refs_6_), channel_id=1, source_target_pairs={{4,0},{8,4},{12,8},{14,12},{10,14},{6,10},{2,6},{0,2},{5,1},{9,5},... | collective-permute-start | bytes 1105928 | tf_op jit(solution)/shard_map/ppermute | solution.py:277
  62.0 5.8 %collective-permute-start.22 = (f32[640,128]{1,0:T(8,128)S(1)}, f32[640,128]{1,0:T(8,128)S(1)}, u32[]{:S(2)}, u32[]{:S(2)}) collective-permute-start(f32[640,128]{1,0:T(8,128)S(1)} %get-tuple-element.66), channel_id=1, source_target_pairs={{0,1},{1,0},{2,3},{3,2},{4,5},{5,4},{6,7},{7,6},{8,9},{9,8},{10,11... | collective-permute-start | bytes 983048 | tf_op jit(solution)/shard_map/ppermute | solution.py:26
  62.0 12.3 %collective-permute-start.16 = (bf16[80,2432]{1,0:T(8,128)(2,1)S(1)}, bf16[80,2432]{1,0:T(8,128)(2,1)S(1)}, u32[]{:S(2)}, u32[]{:S(2)}) collective-permute-start(bf16[80,2432]{1,0:T(8,128)(2,1)S(1)} %collective-permute-done.12.refs_3_), channel_id=1, source_target_pairs={{4,0},{8,4},{12,8},{14,12},{10,14},{6,10},{2,6},{0,2},{5,1},{9,5},... | collective-permute-start | bytes 1167368 | tf_op jit(solution)/shard_map/ppermute | solution.py:346
  63.7 10.7 %collective-permute-start.15 = (bf16[80,2304]{1,0:T(8,128)(2,1)S(1)}, bf16[80,2304]{1,0:T(8,128)(2,1)S(1)}, u32[]{:S(2)}, u32[]{:S(2)}) collective-permute-start(bf16[80,2304]{1,0:T(8,128)(2,1)S(1)} %collective-permute-done.6.refs_0_), channel_id=1, source_target_pairs={{0,4},{4,8},{8,12},{12,14},{14,10},{10,6},{6,2},{2,0},{1,5},{5,9},... | collective-permute-start | bytes 1105928 | tf_op jit(solution)/shard_map/ppermute | solution.py:346
  65.2 13.5 %collective-permute-start.21 = (f32[640,128]{1,0:T(8,128)S(1)}, f32[640,128]{1,0:T(8,128)S(1)}, u32[]{:S(2)}, u32[]{:S(2)}) collective-permute-start(f32[640,128]{1,0:T(8,128)S(1)} %get-tuple-element.55), channel_id=1, source_target_pairs={{0,1},{1,0},{2,3},{3,2},{4,5},{5,4},{6,7},{7,6},{8,9},{9,8},{10,11... | collective-permute-start | bytes 983048 | tf_op jit(solution)/shard_map/ppermute | solution.py:26
  66.6 7.1 %collective-permute-start.14 = (f32[320,128]{1,0:T(8,128)S(1)}, f32[320,128]{1,0:T(8,128)S(1)}, u32[]{:S(2)}, u32[]{:S(2)}) collective-permute-start(f32[320,128]{1,0:T(8,128)S(1)} %add.18), channel_id=1, source_target_pairs={{0,16},{16,0},{1,17},{17,1},{2,18},{18,2},{3,19},{19,3},{4,20},{20... | collective-permute-start | bytes 491528 | tf_op jit(solution)/shard_map/ppermute | solution.py:26
  67.8 12.2 %collective-permute-start.23 = (f32[640,128]{1,0:T(8,128)S(1)}, f32[640,128]{1,0:T(8,128)S(1)}, u32[]{:S(2)}, u32[]{:S(2)}) collective-permute-start(f32[640,128]{1,0:T(8,128)S(1)} %add.20), channel_id=1, source_target_pairs={{0,16},{16,0},{1,17},{17,1},{2,18},{18,2},{3,19},{19,3},{4,20},{20... | collective-permute-start | bytes 983048 | tf_op jit(solution)/shard_map/ppermute | solution.py:26
  73.8 5.0 %collective-permute-start.24 = (f32[320,128]{1,0:T(8,128)S(1)}, f32[320,128]{1,0:T(8,128)S(1)}, u32[]{:S(2)}, u32[]{:S(2)}) collective-permute-start(f32[320,128]{1,0:T(8,128)S(1)} %get-tuple-element.68), channel_id=1, source_target_pairs={{0,1},{1,0},{2,3},{3,2},{4,5},{5,4},{6,7},{7,6},{8,9},{9,8},{10,11... | collective-permute-start | bytes 491528 | tf_op jit(solution)/shard_map/ppermute | solution.py:26
  77.3 3.9 %collective-permute-start.17 = (f32[160,128]{1,0:T(8,128)S(1)}, f32[160,128]{1,0:T(8,128)S(1)}, u32[]{:S(2)}, u32[]{:S(2)}) collective-permute-start(f32[160,128]{1,0:T(8,128)S(1)} %get-tuple-element.59), channel_id=1, source_target_pairs={{0,1},{1,0},{2,3},{3,2},{4,5},{5,4},{6,7},{7,6},{8,9},{9,8},{10,11... | collective-permute-start | bytes 245768 | tf_op jit(solution)/shard_map/ppermute | solution.py:26
  77.5 4.8 %collective-permute-start.19 = (f32[160,128]{1,0:T(8,128)S(1)}, f32[160,128]{1,0:T(8,128)S(1)}, u32[]{:S(2)}, u32[]{:S(2)}) collective-permute-start(f32[160,128]{1,0:T(8,128)S(1)} %add.19), channel_id=1, source_target_pairs={{0,16},{16,0},{1,17},{17,1},{2,18},{18,2},{3,19},{19,3},{4,20},{20... | collective-permute-start | bytes 245768 | tf_op jit(solution)/shard_map/ppermute | solution.py:26
  84.5 6.3 %collective-permute-start.26 = (f32[8,32]{1,0:T(8,128)S(1)}, f32[8,32]{1,0:T(8,128)S(1)}, u32[]{:S(2)}, u32[]{:S(2)}) collective-permute-start(f32[8,32]{1,0:T(8,128)S(1)} %get-tuple-element.69), channel_id=1, source_target_pairs={{0,14},{2,4},{4,2},{6,8},{8,6},{10,12},{12,10},{14,0},{1,15},{3,5}... | collective-permute-start | bytes 3080 | tf_op jit(solution)/shard_map/ppermute | solution.py:389
  88.2 3.6 %collective-permute-start.27 = (f32[8,32]{1,0:T(8,128)S(1)}, f32[8,32]{1,0:T(8,128)S(1)}, u32[]{:S(2)}, u32[]{:S(2)}) collective-permute-start(f32[8,32]{1,0:T(8,128)S(1)} %get-tuple-element.70), channel_id=1, source_target_pairs={{0,2},{2,0},{4,6},{6,4},{8,10},{10,8},{12,14},{14,12},{1,3},{3,1},... | collective-permute-start | bytes 3080 | tf_op jit(solution)/shard_map/ppermute | solution.py:389
  (11 other events, 81.7 us)

commit v6 on v4

--- a/solution.py
+++ b/solution.py
@@ -295,7 +295,7 @@
             (activations, out_grads, act_factor, grad_factor, *from_back[1], *from_ahead[1])
         )[:4],
         scratch=[sums],
-        flops=0 * work(rows, 2 * width),
+        flops=0,
     )
     own_got = swapped(own_give, "tensor")
 
@@ -345,7 +345,7 @@
     last_first, last_second = tied((from_back[-1][0], from_ahead[-1][1]), near_give)
     last = [lax.ppermute(last_first, "dp", ahead), lax.ppermute(last_second, "dp", back)]
     far, far_give, far_keep, far_got = against_own(far_pieces)
-    other = after(other, far)
+    other = after(other, from_back[-1][0], from_ahead[-1][1])
     far_other, far_total = against_other(far, other)
     near_other, near_total = against_other(near, other)
 
@@ -356,7 +356,7 @@
         [whole] * 4,
         (own, after(other, far_other), *last),
         scratch=[sums],
-        flops=0,
+        flops=64 * work(rows, width),
     )
     last_got = swapped(last_give, "tensor")
     last_other = swapped(shared_keep + swapped(shared_give, "tensor"), "groups")

time: 92.8 us -> 92.5 us (level)
  transfers between devices with their start and end apart: 28 -> 28, of which waited for: 16 -> 13; matrix products, arithmetic and copies ran while one was open for 0% -> 0% of each run, Pallas kernels for 8% -> 10%
where the time goes in v6:
time: 92.5 us; the launch traced here: 92.3 us
  waiting for transfers between devices  49.7 us (54%)
  starting transfers between devices  25 us (27%)
  Pallas kernels  14 us (15%)
  local copies, waits for them, and re-layouts  3.39 us (4%)
    ppermute x12, waiting for transfers between devices, sent(): return tuple((lax.ppermute(piece, 'dp', pairs) for piece in pieces))  34.1 us
    pallas_call x8, Pallas kernels, kernel_call(): pl.pallas_call(body, out_shape=out_shape, in_specs=in_specs, out_specs=ou...  14 us
    ppermute x12, starting transfers between devices, sent(): return tuple((lax.ppermute(piece, 'dp', pairs) for piece in pieces))  12.2 us
    ppermute x12, waiting for transfers between devices, swapped(): return lax.ppermute(value, axis, [(0, 1), (1, 0)])  12 us
    ppermute x12, starting transfers between devices, swapped(): return lax.ppermute(value, axis, [(0, 1), (1, 0)])  7.23 us
    ppermute x1, starting transfers between devices, ringed(): lax.ppermute(outer, 'dp', outer_pairs)  3.58 us
    ppermute x1, waiting for transfers between devices, ringed(): lax.ppermute(outer, 'dp', outer_pairs)  2.72 us
    unnamed x15, local copies, waits for them, and re-layouts  2.67 us
  transfers between devices with their start and end apart: 28, of which 13 were waited for; matrix products, arithmetic and copies ran while one was open for 0% of the time, Pallas kernels for 10%

profile of v6, /device:TPU:0, one launch (start us, length us, event | category | flops | bytes accessed | tf_op | source)
XLA Modules:
  0.0 92.3 jit_solution(13295494851680977554)
XLA Ops:
  0.0 3.8 %shard_map.73 = (bf16[80,2304]{1,0:T(8,128)(2,1)}, bf16[80,2432]{1,0:T(8,128)(2,1)}, bf16[256,4736]{1,0:T(8,128)(2,1)}) custom-call(bf16[256,6912]{1,0:T(8,128)(2,1)} %acts.2, bf16[256,2560]{1,0:T(8,128)(2,1)} %grads.2, bf16[80,6912]{1,0:T(8,128)(2,1)} %act_factor.2, bf16[80,2560]{1,0:T(8,128)(2,1)} %grad_factor.2), custom_call_target="tpu_custom_call" | custom-call | tf_op jit(solution)/shard_map/pallas_call | solution.py:99
  3.8 3.0 %collective-permute-start.10 = (bf16[256,4736]{1,0:T(8,128)(2,1)}, bf16[256,4736]{1,0:T(8,128)(2,1)S(1)}, u32[]{:S(2)}, u32[]{:S(2)}) collective-permute-start(bf16[256,4736]{1,0:T(8,128)(2,1)} %get-tuple-element.48), channel_id=1, source_target_pairs={{0,16},{16,0},{1,17},{17,1},{2,18},{18,2},{3,19},{19,3},{4,20},{20... | collective-permute-start | bytes 7274504 | tf_op jit(solution)/shard_map/ppermute | solution.py:26
  6.8 1.5 %collective-permute-start.3 = (bf16[80,2432]{1,0:T(8,128)(2,1)}, bf16[80,2432]{1,0:T(8,128)(2,1)S(1)}, u32[]{:S(2)}, u32[]{:S(2)}) collective-permute-start(bf16[80,2432]{1,0:T(8,128)(2,1)} %get-tuple-element.38), channel_id=1, source_target_pairs={{4,0},{8,4},{12,8},{14,12},{10,14},{6,10},{2,6},{0,2},{5,1},{9,5},... | collective-permute-start | bytes 1167368 | tf_op jit(solution)/shard_map/ppermute | solution.py:277
  8.9 1.6 %collective-permute-start = (bf16[80,2304]{1,0:T(8,128)(2,1)}, bf16[80,2304]{1,0:T(8,128)(2,1)S(1)}, u32[]{:S(2)}, u32[]{:S(2)}) collective-permute-start(bf16[80,2304]{1,0:T(8,128)(2,1)} %get-tuple-element.37), channel_id=1, source_target_pairs={{0,4},{4,8},{8,12},{12,14},{14,10},{10,6},{6,2},{2,0},{1,5},{5,9},... | collective-permute-start | bytes 1105928 | tf_op jit(solution)/shard_map/ppermute | solution.py:277
  10.9 8.1 %collective-permute-done.3.refs_3_ = bf16[80,2432]{1,0:T(8,128)(2,1)S(1)} collective-permute-done((bf16[80,2432]{1,0:T(8,128)(2,1)}, bf16[80,2432]{1,0:T(8,128)(2,1)S(1)}, u32[]{:S(2)}, u32[]{:S(2)}) %collective-permute-start.3) | collective-permute-done | bytes 389152 | tf_op jit(solution)/shard_map/ppermute | solution.py:277
  19.0 1.5 %collective-permute-start.8 = (bf16[80,2432]{1,0:T(8,128)(2,1)S(1)}, bf16[80,2432]{1,0:T(8,128)(2,1)S(1)}, u32[]{:S(2)}, u32[]{:S(2)}) collective-permute-start(bf16[80,2432]{1,0:T(8,128)(2,1)S(1)} %collective-permute-done.3.refs_3_), channel_id=1, source_target_pairs={{4,0},{8,4},{12,8},{14,12},{10,14},{6,10},{2,6},{0,2},{5,1},{9,5},... | collective-permute-start | bytes 1167368 | tf_op jit(solution)/shard_map/ppermute | solution.py:277
  21.0 7.4 %collective-permute-done.refs_0_ = bf16[80,2304]{1,0:T(8,128)(2,1)S(1)} collective-permute-done((bf16[80,2304]{1,0:T(8,128)(2,1)}, bf16[80,2304]{1,0:T(8,128)(2,1)S(1)}, u32[]{:S(2)}, u32[]{:S(2)}) %collective-permute-start) | collective-permute-done | bytes 368672 | tf_op jit(solution)/shard_map/ppermute | solution.py:277
  28.9 1.5 %collective-permute-start.7 = (bf16[80,2304]{1,0:T(8,128)(2,1)S(1)}, bf16[80,2304]{1,0:T(8,128)(2,1)S(1)}, u32[]{:S(2)}, u32[]{:S(2)}) collective-permute-start(bf16[80,2304]{1,0:T(8,128)(2,1)S(1)} %collective-permute-done.2.refs_2_), channel_id=1, source_target_pairs={{4,0},{8,4},{12,8},{14,12},{10,14},{6,10},{2,6},{0,2},{5,1},{9,5},... | collective-permute-start | bytes 1105928 | tf_op jit(solution)/shard_map/ppermute | solution.py:277
  30.4 1.3 %copy-done.1 = bf16[256,2560]{1,0:T(8,128)(2,1)S(1)} copy-done((bf16[256,2560]{1,0:T(8,128)(2,1)S(1)}, bf16[256,2560]{1,0:T(8,128)(2,1)}, u32[]{:S(2)}) %copy-start.1) | copy-done | bytes 1310744
  33.0 1.5 %shard_map.74 = (f32[160,128]{1,0:T(8,128)S(1)}, f32[160,128]{1,0:T(8,128)S(1)}, bf16[256,4736]{1,0:T(8,128)(2,1)S(1)}) custom-call(bf16[256,6912]{1,0:T(8,128)(2,1)S(1)} %copy-done, bf16[256,2560]{1,0:T(8,128)(2,1)S(1)} %copy-done.1, bf16[80,6912]{1,0:T(8,128)(2,1)S(1)} %copy-done.2, bf16[80,2560]{1,0:T(8,128)(2,1)S(1)} %copy-done.3), custom_call_target="tpu_custom_call" | custom-call | tf_op jit(solution)/shard_map/pallas_call | solution.py:99
  35.2 1.5 %collective-permute-start.12 = (bf16[80,2432]{1,0:T(8,128)(2,1)S(1)}, bf16[80,2432]{1,0:T(8,128)(2,1)S(1)}, u32[]{:S(2)}, u32[]{:S(2)}) collective-permute-start(bf16[80,2432]{1,0:T(8,128)(2,1)S(1)} %collective-permute-done.8.refs_7_), channel_id=1, source_target_pairs={{4,0},{8,4},{12,8},{14,12},{10,14},{6,10},{2,6},{0,2},{5,1},{9,5},... | collective-permute-start | bytes 1167368 | tf_op jit(solution)/shard_map/ppermute | solution.py:277
  37.3 7.4 %collective-permute-done.5.refs_4_ = bf16[80,2304]{1,0:T(8,128)(2,1)S(1)} collective-permute-done((bf16[80,2304]{1,0:T(8,128)(2,1)S(1)}, bf16[80,2304]{1,0:T(8,128)(2,1)S(1)}, u32[]{:S(2)}, u32[]{:S(2)}) %collective-permute-start.5) | collective-permute-done | bytes 368672 | tf_op jit(solution)/shard_map/ppermute | solution.py:277
  45.2 1.5 %collective-permute-start.16 = (bf16[80,2304]{1,0:T(8,128)(2,1)S(1)}, bf16[80,2304]{1,0:T(8,128)(2,1)S(1)}, u32[]{:S(2)}, u32[]{:S(2)}) collective-permute-start(bf16[80,2304]{1,0:T(8,128)(2,1)S(1)} %collective-permute-done.7.refs_6_), channel_id=1, source_target_pairs={{4,0},{8,4},{12,8},{14,12},{10,14},{6,10},{2,6},{0,2},{5,1},{9,5},... | collective-permute-start | bytes 1105928 | tf_op jit(solution)/shard_map/ppermute | solution.py:277
  46.7 1.9 %shard_map.75 = (bf16[320,4736]{1,0:T(8,128)(2,1)S(1)}, f32[640,128]{1,0:T(8,128)S(1)}, f32[640,128]{1,0:T(8,128)S(1)}) custom-call(bf16[256,4736]{1,0:T(8,128)(2,1)S(1)} %get-tuple-element.45.tokens.own, bf16[80,2304]{1,0:T(8,128)(2,1)S(1)} %collective-permute-done.refs_0_, bf16[80,2432]{1,0:T(8,128)(2,1)S(1)} %collective-permute-done.1.refs_1_, ...), custom_call_target="tpu_custom_call" | custom-call | flops 775946240 | tf_op jit(solution)/shard_map/pallas_call | solution.py:99
  48.6 10.5 %collective-permute-done.11.refs_0_ = bf16[80,2304]{1,0:T(8,128)(2,1)S(1)} collective-permute-done((bf16[80,2304]{1,0:T(8,128)(2,1)S(1)}, bf16[80,2304]{1,0:T(8,128)(2,1)S(1)}, u32[]{:S(2)}, u32[]{:S(2)}) %collective-permute-start.11) | collective-permute-done | bytes 368672 | tf_op jit(solution)/shard_map/ppermute | solution.py:277
  59.7 1.5 %collective-permute-start.21 = (bf16[80,2432]{1,0:T(8,128)(2,1)S(1)}, bf16[80,2432]{1,0:T(8,128)(2,1)S(1)}, u32[]{:S(2)}, u32[]{:S(2)}) collective-permute-start(bf16[80,2432]{1,0:T(8,128)(2,1)S(1)} %collective-permute-done.12.refs_3_), channel_id=1, source_target_pairs={{4,0},{8,4},{12,8},{14,12},{10,14},{6,10},{2,6},{0,2},{5,1},{9,5},... | collective-permute-start | bytes 1167368 | tf_op jit(solution)/shard_map/ppermute | solution.py:346
  62.4 1.6 %shard_map.76 = (f32[640,128]{1,0:T(8,128)S(1)}, f32[640,128]{1,0:T(8,128)S(1)}) custom-call(bf16[256,4736]{1,0:T(8,128)(2,1)S(1)} %collective-permute-done.10.tokens.other, bf16[320,4736]{1,0:T(8,128)(2,1)S(1)} %get-tuple-element.52.factor), custom_call_target="tpu_custom_call" | custom-call | flops 775946240 | tf_op jit(solution)/shard_map/pallas_call | solution.py:99
  67.5 1.6 %collective-permute-start.14 = (f32[640,128]{1,0:T(8,128)S(1)}, f32[640,128]{1,0:T(8,128)S(1)}, u32[]{:S(2)}, u32[]{:S(2)}) collective-permute-start(f32[640,128]{1,0:T(8,128)S(1)} %add.18), channel_id=1, source_target_pairs={{0,16},{16,0},{1,17},{17,1},{2,18},{18,2},{3,19},{19,3},{4,20},{20... | collective-permute-start | bytes 983048 | tf_op jit(solution)/shard_map/ppermute | solution.py:26
  69.0 4.8 %collective-permute-done.19.refs_7_ = f32[320,128]{1,0:T(8,128)S(1)} collective-permute-done((f32[320,128]{1,0:T(8,128)S(1)}, f32[320,128]{1,0:T(8,128)S(1)}, u32[]{:S(2)}, u32[]{:S(2)}) %collective-permute-start.19) | collective-permute-done | bytes 163872 | tf_op jit(solution)/shard_map/ppermute | solution.py:26
  73.8 1.6 %shard_map.79 = (f32[160,128]{1,0:T(8,128)S(1)}, f32[160,128]{1,0:T(8,128)S(1)}, f32[160,128]{1,0:T(8,128)S(1)}, f32[160,128]{1,0:T(8,128)S(1)}) custom-call(bf16[256,4736]{1,0:T(8,128)(2,1)S(1)} %get-tuple-element.45.tokens.own, bf16[256,4736]{1,0:T(8,128)(2,1)S(1)} %collective-permute-done.10.tokens.other, ...), custom_call_target="tpu_custom_call" | custom-call | flops 12415139840 | tf_op jit(solution)/shard_map/pallas_call | solution.py:99
  78.0 4.0 %collective-permute-done.24.refs_10_ = f32[160,128]{1,0:T(8,128)S(1)} collective-permute-done((f32[160,128]{1,0:T(8,128)S(1)}, f32[160,128]{1,0:T(8,128)S(1)}, u32[]{:S(2)}, u32[]{:S(2)}) %collective-permute-start.24) | collective-permute-done | bytes 81952 | tf_op jit(solution)/shard_map/ppermute | solution.py:26
  82.0 1.3 %shard_map.80 = f32[24,32]{1,0:T(8,128)S(1)} custom-call(s32[8]{0:T(128)S(1)} %copy-done.4, s32[8,2]{1,0:T(8,128)S(1)} %copy.9.move_plan, s32[640,1]{1,0:T(8,128)S(1)} %reshape.4.query, f32[160,128]{1,0:T(8,128)S(1)} %get-tuple-element.43.refs_0_, f32[160,128]{1,0:T(8,128)S(1)} %collective-permute-done.4.refs_1_, f32[640,128]{1,0:T(8,128)S(1)} %get-tuple-element.46.refs_2_, ...), custom_call_target="tpu_custom_call" | custom-call | tf_op jit(solution)/shard_map/pallas_call | solution.py:99
  84.5 3.6 %collective-permute-start.26 = (f32[8,32]{1,0:T(8,128)S(1)}, f32[8,32]{1,0:T(8,128)S(1)}, u32[]{:S(2)}, u32[]{:S(2)}) collective-permute-start(f32[8,32]{1,0:T(8,128)S(1)} %get-tuple-element.69), channel_id=1, source_target_pairs={{0,14},{2,4},{4,2},{6,8},{8,6},{10,12},{12,10},{14,0},{1,15},{3,5}... | collective-permute-start | bytes 3080 | tf_op jit(solution)/shard_map/ppermute | solution.py:376
  88.1 2.7 %collective-permute-done.26 = f32[8,32]{1,0:T(8,128)S(1)} collective-permute-done((f32[8,32]{1,0:T(8,128)S(1)}, f32[8,32]{1,0:T(8,128)S(1)}, u32[]{:S(2)}, u32[]{:S(2)}) %collective-permute-start.26) | collective-permute-done | bytes 1056 | tf_op jit(solution)/shard_map/ppermute | solution.py:376
  (63 shorter events, 15.5 us)
Async XLA Ops:
  3.8 58.6 %collective-permute-start.10 = (bf16[256,4736]{1,0:T(8,128)(2,1)}, bf16[256,4736]{1,0:T(8,128)(2,1)S(1)}, u32[]{:S(2)}, u32[]{:S(2)}) collective-permute-start(bf16[256,4736]{1,0:T(8,128)(2,1)} %get-tuple-element.48), channel_id=1, source_target_pairs={{0,16},{16,0},{1,17},{17,1},{2,18},{18,2},{3,19},{19,3},{4,20},{20... | collective-permute-start | bytes 7274504 | tf_op jit(solution)/shard_map/ppermute | solution.py:26
  6.8 12.2 %collective-permute-start.3 = (bf16[80,2432]{1,0:T(8,128)(2,1)}, bf16[80,2432]{1,0:T(8,128)(2,1)S(1)}, u32[]{:S(2)}, u32[]{:S(2)}) collective-permute-start(bf16[80,2432]{1,0:T(8,128)(2,1)} %get-tuple-element.38), channel_id=1, source_target_pairs={{4,0},{8,4},{12,8},{14,12},{10,14},{6,10},{2,6},{0,2},{5,1},{9,5},... | collective-permute-start | bytes 1167368 | tf_op jit(solution)/shard_map/ppermute | solution.py:277
  8.3 12.2 %collective-permute-start.1 = (bf16[80,2432]{1,0:T(8,128)(2,1)}, bf16[80,2432]{1,0:T(8,128)(2,1)S(1)}, u32[]{:S(2)}, u32[]{:S(2)}) collective-permute-start(bf16[80,2432]{1,0:T(8,128)(2,1)} %get-tuple-element.38), channel_id=1, source_target_pairs={{0,4},{4,8},{8,12},{12,14},{14,10},{10,6},{6,2},{2,0},{1,5},{5,9},... | collective-permute-start | bytes 1167368 | tf_op jit(solution)/shard_map/ppermute | solution.py:277
  8.9 19.5 %collective-permute-start = (bf16[80,2304]{1,0:T(8,128)(2,1)}, bf16[80,2304]{1,0:T(8,128)(2,1)S(1)}, u32[]{:S(2)}, u32[]{:S(2)}) collective-permute-start(bf16[80,2304]{1,0:T(8,128)(2,1)} %get-tuple-element.37), channel_id=1, source_target_pairs={{0,4},{4,8},{8,12},{12,14},{14,10},{10,6},{6,2},{2,0},{1,5},{5,9},... | collective-permute-start | bytes 1105928 | tf_op jit(solution)/shard_map/ppermute | solution.py:277
  10.4 18.5 %collective-permute-start.2 = (bf16[80,2304]{1,0:T(8,128)(2,1)}, bf16[80,2304]{1,0:T(8,128)(2,1)S(1)}, u32[]{:S(2)}, u32[]{:S(2)}) collective-permute-start(bf16[80,2304]{1,0:T(8,128)(2,1)} %get-tuple-element.37), channel_id=1, source_target_pairs={{4,0},{8,4},{12,8},{14,12},{10,14},{6,10},{2,6},{0,2},{5,1},{9,5},... | collective-permute-start | bytes 1105928 | tf_op jit(solution)/shard_map/ppermute | solution.py:277
  19.0 16.2 %collective-permute-start.8 = (bf16[80,2432]{1,0:T(8,128)(2,1)S(1)}, bf16[80,2432]{1,0:T(8,128)(2,1)S(1)}, u32[]{:S(2)}, u32[]{:S(2)}) collective-permute-start(bf16[80,2432]{1,0:T(8,128)(2,1)S(1)} %collective-permute-done.3.refs_3_), channel_id=1, source_target_pairs={{4,0},{8,4},{12,8},{14,12},{10,14},{6,10},{2,6},{0,2},{5,1},{9,5},... | collective-permute-start | bytes 1167368 | tf_op jit(solution)/shard_map/ppermute | solution.py:277
  20.5 16.2 %collective-permute-start.6 = (bf16[80,2432]{1,0:T(8,128)(2,1)S(1)}, bf16[80,2432]{1,0:T(8,128)(2,1)S(1)}, u32[]{:S(2)}, u32[]{:S(2)}) collective-permute-start(bf16[80,2432]{1,0:T(8,128)(2,1)S(1)} %collective-permute-done.1.refs_1_), channel_id=1, source_target_pairs={{0,4},{4,8},{8,12},{12,14},{14,10},{10,6},{6,2},{2,0},{1,5},{5,9},... | collective-permute-start | bytes 1167368 | tf_op jit(solution)/shard_map/ppermute | solution.py:277
  28.4 16.2 %collective-permute-start.5 = (bf16[80,2304]{1,0:T(8,128)(2,1)S(1)}, bf16[80,2304]{1,0:T(8,128)(2,1)S(1)}, u32[]{:S(2)}, u32[]{:S(2)}) collective-permute-start(bf16[80,2304]{1,0:T(8,128)(2,1)S(1)} %collective-permute-done.refs_0_), channel_id=1, source_target_pairs={{0,4},{4,8},{8,12},{12,14},{14,10},{10,6},{6,2},{2,0},{1,5},{5,9},... | collective-permute-start | bytes 1105928 | tf_op jit(solution)/shard_map/ppermute | solution.py:277
  28.9 16.2 %collective-permute-start.7 = (bf16[80,2304]{1,0:T(8,128)(2,1)S(1)}, bf16[80,2304]{1,0:T(8,128)(2,1)S(1)}, u32[]{:S(2)}, u32[]{:S(2)}) collective-permute-start(bf16[80,2304]{1,0:T(8,128)(2,1)S(1)} %collective-permute-done.2.refs_2_), channel_id=1, source_target_pairs={{4,0},{8,4},{12,8},{14,12},{10,14},{6,10},{2,6},{0,2},{5,1},{9,5},... | collective-permute-start | bytes 1105928 | tf_op jit(solution)/shard_map/ppermute | solution.py:277
  35.2 24.4 %collective-permute-start.12 = (bf16[80,2432]{1,0:T(8,128)(2,1)S(1)}, bf16[80,2432]{1,0:T(8,128)(2,1)S(1)}, u32[]{:S(2)}, u32[]{:S(2)}) collective-permute-start(bf16[80,2432]{1,0:T(8,128)(2,1)S(1)} %collective-permute-done.8.refs_7_), channel_id=1, source_target_pairs={{4,0},{8,4},{12,8},{14,12},{10,14},{6,10},{2,6},{0,2},{5,1},{9,5},... | collective-permute-start | bytes 1167368 | tf_op jit(solution)/shard_map/ppermute | solution.py:277
  36.7 24.4 %collective-permute-start.15 = (bf16[80,2432]{1,0:T(8,128)(2,1)S(1)}, bf16[80,2432]{1,0:T(8,128)(2,1)S(1)}, u32[]{:S(2)}, u32[]{:S(2)}) collective-permute-start(bf16[80,2432]{1,0:T(8,128)(2,1)S(1)} %collective-permute-done.6.refs_5_), channel_id=1, source_target_pairs={{0,4},{4,8},{8,12},{12,14},{14,10},{10,6},{6,2},{2,0},{1,5},{5,9},... | collective-permute-start | bytes 1167368 | tf_op jit(solution)/shard_map/ppermute | solution.py:277
  44.6 14.5 %collective-permute-start.11 = (bf16[80,2304]{1,0:T(8,128)(2,1)S(1)}, bf16[80,2304]{1,0:T(8,128)(2,1)S(1)}, u32[]{:S(2)}, u32[]{:S(2)}) collective-permute-start(bf16[80,2304]{1,0:T(8,128)(2,1)S(1)} %collective-permute-done.5.refs_4_), channel_id=1, source_target_pairs={{0,4},{4,8},{8,12},{12,14},{14,10},{10,6},{6,2},{2,0},{1,5},{5,9},... | collective-permute-start | bytes 1105928 | tf_op jit(solution)/shard_map/ppermute | solution.py:277
  45.2 16.0 %collective-permute-start.16 = (bf16[80,2304]{1,0:T(8,128)(2,1)S(1)}, bf16[80,2304]{1,0:T(8,128)(2,1)S(1)}, u32[]{:S(2)}, u32[]{:S(2)}) collective-permute-start(bf16[80,2304]{1,0:T(8,128)(2,1)S(1)} %collective-permute-done.7.refs_6_), channel_id=1, source_target_pairs={{4,0},{8,4},{12,8},{14,12},{10,14},{6,10},{2,6},{0,2},{5,1},{9,5},... | collective-permute-start | bytes 1105928 | tf_op jit(solution)/shard_map/ppermute | solution.py:277
  59.1 14.7 %collective-permute-start.20 = (bf16[80,2304]{1,0:T(8,128)(2,1)S(1)}, bf16[80,2304]{1,0:T(8,128)(2,1)S(1)}, u32[]{:S(2)}, u32[]{:S(2)}) collective-permute-start(bf16[80,2304]{1,0:T(8,128)(2,1)S(1)} %collective-permute-done.11.refs_0_), channel_id=1, source_target_pairs={{0,4},{4,8},{8,12},{12,14},{14,10},{10,6},{6,2},{2,0},{1,5},{5,9},... | collective-permute-start | bytes 1105928 | tf_op jit(solution)/shard_map/ppermute | solution.py:346
  59.7 14.2 %collective-permute-start.21 = (bf16[80,2432]{1,0:T(8,128)(2,1)S(1)}, bf16[80,2432]{1,0:T(8,128)(2,1)S(1)}, u32[]{:S(2)}, u32[]{:S(2)}) collective-permute-start(bf16[80,2432]{1,0:T(8,128)(2,1)S(1)} %collective-permute-done.12.refs_3_), channel_id=1, source_target_pairs={{4,0},{8,4},{12,8},{14,12},{10,14},{6,10},{2,6},{0,2},{5,1},{9,5},... | collective-permute-start | bytes 1167368 | tf_op jit(solution)/shard_map/ppermute | solution.py:346
  64.0 3.4 %collective-permute-start.13 = (f32[640,128]{1,0:T(8,128)S(1)}, f32[640,128]{1,0:T(8,128)S(1)}, u32[]{:S(2)}, u32[]{:S(2)}) collective-permute-start(f32[640,128]{1,0:T(8,128)S(1)} %get-tuple-element.54), channel_id=1, source_target_pairs={{0,1},{1,0},{2,3},{3,2},{4,5},{5,4},{6,7},{7,6},{8,9},{9,8},{10,11... | collective-permute-start | bytes 983048 | tf_op jit(solution)/shard_map/ppermute | solution.py:26
  65.1 1.6 %collective-permute-start.18 = (f32[320,128]{1,0:T(8,128)S(1)}, f32[320,128]{1,0:T(8,128)S(1)}, u32[]{:S(2)}, u32[]{:S(2)}) collective-permute-start(f32[320,128]{1,0:T(8,128)S(1)} %get-tuple-element.61), channel_id=1, source_target_pairs={{0,1},{1,0},{2,3},{3,2},{4,5},{5,4},{6,7},{7,6},{8,9},{9,8},{10,11... | collective-permute-start | bytes 491528 | tf_op jit(solution)/shard_map/ppermute | solution.py:26
  66.7 7.1 %collective-permute-start.19 = (f32[320,128]{1,0:T(8,128)S(1)}, f32[320,128]{1,0:T(8,128)S(1)}, u32[]{:S(2)}, u32[]{:S(2)}) collective-permute-start(f32[320,128]{1,0:T(8,128)S(1)} %add.19), channel_id=1, source_target_pairs={{0,16},{16,0},{1,17},{17,1},{2,18},{18,2},{3,19},{19,3},{4,20},{20... | collective-permute-start | bytes 491528 | tf_op jit(solution)/shard_map/ppermute | solution.py:26
  67.3 10.7 %collective-permute-start.9 = (f32[640,128]{1,0:T(8,128)S(1)}, f32[640,128]{1,0:T(8,128)S(1)}, u32[]{:S(2)}, u32[]{:S(2)}) collective-permute-start(f32[640,128]{1,0:T(8,128)S(1)} %get-tuple-element.47), channel_id=1, source_target_pairs={{0,1},{1,0},{2,3},{3,2},{4,5},{5,4},{6,7},{7,6},{8,9},{9,8},{10,11... | collective-permute-start | bytes 983048 | tf_op jit(solution)/shard_map/ppermute | solution.py:26
  67.5 14.6 %collective-permute-start.14 = (f32[640,128]{1,0:T(8,128)S(1)}, f32[640,128]{1,0:T(8,128)S(1)}, u32[]{:S(2)}, u32[]{:S(2)}) collective-permute-start(f32[640,128]{1,0:T(8,128)S(1)} %add.18), channel_id=1, source_target_pairs={{0,16},{16,0},{1,17},{17,1},{2,18},{18,2},{3,19},{19,3},{4,20},{20... | collective-permute-start | bytes 983048 | tf_op jit(solution)/shard_map/ppermute | solution.py:26
  75.5 2.5 %collective-permute-start.17 = (f32[320,128]{1,0:T(8,128)S(1)}, f32[320,128]{1,0:T(8,128)S(1)}, u32[]{:S(2)}, u32[]{:S(2)}) collective-permute-start(f32[320,128]{1,0:T(8,128)S(1)} %get-tuple-element.58), channel_id=1, source_target_pairs={{0,1},{1,0},{2,3},{3,2},{4,5},{5,4},{6,7},{7,6},{8,9},{9,8},{10,11... | collective-permute-start | bytes 491528 | tf_op jit(solution)/shard_map/ppermute | solution.py:26
  77.3 4.8 %collective-permute-start.24 = (f32[160,128]{1,0:T(8,128)S(1)}, f32[160,128]{1,0:T(8,128)S(1)}, u32[]{:S(2)}, u32[]{:S(2)}) collective-permute-start(f32[160,128]{1,0:T(8,128)S(1)} %add.20), channel_id=1, source_target_pairs={{0,16},{16,0},{1,17},{17,1},{2,18},{18,2},{3,19},{19,3},{4,20},{20... | collective-permute-start | bytes 245768 | tf_op jit(solution)/shard_map/ppermute | solution.py:26
  84.5 6.3 %collective-permute-start.26 = (f32[8,32]{1,0:T(8,128)S(1)}, f32[8,32]{1,0:T(8,128)S(1)}, u32[]{:S(2)}, u32[]{:S(2)}) collective-permute-start(f32[8,32]{1,0:T(8,128)S(1)} %get-tuple-element.69), channel_id=1, source_target_pairs={{0,14},{2,4},{4,2},{6,8},{8,6},{10,12},{12,10},{14,0},{1,15},{3,5}... | collective-permute-start | bytes 3080 | tf_op jit(solution)/shard_map/ppermute | solution.py:376
  88.1 3.6 %collective-permute-start.27 = (f32[8,32]{1,0:T(8,128)S(1)}, f32[8,32]{1,0:T(8,128)S(1)}, u32[]{:S(2)}, u32[]{:S(2)}) collective-permute-start(f32[8,32]{1,0:T(8,128)S(1)} %get-tuple-element.70), channel_id=1, source_target_pairs={{0,2},{2,0},{4,6},{6,4},{8,10},{10,8},{12,14},{14,12},{1,3},{3,1},... | collective-permute-start | bytes 3080 | tf_op jit(solution)/shard_map/ppermute | solution.py:376
  (11 other events, 103.9 us)
